TPU v7x, 32 devices: a whole 2x2x4 slice. The times are simulated.
32 devices in a mesh: grp: 1, lat: 32 (over z, y, x, core).
Axes of the slice: x: 2, y: 2, z: 4, core: 2. Of those that a mesh axis runs over, the one named last changes fastest.
Arguments:
- fields: bfloat16 [768, 64, 2048], P(('grp', 'lat')), may hold values from -6 to 6
- spectral_weight: bfloat16 [2, 128, 64, 128], replicated, may hold values from -0.5 to 0.5
- local_weight: bfloat16 [2, 64, 64], replicated, may hold values from -0.75 to 0.75
Outputs:
- updated: bfloat16 [768, 64, 2048], P(('grp', 'lat'))
All inputs are finite; a program needn't handle non-finite values.
Results may differ from a plain program's by a relative error of at most 0.011.
Values may be sent and summed in bfloat16 or wider, within the bound.
No kernel may reach another device: no remote copies, remote signals or barrier semaphores. Data moves between devices by JAX's collectives and lax.ppermute only.
A program may use at most 128 MiB of HBM per device.

v0:
```python
import math

import jax
import jax.numpy as jnp
from jax import lax
from jax.sharding import PartitionSpec as P

KY = 128


def lon_forward_table(lon_count, mode_count):
    cells = jnp.arange(lon_count, dtype=jnp.int32)[:, None]
    modes = jnp.arange(mode_count, dtype=jnp.int32)[None, :]
    angle = 2.0 * jnp.pi / lon_count * (cells * modes % lon_count).astype(jnp.float32)
    factor = 1.0 / math.sqrt(lon_count)
    return jnp.stack([jnp.cos(angle) * factor, -jnp.sin(angle) * factor], axis=1).astype(
        jnp.bfloat16
    )


def lon_back_table(lon_count, mode_count):
    modes = jnp.arange(mode_count, dtype=jnp.int32)[:, None]
    cells = jnp.arange(lon_count, dtype=jnp.int32)[None, :]
    angle = 2.0 * jnp.pi / lon_count * (cells * modes % lon_count).astype(jnp.float32)
    factor = 1.0 / math.sqrt(mode_count)
    return jnp.stack([jnp.cos(angle) * factor, -jnp.sin(angle) * factor], axis=1).astype(
        jnp.bfloat16
    )


def lat_tables(lat_count, kept_count, block_rows):
    index = jnp.arange(kept_count, dtype=jnp.int32)
    waves = jnp.where(index < kept_count // 2, index, lat_count - kept_count + index)
    rowids = jnp.arange(lat_count, dtype=jnp.int32)
    stride = lat_count // block_rows
    latitudes = rowids % block_rows * stride + rowids // block_rows
    angle = (
        2.0
        * jnp.pi
        / lat_count
        * (waves[:, None] * latitudes[None, :] % lat_count).astype(jnp.float32)
    )
    forward = jnp.stack([jnp.cos(angle), jnp.sin(angle)], axis=0) * (1.0 / math.sqrt(lat_count))
    backward = jnp.stack([jnp.cos(angle).T, jnp.sin(angle).T], axis=0) * (
        1.0 / math.sqrt(kept_count)
    )
    return (forward.astype(jnp.bfloat16), backward.astype(jnp.bfloat16))


def lat_forward(table, values, channels):
    products = jnp.einsum("pjn,nkc->pjkc", table, values, preferred_element_type=jnp.float32)
    real_part = products[0, ..., :channels] + products[1, ..., channels:]
    imag_part = products[0, ..., channels:] - products[1, ..., :channels]
    return jnp.concatenate([real_part, imag_part], axis=-1)


def lat_backward(table, modes, channels):
    products = jnp.einsum("pnj,jkc->pnkc", table, modes, preferred_element_type=jnp.float32)
    real_part = products[0, ..., :channels] - products[1, ..., channels:]
    imag_part = products[1, ..., :channels] + products[0, ..., channels:]
    return jnp.concatenate([real_part, imag_part], axis=-1)


def mix_matrix(weight, channels):
    real_w = weight[..., :channels]
    imag_w = weight[..., channels:]
    lower = jnp.concatenate([-imag_w, real_w], axis=-1)
    return jnp.concatenate([weight, lower], axis=1)


def spectral_block(gathered, mixing, forward_lat, backward_lat, channels):
    lat_modes = lat_forward(forward_lat, gathered, channels).astype(jnp.bfloat16)
    mixed_modes = jnp.einsum(
        "jkc,kcd->jkd", lat_modes, mixing, preferred_element_type=jnp.float32
    ).astype(jnp.bfloat16)
    return lat_backward(backward_lat, mixed_modes, channels).astype(jnp.bfloat16)


def shards(fields, spectral_weight, local_weight):
    row_count, channels, lon_count = fields.shape
    layer_count = spectral_weight.shape[0]
    mode_rows = spectral_weight.shape[1]
    devices = lax.axis_size("lat")
    my_index = lax.axis_index("lat")
    lat_count = row_count * devices
    forward_lon = lon_forward_table(lon_count, mode_rows)
    backward_lon = lon_back_table(lon_count, mode_rows)
    forward_lat, backward_lat = lat_tables(lat_count, KY, row_count)
    current = fields
    for layer_idx in range(layer_count):
        mixing = mix_matrix(spectral_weight[layer_idx], channels)
        lon_modes = jnp.einsum(
            "rcl,lpk->rkpc", current, forward_lon, preferred_element_type=jnp.float32
        )
        lon_modes = lon_modes.reshape(row_count, mode_rows, 2 * channels).astype(jnp.bfloat16)
        slice_size = mode_rows // devices
        gathered = lax.all_to_all(lon_modes, "lat", split_axis=1, concat_axis=0, tiled=True)
        my_mixing = lax.dynamic_slice_in_dim(mixing, my_index * slice_size, slice_size, 0)
        rebuilt = spectral_block(gathered, my_mixing, forward_lat, backward_lat, channels)
        lat_back = lax.all_to_all(rebuilt, "lat", split_axis=0, concat_axis=1, tiled=True)
        spectral = jnp.einsum(
            "rkpc,kpl->rcl",
            lat_back.reshape(row_count, mode_rows, 2, channels),
            backward_lon,
            preferred_element_type=jnp.float32,
        )
        pointwise = jnp.einsum(
            "rcl,cd->rdl", current, local_weight[layer_idx], preferred_element_type=jnp.float32
        )
        current = jax.nn.gelu(spectral + pointwise, approximate=True).astype(jnp.bfloat16)
    return current


def solution(mesh):
    return jax.shard_map(
        shards,
        mesh=mesh,
        in_specs=(P(("grp", "lat"), None, None), P(), P()),
        out_specs=P(("grp", "lat"), None, None),
        check_vma=False,
    )
```

profile of v0, /device:TPU:0, one launch (start us, length us, event | category | flops | bytes accessed | tf_op | source)
XLA Modules:
  0.0 144.2 jit_solution(10989742851166684646)
XLA Ops:
  0.0 4.4 %multiply_convert_fusion.2 = (bf16[2048,1,128]{2,0,1:T(8,128)(2,1)S(1)}, bf16[2048,1,128]{2,0,1:T(8,128)(2,1)S(1)}) fusion(), kind=kLoop, calls=%fused_computation.60 | loop fusion | flops 4980736 | bytes 1048576 | tf_op jit(solution)/shard_map/convert.19
  4.4 0.0 copy-start.6
  4.4 0.0 copy-start.8
  4.5 5.0 %fusion.31 = bf16[24,128,2,64]{1,3,0,2:T(8,128)(2,1)S(1)} fusion(bf16[24,64,2048]{2,1,0:T(8,128)(2,1)} %param.3, bf16[2048,1,128]{2,0,1:T(8,128)(2,1)S(1)} %get-tuple-element.23, bf16[2048,1,128]{2,0,1:T(8,128)(2,1)S(1)} %get-tuple-element.24), kind=kOutput, calls=%fused_computation.43 | convolution fusion | flops 1613103104 | bytes 8126464 | tf_op jit(solution)/shard_map/rcl,lpk->rkpc/dot_general | solution.py:92
  9.4 0.0 copy-done.6
  9.4 0.0 copy-done.8
  9.4 0.1 copy.26
  9.5 1.3 copy.27
  10.8 7.3 %all-to-all-start = ((bf16[24,128,128]{2,0,1:T(8,128)(2,1)}), bf16[24,128,128]{2,0,1:T(8,128)(2,1)S(1)}, u32[]{:S(2)}, u32[]{:S(2)}) async-start(bf16[24,128,128]{2,0,1:T(8,128)(2,1)} %copy.27), calls=%async_computation | async-start | bytes 1572864 | tf_op jit(solution)/shard_map/all_to_all | solution.py:97
  18.1 4.5 %fusion.150 = (bf16[1,128,64,128]{3,2,1,0:T(8,128)(2,1)}, bf16[1,128,64,128]{3,2,1,0:T(8,128)(2,1)S(1)}) fusion(bf16[2,128,64,128]{3,2,1,0:T(8,128)(2,1)} %param.4), kind=kLoop, calls=%fused_computation.167 | loop fusion | bytes 8388608 | tf_op jit(solution)/shard_map/slice | solution.py:91
  22.6 3.1 %copy.58 = bf16[1,128,64,128]{2,3,1,0:T(8,128)(2,1)} copy(bf16[1,128,64,128]{3,2,1,0:T(8,128)(2,1)S(1)} %get-tuple-element.8) | data formatting | bytes 4194304
  25.7 1.6 %fusion.69 = (f32[1,128,768]{2,1,0:T(8,128)S(1)}, f32[1,128,768]{2,1,0:T(8,128)S(1)}) fusion(s32[768]{0:T(1024)S(1)} %fusion.126, s32[128]{0:T(128)S(1)} %compare_select_fusion), kind=kLoop, calls=%fused_computation.98 | loop fusion | flops 884736 | bytes 790016 | tf_op jit(solution)/shard_map/cos | solution.py:44
  27.4 0.0 copy-start.2
  27.4 0.0 copy-start.4
  27.4 2.8 %fusion.73 = (f32[1,768,128]{2,1,0:T(8,128)S(1)}, f32[1,768,128]{2,1,0:T(8,128)}) fusion(s32[768]{0:T(1024)S(1)} %fusion.126, s32[128]{0:T(128)S(1)} %compare_select_fusion), kind=kLoop, calls=%fused_computation.103 | loop fusion | flops 884736 | bytes 790016 | tf_op jit(solution)/shard_map/cos | solution.py:44
  30.2 4.6 %fusion.151 = (bf16[128,64,64]{1,2,0:T(8,128)(2,1)}, bf16[128,64,64]{1,2,0:T(8,128)(2,1)}) fusion(bf16[128,64,128]{1,2,0:T(8,128)(2,1)} %bitcast.126), kind=kLoop, calls=%fused_computation.168 | loop fusion | flops 524288 | bytes 4194304 | tf_op jit(solution)/shard_map/slice | solution.py:65
  34.8 3.9 %all-to-all-done = bf16[24,128,128]{2,0,1:T(8,128)(2,1)S(1)} async-done(((bf16[24,128,128]{2,0,1:T(8,128)(2,1)}), bf16[24,128,128]{2,0,1:T(8,128)(2,1)S(1)}, u32[]{:S(2)}, u32[]{:S(2)}) %all-to-all-start) | async-done | bytes 786464 | tf_op jit(solution)/shard_map/all_to_all | solution.py:97
  38.7 0.1 copy.28
  38.8 0.0 copy-done.2
  38.8 0.0 copy-done.4
  38.8 0.5 fusion.112
  39.3 0.7 fusion.104
  40.0 1.8 %fusion.55 = f32[2,768,4,128]{1,3,2,0:T(8,128)S(1)} fusion(s32[]{:T(128)S(6)} %select_n.128, bf16[128,64,128]{1,2,0:T(8,128)(2,1)} %bitcast.127, bf16[128,64,64]{1,2,0:T(8,128)(2,1)} %get-tuple-element.10, bf16[128,64,64]{1,2,0:T(8,128)(2,1)} %get-tuple-element.9, bf16[128,4,64]{0,2,1:T(8,128)(2,1)} %get-tuple-element.18, ...), kind=kOutput, calls=%fused_computation.83 | convolution fusion | flops 219414528 | bytes 8257540 | tf_op jit(solution)/shard_map/pnj,jkc->pnkc/dot_general | solution.py:58
  41.8 0.2 fusion.62
  41.9 0.0 copy-start.12
  42.0 0.1 pad_maximum_fusion
  42.0 1.3 copy.31
  43.3 3.8 %all-to-all-start.1 = ((bf16[768,4,128]{2,1,0:T(4,128)(2,1)}), bf16[768,4,128]{2,1,0:T(4,128)(2,1)S(1)}, u32[]{:S(2)}, u32[]{:S(2)}) async-start(bf16[768,4,128]{2,1,0:T(4,128)(2,1)} %copy.31), calls=%async_computation.1 | async-start | bytes 1572864 | tf_op jit(solution)/shard_map/all_to_all | solution.py:100
  47.1 5.4 %multiply_convert_fusion = (bf16[128,1,2048]{2,0,1:T(8,128)(2,1)}, bf16[128,1,2048]{2,0,1:T(8,128)(2,1)}) fusion(), kind=kLoop, calls=%fused_computation.56 | loop fusion | flops 4980736 | bytes 1048576 | tf_op jit(solution)/shard_map/convert.9
  52.5 9.1 %fusion.116 = f32[64,24,2048]{2,0,1:T(8,128)} fusion(bf16[24,64,2048]{2,1,0:T(8,128)(2,1)} %param.3, bf16[2,64,64]{2,1,0:T(8,128)(2,1)S(1)} %copy-done.12), kind=kOutput, calls=%fused_computation.132 | convolution fusion | flops 402653184 | bytes 18890752 | tf_op jit(solution)/shard_map/rcl,cd->rdl/dot_general | solution.py:107
  61.6 6.0 %all-to-all-done.1 = bf16[768,4,128]{2,1,0:T(4,128)(2,1)S(1)} async-done(((bf16[768,4,128]{2,1,0:T(4,128)(2,1)}), bf16[768,4,128]{2,1,0:T(4,128)(2,1)S(1)}, u32[]{:S(2)}, u32[]{:S(2)}) %all-to-all-start.1) | async-done | bytes 786464 | tf_op jit(solution)/shard_map/all_to_all | solution.py:100
  67.5 0.1 copy.32
  67.6 0.1 copy.33
  67.7 0.7 reshape.429
  68.5 8.1 %fusion.7 = bf16[24,64,2048]{2,1,0:T(8,128)(2,1)S(1)} fusion(f32[64,24,2048]{2,0,1:T(8,128)} %fusion.116, bf16[24,128,2,64]{3,2,0,1:T(2,128)(2,1)S(1)} %reshape.429, bf16[128,1,2048]{2,0,1:T(8,128)(2,1)} %get-tuple-element.25, bf16[128,1,2048]{2,0,1:T(8,128)(2,1)} %get-tuple-element.26), kind=kOutput, calls=%fused_computation.9 | convolution fusion | flops 1642594304 | bytes 20709376 | tf_op jit(solution)/shard_map/rkpc,kpl->rcl/dot_general | solution.py:101
  76.6 0.0 copy-done.7
  76.6 0.0 copy-done.9
  76.6 0.0 copy-start.1
  76.7 1.8 %fusion.28 = bf16[24,128,2,64]{1,3,0,2:T(8,128)(2,1)S(1)} fusion(bf16[24,64,2048]{2,1,0:T(8,128)(2,1)S(1)} %fusion.7, bf16[2048,1,128]{2,0,1:T(8,128)(2,1)S(1)} %copy-done.7, bf16[2048,1,128]{2,0,1:T(8,128)(2,1)S(1)} %copy-done.9), kind=kOutput, calls=%fused_computation.42 | convolution fusion | flops 1613103104 | bytes 8126464 | tf_op jit(solution)/shard_map/rcl,lpk->rkpc/dot_general | solution.py:92
  78.5 0.9 copy-done.1
  79.4 0.1 copy.36
  79.4 1.3 copy.37
  80.7 3.6 %all-to-all-start.2 = ((bf16[24,128,128]{2,0,1:T(8,128)(2,1)}), bf16[24,128,128]{2,0,1:T(8,128)(2,1)S(1)}, u32[]{:S(2)}, u32[]{:S(2)}) async-start(bf16[24,128,128]{2,0,1:T(8,128)(2,1)} %copy.37), calls=%async_computation.2 | async-start | bytes 1572864 | tf_op jit(solution)/shard_map/all_to_all | solution.py:97
  84.4 3.1 %copy.57 = bf16[1,128,64,128]{2,3,1,0:T(8,128)(2,1)} copy(bf16[1,128,64,128]{3,2,1,0:T(8,128)(2,1)S(1)} %copy-done) | data formatting | bytes 4194304
  87.5 4.7 %fusion.149 = (bf16[128,64,64]{1,2,0:T(8,128)(2,1)}, bf16[128,64,64]{1,2,0:T(8,128)(2,1)}) fusion(bf16[128,64,128]{1,2,0:T(8,128)(2,1)} %bitcast.128), kind=kLoop, calls=%fused_computation.166 | loop fusion | flops 524288 | bytes 4194304 | tf_op jit(solution)/shard_map/slice | solution.py:65
  92.2 12.7 %all-to-all-done.2 = bf16[24,128,128]{2,0,1:T(8,128)(2,1)S(1)} async-done(((bf16[24,128,128]{2,0,1:T(8,128)(2,1)}), bf16[24,128,128]{2,0,1:T(8,128)(2,1)S(1)}, u32[]{:S(2)}, u32[]{:S(2)}) %all-to-all-start.2) | async-done | bytes 786464 | tf_op jit(solution)/shard_map/all_to_all | solution.py:97
  105.0 0.1 copy.38
  105.1 0.0 copy-done.3
  105.1 0.0 copy-done.5
  105.1 0.4 fusion.110
  105.5 0.7 fusion.106
  106.2 1.8 %fusion.54 = f32[2,768,4,128]{1,3,2,0:T(8,128)S(1)} fusion(s32[]{:T(128)S(6)} %select_n.128, bf16[128,64,128]{1,2,0:T(8,128)(2,1)} %bitcast.129, bf16[128,64,64]{1,2,0:T(8,128)(2,1)} %get-tuple-element.6, bf16[128,64,64]{1,2,0:T(8,128)(2,1)} %get-tuple-element.5, bf16[128,4,64]{0,2,1:T(8,128)(2,1)} %get-tuple-element.16, ...), kind=kOutput, calls=%fused_computation.82 | convolution fusion | flops 219414528 | bytes 8257540 | tf_op jit(solution)/shard_map/pnj,jkc->pnkc/dot_general | solution.py:58
  108.0 0.0 copy-start.13
  108.0 0.2 fusion.64
  108.2 0.1 pad_maximum_fusion.1
  108.2 1.3 copy.41
  109.5 3.8 %all-to-all-start.3 = ((bf16[768,4,128]{2,1,0:T(4,128)(2,1)}), bf16[768,4,128]{2,1,0:T(4,128)(2,1)S(1)}, u32[]{:S(2)}, u32[]{:S(2)}) async-start(bf16[768,4,128]{2,1,0:T(4,128)(2,1)} %copy.41), calls=%async_computation.3 | async-start | bytes 1572864 | tf_op jit(solution)/shard_map/all_to_all | solution.py:100
  113.4 0.0 copy-done.13
  113.4 9.1 %fusion.114 = f32[24,2048,64]{1,2,0:T(8,128)} fusion(bf16[24,64,2048]{2,1,0:T(8,128)(2,1)} %copy-done.1, bf16[2,64,64]{2,1,0:T(8,128)(2,1)S(1)} %copy-done.13), kind=kOutput, calls=%fused_computation.130 | convolution fusion | flops 402653184 | bytes 18890752 | tf_op jit(solution)/shard_map/rcl,cd->rdl/dot_general | solution.py:107
  122.5 11.3 %all-to-all-done.3 = bf16[768,4,128]{2,1,0:T(4,128)(2,1)S(1)} async-done(((bf16[768,4,128]{2,1,0:T(4,128)(2,1)}), bf16[768,4,128]{2,1,0:T(4,128)(2,1)S(1)}, u32[]{:S(2)}, u32[]{:S(2)}) %all-to-all-start.3) | async-done | bytes 786464 | tf_op jit(solution)/shard_map/all_to_all | solution.py:100
  133.8 0.1 copy.42
  133.9 0.1 copy.43
  134.0 0.7 reshape.430
  134.7 9.5 %fusion.15 = bf16[24,64,2048]{2,1,0:T(8,128)(2,1)} fusion(f32[24,2048,64]{1,2,0:T(8,128)} %fusion.114, bf16[24,128,2,64]{3,2,0,1:T(2,128)(2,1)S(1)} %reshape.430, bf16[128,1,2048]{2,0,1:T(8,128)(2,1)S(1)} %copy-done.10, bf16[128,1,2048]{2,0,1:T(8,128)(2,1)S(1)} %copy-done.11), kind=kOutput, calls=%fused_computation.17 | convolution fusion | flops 1642594304 | bytes 20709376 | tf_op jit(solution)/shard_map/rkpc,kpl->rcl/dot_general | solution.py:101
  (13 shorter events, 0.0 us)
Async XLA Ops:
  4.4 5.0 %copy-start.6 = (bf16[2048,1,128]{2,0,1:T(8,128)(2,1)}, bf16[2048,1,128]{2,0,1:T(8,128)(2,1)S(1)}, u32[]{:S(2)}) copy-start(bf16[2048,1,128]{2,0,1:T(8,128)(2,1)S(1)} %get-tuple-element.23) | copy-start | bytes 1572868
  4.4 5.0 %copy-start.8 = (bf16[2048,1,128]{2,0,1:T(8,128)(2,1)}, bf16[2048,1,128]{2,0,1:T(8,128)(2,1)S(1)}, u32[]{:S(2)}) copy-start(bf16[2048,1,128]{2,0,1:T(8,128)(2,1)S(1)} %get-tuple-element.24) | copy-start | bytes 1572868
  10.8 27.9 %all-to-all-start = ((bf16[24,128,128]{2,0,1:T(8,128)(2,1)}), bf16[24,128,128]{2,0,1:T(8,128)(2,1)S(1)}, u32[]{:S(2)}, u32[]{:S(2)}) async-start(bf16[24,128,128]{2,0,1:T(8,128)(2,1)} %copy.27), calls=%async_computation | async-start | bytes 1572864 | tf_op jit(solution)/shard_map/all_to_all | solution.py:97
  27.4 11.4 %copy-start.2 = (f32[1,128,768]{2,1,0:T(8,128)}, f32[1,128,768]{2,1,0:T(8,128)S(1)}, u32[]{:S(2)}) copy-start(f32[1,128,768]{2,1,0:T(8,128)S(1)} %get-tuple-element.21) | copy-start | bytes 1179652
  27.4 11.4 %copy-start.4 = (f32[1,128,768]{2,1,0:T(8,128)}, f32[1,128,768]{2,1,0:T(8,128)S(1)}, u32[]{:S(2)}) copy-start(f32[1,128,768]{2,1,0:T(8,128)S(1)} %get-tuple-element.22) | copy-start | bytes 1179652
  41.9 10.5 %copy-start.12 = (bf16[2,64,64]{2,1,0:T(8,128)(2,1)S(1)}, bf16[2,64,64]{2,1,0:T(8,128)(2,1)}, u32[]{:S(2)}) copy-start(bf16[2,64,64]{2,1,0:T(8,128)(2,1)} %param.5) | copy-start | bytes 49156
  43.3 24.2 %all-to-all-start.1 = ((bf16[768,4,128]{2,1,0:T(4,128)(2,1)}), bf16[768,4,128]{2,1,0:T(4,128)(2,1)S(1)}, u32[]{:S(2)}, u32[]{:S(2)}) async-start(bf16[768,4,128]{2,1,0:T(4,128)(2,1)} %copy.31), calls=%async_computation.1 | async-start | bytes 1572864 | tf_op jit(solution)/shard_map/all_to_all | solution.py:100
  68.5 8.2 %copy-start.7 = (bf16[2048,1,128]{2,0,1:T(8,128)(2,1)S(1)}, bf16[2048,1,128]{2,0,1:T(8,128)(2,1)}, u32[]{:S(2)}) copy-start(bf16[2048,1,128]{2,0,1:T(8,128)(2,1)} %copy-done.6) | copy-start | bytes 1572868
  68.5 8.2 %copy-start.9 = (bf16[2048,1,128]{2,0,1:T(8,128)(2,1)S(1)}, bf16[2048,1,128]{2,0,1:T(8,128)(2,1)}, u32[]{:S(2)}) copy-start(bf16[2048,1,128]{2,0,1:T(8,128)(2,1)} %copy-done.8) | copy-start | bytes 1572868
  76.6 2.7 %copy-start.1 = (bf16[24,64,2048]{2,1,0:T(8,128)(2,1)}, bf16[24,64,2048]{2,1,0:T(8,128)(2,1)S(1)}, u32[]{:S(2)}) copy-start(bf16[24,64,2048]{2,1,0:T(8,128)(2,1)S(1)} %fusion.7) | copy-start | bytes 18874372
  79.4 5.0 %copy-start = (bf16[1,128,64,128]{3,2,1,0:T(8,128)(2,1)S(1)}, bf16[1,128,64,128]{3,2,1,0:T(8,128)(2,1)}, u32[]{:S(2)}) copy-start(bf16[1,128,64,128]{3,2,1,0:T(8,128)(2,1)} %get-tuple-element.7) | copy-start | bytes 6291460
  80.7 24.2 %all-to-all-start.2 = ((bf16[24,128,128]{2,0,1:T(8,128)(2,1)}), bf16[24,128,128]{2,0,1:T(8,128)(2,1)S(1)}, u32[]{:S(2)}, u32[]{:S(2)}) async-start(bf16[24,128,128]{2,0,1:T(8,128)(2,1)} %copy.37), calls=%async_computation.2 | async-start | bytes 1572864 | tf_op jit(solution)/shard_map/all_to_all | solution.py:97
  87.5 17.6 %copy-start.3 = (f32[1,128,768]{2,1,0:T(8,128)S(1)}, f32[1,128,768]{2,1,0:T(8,128)}, u32[]{:S(2)}) copy-start(f32[1,128,768]{2,1,0:T(8,128)} %copy-done.2) | copy-start | bytes 1179652
  87.5 17.6 %copy-start.5 = (f32[1,128,768]{2,1,0:T(8,128)S(1)}, f32[1,128,768]{2,1,0:T(8,128)}, u32[]{:S(2)}) copy-start(f32[1,128,768]{2,1,0:T(8,128)} %copy-done.4) | copy-start | bytes 1179652
  108.0 5.4 %copy-start.13 = (bf16[2,64,64]{2,1,0:T(8,128)(2,1)S(1)}, bf16[2,64,64]{2,1,0:T(8,128)(2,1)}, u32[]{:S(2)}) copy-start(bf16[2,64,64]{2,1,0:T(8,128)(2,1)} %param.5) | copy-start | bytes 49156
  109.5 24.3 %all-to-all-start.3 = ((bf16[768,4,128]{2,1,0:T(4,128)(2,1)}), bf16[768,4,128]{2,1,0:T(4,128)(2,1)S(1)}, u32[]{:S(2)}, u32[]{:S(2)}) async-start(bf16[768,4,128]{2,1,0:T(4,128)(2,1)} %copy.41), calls=%async_computation.3 | async-start | bytes 1572864 | tf_op jit(solution)/shard_map/all_to_all | solution.py:100
  122.5 12.2 %copy-start.10 = (bf16[128,1,2048]{2,0,1:T(8,128)(2,1)S(1)}, bf16[128,1,2048]{2,0,1:T(8,128)(2,1)}, u32[]{:S(2)}) copy-start(bf16[128,1,2048]{2,0,1:T(8,128)(2,1)} %get-tuple-element.25) | copy-start | bytes 1572868
  122.5 12.2 %copy-start.11 = (bf16[128,1,2048]{2,0,1:T(8,128)(2,1)S(1)}, bf16[128,1,2048]{2,0,1:T(8,128)(2,1)}, u32[]{:S(2)}) copy-start(bf16[128,1,2048]{2,0,1:T(8,128)(2,1)} %get-tuple-element.26) | copy-start | bytes 1572868
where the time goes:
time: 145 us; the launch traced here: 144 us
  matrix products  47.2 us (33%)
  waiting for transfers between devices  33.9 us (23%)
  other arithmetic  25.3 us (17%)
  local copies, waits for them, and re-layouts  18.9 us (13%)
  starting transfers between devices  18.5 us (13%)
    dot_general x2, matrix products, shards(): jnp.einsum('rcl,cd->rdl', current, local_weight[layer_idx], preferred_ele...  18.2 us
    dot_general x2, matrix products, shards(): jnp.einsum('rkpc,kpl->rcl', lat_back.reshape(row_count, mode_rows, 2, cha...  17.6 us
    all_to_all x2, waiting for transfers between devices, shards(): lax.all_to_all(rebuilt, 'lat', split_axis=0, concat_axis=1, tiled=True)  17.2 us
    all_to_all x2, waiting for transfers between devices, shards(): lax.all_to_all(lon_modes, 'lat', split_axis=1, concat_axis=0, tiled=True)  16.7 us
    all_to_all x2, starting transfers between devices, shards(): lax.all_to_all(lon_modes, 'lat', split_axis=1, concat_axis=0, tiled=True)  10.9 us
    another operation x2, other arithmetic  9.78 us
    slice x2, other arithmetic, mix_matrix(): real_w = weight[..., :channels]  9.35 us
    all_to_all x2, starting transfers between devices, shards(): lax.all_to_all(rebuilt, 'lat', split_axis=0, concat_axis=1, tiled=True)  7.64 us
  transfers between devices with their start and end apart: 4, of which 4 were waited for; matrix products, arithmetic and copies ran while one was open for 33% of the time, Pallas kernels for 0%

commit v1 on v0

v1 whole, which is shorter than its diff:
```python
import functools
import math

import jax
import jax.numpy as jnp
import ml_dtypes
import numpy as np
from jax import lax
from jax.experimental import pallas as pl
from jax.experimental.pallas import tpu as pltpu
from jax.sharding import PartitionSpec as P

KY = 128
VMEM = 56 * 2**20
F32 = jnp.float32
BF16 = jnp.bfloat16


def rounded(table):
    return np.asarray(table, np.float32).astype(ml_dtypes.bfloat16)


def mode_order(mode_count, devices):
    per_device = mode_count // devices
    return np.arange(mode_count).reshape(devices, per_device).T.reshape(-1)


def lon_tables(lon_count, mode_count, devices):
    modes = mode_order(mode_count, devices).astype(np.int64)[:, None]
    cells = np.arange(lon_count, dtype=np.int64)[None, :]
    angle = 2.0 * np.pi / lon_count * (cells * modes % lon_count)
    both = np.concatenate([np.cos(angle), -np.sin(angle)], axis=0)
    return (rounded(both / math.sqrt(lon_count)), rounded(both / math.sqrt(mode_count)))


def lat_tables(lat_count, kept_count, block_rows):
    index = np.arange(kept_count, dtype=np.int64)
    waves = np.where(index < kept_count // 2, index, lat_count - kept_count + index)
    rowids = np.arange(lat_count, dtype=np.int64)
    latitudes = rowids % block_rows * (lat_count // block_rows) + rowids // block_rows
    angle = 2.0 * np.pi / lat_count * (waves[:, None] * latitudes[None, :] % lat_count)
    both = np.concatenate([np.cos(angle), np.sin(angle)], axis=0)
    return (rounded(both / math.sqrt(lat_count)), rounded(both.T / math.sqrt(kept_count)))


def low_half(shape, channels):
    return lax.broadcasted_iota(jnp.int32, shape, len(shape) - 1) % (2 * channels) < channels


def dot(a, b, dims):
    return lax.dot_general(a, b, (dims, ((), ())), preferred_element_type=F32)


def scatter_modes(modes_out, wide_ref, first_row, rows, block_rows, channels, devices):
    half = modes_out.shape[0] // 2
    per_device = half // devices
    lanes = 2 * channels
    low = low_half((half, lanes), channels)
    for pair in range(rows // 2):
        real = modes_out[:half, pair * lanes : (pair + 1) * lanes]
        imag = modes_out[half:, pair * lanes : (pair + 1) * lanes]
        even = jnp.where(low, real, pltpu.roll(imag, channels, 1))
        odd = jnp.where(low, pltpu.roll(real, channels, 1), imag)
        for offset, values in ((0, even), (1, odd)):
            row = first_row + 2 * pair + offset
            for k in range(per_device):
                wide_ref[k, pl.ds(row, devices, stride=block_rows), :] = values[
                    k * devices : (k + 1) * devices
                ]


def gather_modes(wide_ref, first_row, rows, block_rows, channels, devices):
    lanes = 2 * channels
    per_device = wide_ref.shape[0]
    low = low_half((per_device * devices, lanes), channels)
    reals, imags = [], []
    for pair in range(rows // 2):
        even, odd = [
            jnp.concatenate(
                [
                    wide_ref[
                        k, pl.ds(first_row + 2 * pair + offset, devices, stride=block_rows), :
                    ]
                    for k in range(per_device)
                ],
                axis=0,
            )
            for offset in range(2)
        ]
        reals.append(jnp.where(low, even, pltpu.roll(odd, channels, 1)))
        imags.append(jnp.where(low, pltpu.roll(even, channels, 1), odd))
    return jnp.concatenate(
        [jnp.concatenate(reals, axis=1), jnp.concatenate(imags, axis=1)], axis=0
    )


def pack(wide_ref, out_ref):
    lanes = wide_ref.shape[2]
    for k in range(wide_ref.shape[0]):
        out_ref[:, k * lanes : (k + 1) * lanes] = wide_ref[k].astype(BF16)


def unpack(in_ref, wide_ref):
    lanes = wide_ref.shape[2]
    for k in range(wide_ref.shape[0]):
        wide_ref[k] = in_ref[:, k * lanes : (k + 1) * lanes].astype(F32)


def wide_scratch(shape, channels):
    return pltpu.VMEM((shape[1] // (2 * channels), shape[0], 2 * channels), F32)


def first_kernel(block_rows, channels, devices, rows, fields_ref, table_ref, out_ref, wide_ref):
    step = pl.program_id(0)
    modes = dot(table_ref[...], fields_ref[...], ((1,), (1,)))
    scatter_modes(modes, wide_ref, step * rows, rows, block_rows, channels, devices)

    @pl.when(step == pl.num_programs(0) - 1)
    def _():
        pack(wide_ref, out_ref)


def first_transform(fields, table, block_rows, channels, devices, rows):
    lon_count = fields.shape[1]
    block = rows * channels
    wide = (devices * block_rows, table.shape[0] // devices * channels)
    return pl.pallas_call(
        functools.partial(first_kernel, block_rows, channels, devices, rows),
        grid=(block_rows // rows,),
        in_specs=[
            pl.BlockSpec((block, lon_count), lambda g: (g, 0)),
            pl.BlockSpec(table.shape, lambda g: (0, 0)),
        ],
        out_specs=pl.BlockSpec(wide, lambda g: (0, 0)),
        out_shape=jax.ShapeDtypeStruct(wide, BF16),
        scratch_shapes=[wide_scratch(wide, channels)],
        compiler_params=pltpu.CompilerParams(vmem_limit_bytes=VMEM),
    )(fields, table)


def middle_kernel(channels, values_ref, weight_ref, forward_ref, backward_ref, out_ref):
    kept = forward_ref.shape[0] // 2
    lanes = 2 * channels
    products = dot(forward_ref[...], values_ref[...], ((1,), (0,)))
    low = low_half((kept, lanes), channels)
    low_w = low_half((channels, lanes), channels)
    for k in range(values_ref.shape[1] // lanes):
        part = slice(k * lanes, (k + 1) * lanes)
        turned = pltpu.roll(products[kept:, part], channels, 1)
        modes = (products[:kept, part] + jnp.where(low, turned, -turned)).astype(BF16)
        weight = weight_ref[k].astype(F32)
        swapped = pltpu.roll(weight, channels, 1)
        mixing = jnp.concatenate([weight, jnp.where(low_w, -swapped, swapped)], axis=0)
        mixed = dot(modes, mixing.astype(BF16), ((1,), (0,)))
        swapped = pltpu.roll(mixed, channels, 1)
        both = jnp.concatenate([mixed, jnp.where(low, -swapped, swapped)], axis=0).astype(BF16)
        out_ref[:, part] = dot(backward_ref[...], both, ((1,), (0,))).astype(BF16)


def middle(values, weight, forward, backward, channels):
    return pl.pallas_call(
        functools.partial(middle_kernel, channels),
        out_shape=jax.ShapeDtypeStruct(values.shape, BF16),
        compiler_params=pltpu.CompilerParams(vmem_limit_bytes=VMEM),
    )(values, weight, forward, backward)


def gelu(x):
    u = x * (math.sqrt(2.0 / math.pi) + (0.044715 * math.sqrt(2.0 / math.pi)) * (x * x))
    half = 0.5 * x
    return half * jnp.tanh(u) + half


def back_kernel(
    block_rows, channels, devices, rows, again,
    modes_ref, field_ref, local_ref, back_ref, *rest,
):
    if again:
        table_ref, field_out_ref, modes_out_ref, wide_ref, wide_out_ref = rest
    else:
        field_out_ref, wide_ref = rest
    step = pl.program_id(0)

    @pl.when(step == 0)
    def _():
        unpack(modes_ref, wide_ref)

    modes = gather_modes(wide_ref, step * rows, rows, block_rows, channels, devices)
    modes = modes.T.astype(BF16)
    lhs = jnp.concatenate([modes, local_ref[...]], axis=1)
    lon_count = field_ref.shape[1]
    chunk = min(512, lon_count)
    total = None
    for start in range(0, lon_count, chunk):
        part = slice(start, start + chunk)
        rhs = jnp.concatenate([back_ref[:, part], field_ref[:, part]], axis=0)
        new = gelu(dot(lhs, rhs, ((1,), (0,)))).astype(BF16)
        field_out_ref[:, part] = new
        if again:
            product = dot(table_ref[:, part], new, ((1,), (1,)))
            total = product if total is None else total + product
    if again:
        scatter_modes(total, wide_out_ref, step * rows, rows, block_rows, channels, devices)

        @pl.when(step == pl.num_programs(0) - 1)
        def _():
            pack(wide_out_ref, modes_out_ref)


def back_transform(modes, field, local, back, table, block_rows, channels, devices, rows):
    again = table is not None
    block = rows * channels
    lon_count = field.shape[1]
    whole = lambda array: pl.BlockSpec(array.shape, lambda g: (0, 0))
    field_spec = pl.BlockSpec((block, lon_count), lambda g: (g, 0))
    args = [modes, field, local, back] + ([table] if again else [])
    out_specs, out_shape = [field_spec], [jax.ShapeDtypeStruct(field.shape, BF16)]
    scratch = [wide_scratch(modes.shape, channels)]
    if again:
        out_specs.append(whole(modes))
        out_shape.append(jax.ShapeDtypeStruct(modes.shape, BF16))
        scratch.append(wide_scratch(modes.shape, channels))
    return pl.pallas_call(
        functools.partial(back_kernel, block_rows, channels, devices, rows, again),
        grid=(block_rows // rows,),
        in_specs=[whole(modes), field_spec, whole(local), whole(back)]
        + ([whole(table)] if again else []),
        out_specs=out_specs,
        out_shape=out_shape,
        scratch_shapes=scratch,
        compiler_params=pltpu.CompilerParams(vmem_limit_bytes=VMEM),
    )(*args)


def exchange(array, devices):
    parts = array.reshape(devices, array.shape[0] // devices, array.shape[1])
    return lax.all_to_all(parts, "lat", 0, 0, tiled=True).reshape(array.shape)


def shards(fields, spectral_weight, local_weight):
    block_rows, channels, lon_count = fields.shape
    layer_count, mode_count = spectral_weight.shape[:2]
    devices = lax.axis_size("lat")
    rows = max(2, 256 // channels)
    per_device = mode_count // devices
    forward_lon, backward_lon = lon_tables(lon_count, mode_count, devices)
    forward_lat, backward_lat = lat_tables(block_rows * devices, KY, block_rows)
    own = lax.dynamic_slice_in_dim(
        spectral_weight, lax.axis_index("lat") * per_device, per_device, 1
    )
    mixers = jnp.einsum(
        "rs,lcd->lrdsc", jnp.eye(rows, dtype=BF16), local_weight
    ).reshape(layer_count, rows * channels, rows * channels)
    sizes = (block_rows, channels, devices, rows)
    current = fields.reshape(block_rows * channels, lon_count)
    modes = first_transform(current, forward_lon, *sizes)
    for layer in range(layer_count):
        arrived = exchange(modes, devices)
        rebuilt = middle(arrived, own[layer], forward_lat, backward_lat, channels)
        returned = exchange(rebuilt, devices)
        last = layer == layer_count - 1
        result = back_transform(
            returned, current, mixers[layer], backward_lon, None if last else forward_lon, *sizes
        )
        current, modes = (result[0], None) if last else result
    return current.reshape(fields.shape)


def solution(mesh):
    return jax.shard_map(
        shards,
        mesh=mesh,
        in_specs=(P(("grp", "lat"), None, None), P(), P()),
        out_specs=P(("grp", "lat"), None, None),
        check_vma=False,
    )
```

time: 145 us -> 144 us (level)
  matrix products: 47.2 us -> 0 us
  Pallas kernels: 0 us -> 39.8 us
  other arithmetic: 25.3 us -> 0.27 us
  blocking collectives: 0 us -> 24.4 us
  waiting for transfers between devices: 33.9 us -> 58 us
  local copies, waits for them, and re-layouts: 18.9 us -> 6.23 us
  starting transfers between devices: 18.5 us -> 14.5 us
    dot_general x10 -> x0, matrix products: 47.2 us -> none  [the longest x2 18.2 us: shards(): jnp.einsum('rcl,cd->rdl', current, local_weight[layer_idx], preferred_ele...]
    pallas_call x0 -> x5, Pallas kernels: none -> 39.8 us  [the longest x2 24.4 us: back_transform(): pl.pallas_call(functools.partial(back_kernel, block_rows, channels, devic...]
    all_to_all x0 -> x1, blocking collectives: none -> 24.4 us  [exchange(): return lax.all_to_all(parts, 'lat', 0, 0, tiled=True).reshape(array.shape)]
    all_to_all x4 -> x3, waiting for transfers between devices: 33.9 us -> 58 us  [exchange(): return lax.all_to_all(parts, 'lat', 0, 0, tiled=True).reshape(array.shape)]
    another operation x2 -> x1, other arithmetic: 9.78 us -> 0.01 us
    slice x2 -> x0, other arithmetic: 9.35 us -> none  [mix_matrix(): real_w = weight[..., :channels]]
    unnamed x30 -> x9, local copies, waits for them, and re-layouts: 7.18 us -> 2.76 us
    cos x2 -> x0, other arithmetic: 4.42 us -> none  [lat_tables(): jnp.cos(angle)]
  transfers between devices with their start and end apart: 4 -> 3, of which waited for: 4 -> 3; matrix products, arithmetic and copies ran while one was open for 33% -> 3% of each run, Pallas kernels for 0% -> 0%
where the time goes in v1:
time: 144 us; the launch traced here: 143 us
  waiting for transfers between devices  58 us (40%)
  Pallas kernels  39.8 us (28%)
  blocking collectives  24.4 us (17%)
  starting transfers between devices  14.5 us (10%)
  local copies, waits for them, and re-layouts  6.23 us (4%)
    all_to_all x3, waiting for transfers between devices, exchange(): return lax.all_to_all(parts, 'lat', 0, 0, tiled=True).reshape(array.shape)  58 us
    pallas_call x2, Pallas kernels, back_transform(): pl.pallas_call(functools.partial(back_kernel, block_rows, channels, devic...  24.4 us
    all_to_all x1, blocking collectives, exchange(): return lax.all_to_all(parts, 'lat', 0, 0, tiled=True).reshape(array.shape)  24.4 us
    all_to_all x3, starting transfers between devices, exchange(): return lax.all_to_all(parts, 'lat', 0, 0, tiled=True).reshape(array.shape)  14.5 us
    pallas_call x2, Pallas kernels, middle(): pl.pallas_call(functools.partial(middle_kernel, channels), out_shape=jax....  8.08 us
    pallas_call x1, Pallas kernels, first_transform(): pl.pallas_call(functools.partial(first_kernel, block_rows, channels, devi...  7.36 us
  transfers between devices with their start and end apart: 3, of which 3 were waited for; matrix products, arithmetic and copies ran while one was open for 3% of the time, Pallas kernels for 0%

profile of v1, /device:TPU:0, one launch (start us, length us, event | category | flops | bytes accessed | tf_op | source)
XLA Modules:
  0.0 143.3 jit_solution(5785814418944405238)
XLA Ops:
  0.0 0.0 copy-start.3
  0.0 7.4 %shard_map.73 = bf16[768,512]{1,0:T(8,128)(2,1)} custom-call(bf16[1536,2048]{1,0:T(8,128)(2,1)} %bitcast.16, bf16[256,2048]{1,0:T(8,128)(2,1)} %constant.18.clone.table_ref.rest_0_), custom_call_target="tpu_custom_call" | custom-call | tf_op jit(solution)/shard_map/pallas_call | solution.py:127
  7.4 7.3 %all-to-all-start = ((bf16[32,24,512]{2,1,0:T(8,128)(2,1)}), bf16[32,24,512]{2,1,0:T(8,128)(2,1)S(1)}, u32[]{:S(2)}, u32[]{:S(2)}) async-start(bf16[32,24,512]{2,1,0:T(8,128)(2,1)} %bitcast.24), calls=%async_computation | async-start | bytes 1572864 | tf_op jit(solution)/shard_map/all_to_all | solution.py:237
  14.7 1.5 %dynamic-slice_bitcast_fusion = (bf16[4,64,128]{2,1,0:T(8,128)(2,1)}, bf16[4,64,128]{2,1,0:T(8,128)(2,1)}) fusion(bf16[2,128,64,128]{3,2,1,0:T(8,128)(2,1)} %param.8, s32[]{:T(128)S(6)} %add.4, s32[]{:T(128)S(6)} %select_n.3), kind=kLoop, calls=%fused_computation.1 | loop fusion | bytes 262152 | tf_op jit(solution)/shard_map/squeeze | solution.py:259
  16.2 19.1 %all-to-all-done = bf16[32,24,512]{2,1,0:T(8,128)(2,1)S(1)} async-done(((bf16[32,24,512]{2,1,0:T(8,128)(2,1)}), bf16[32,24,512]{2,1,0:T(8,128)(2,1)S(1)}, u32[]{:S(2)}, u32[]{:S(2)}) %all-to-all-start) | async-done | bytes 786464 | tf_op jit(solution)/shard_map/all_to_all | solution.py:237
  35.3 0.0 copy-start.2
  35.3 0.9 copy-done.2
  36.2 4.0 %shard_map.74 = bf16[768,512]{1,0:T(8,128)(2,1)} custom-call(bf16[768,512]{1,0:T(8,128)(2,1)} %bitcast.20, bf16[4,64,128]{2,1,0:T(8,128)(2,1)} %get-tuple-element.10.weight_ref, bf16[256,768]{1,0:T(8,128)(2,1)} %constant.19.clone.forward_ref, bf16[768,256]{1,0:T(8,128)(2,1)} %constant.20.clone.backward_ref), custom_call_target="tpu_custom_call" | custom-call | tf_op jit(solution)/shard_map/pallas_call | solution.py:161
  40.2 3.6 %all-to-all-start.1 = ((bf16[32,24,512]{2,1,0:T(8,128)(2,1)}), bf16[32,24,512]{2,1,0:T(8,128)(2,1)S(1)}, u32[]{:S(2)}, u32[]{:S(2)}) async-start(bf16[32,24,512]{2,1,0:T(8,128)(2,1)} %bitcast.21), calls=%async_computation.1 | async-start | bytes 1572864 | tf_op jit(solution)/shard_map/all_to_all | solution.py:237
  43.8 0.0 copy-done.3
  43.9 0.1 copy.8
  44.0 0.3 multiply_bitcast_fusion
  44.2 0.2 fusion.1
  44.4 0.9 squeeze.13.local_ref
  45.3 19.2 %all-to-all-done.1 = bf16[32,24,512]{2,1,0:T(8,128)(2,1)S(1)} async-done(((bf16[32,24,512]{2,1,0:T(8,128)(2,1)}), bf16[32,24,512]{2,1,0:T(8,128)(2,1)S(1)}, u32[]{:S(2)}, u32[]{:S(2)}) %all-to-all-start.1) | async-done | bytes 786464 | tf_op jit(solution)/shard_map/all_to_all | solution.py:237
  64.5 0.0 copy-start.1
  64.5 0.9 copy-done.1
  65.3 13.7 %shard_map.75 = (bf16[1536,2048]{1,0:T(8,128)(2,1)}, bf16[768,512]{1,0:T(8,128)(2,1)}) custom-call(bf16[768,512]{1,0:T(8,128)(2,1)} %bitcast.19, bf16[1536,2048]{1,0:T(8,128)(2,1)} %bitcast.17, bf16[256,256]{1,0:T(8,128)(2,1)} %squeeze.13.local_ref, bf16[256,2048]{1,0:T(8,128)(2,1)} %constant.21.clone.back_ref, ...), custom_call_target="tpu_custom_call" | custom-call | tf_op jit(solution)/shard_map/pallas_call | solution.py:223
  79.0 24.4 %all_to_all.20 = bf16[32,24,512]{2,1,0:T(8,128)(2,1)} all-to-all(bf16[32,24,512]{2,1,0:T(8,128)(2,1)} %bitcast.25), channel_id=1, replica_groups=mesh['grp'=1,'lat'=32] {'lat'}, dimensions={0} | all-to-all | bytes 1572864 | tf_op jit(solution)/shard_map/all_to_all | solution.py:237
  103.4 4.0 %shard_map.76 = bf16[768,512]{1,0:T(8,128)(2,1)} custom-call(bf16[768,512]{1,0:T(8,128)(2,1)} %bitcast.23, bf16[4,64,128]{2,1,0:T(8,128)(2,1)} %get-tuple-element.9.weight_ref, bf16[256,768]{1,0:T(8,128)(2,1)} %constant.19.clone.forward_ref, bf16[768,256]{1,0:T(8,128)(2,1)} %constant.20.clone.backward_ref), custom_call_target="tpu_custom_call" | custom-call | tf_op jit(solution)/shard_map/pallas_call | solution.py:161
  107.4 3.6 %all-to-all-start.3 = ((bf16[32,24,512]{2,1,0:T(8,128)(2,1)}), bf16[32,24,512]{2,1,0:T(8,128)(2,1)S(1)}, u32[]{:S(2)}, u32[]{:S(2)}) async-start(bf16[32,24,512]{2,1,0:T(8,128)(2,1)} %bitcast.22), calls=%async_computation.3 | async-start | bytes 1572864 | tf_op jit(solution)/shard_map/all_to_all | solution.py:237
  111.1 0.9 squeeze.15.local_ref
  111.9 19.7 %all-to-all-done.3 = bf16[32,24,512]{2,1,0:T(8,128)(2,1)S(1)} async-done(((bf16[32,24,512]{2,1,0:T(8,128)(2,1)}), bf16[32,24,512]{2,1,0:T(8,128)(2,1)S(1)}, u32[]{:S(2)}, u32[]{:S(2)}) %all-to-all-start.3) | async-done | bytes 786464 | tf_op jit(solution)/shard_map/all_to_all | solution.py:237
  131.7 0.0 copy-start
  131.7 0.9 copy-done
  132.6 10.7 %shard_map.77 = bf16[1536,2048]{1,0:T(8,128)(2,1)} custom-call(bf16[768,512]{1,0:T(8,128)(2,1)} %bitcast.18, bf16[1536,2048]{1,0:T(8,128)(2,1)} %get-tuple-element.8.field_ref, bf16[256,256]{1,0:T(8,128)(2,1)} %squeeze.15.local_ref, bf16[256,2048]{1,0:T(8,128)(2,1)} %constant.21.clone.back_ref), custom_call_target="tpu_custom_call" | custom-call | tf_op jit(solution)/shard_map/pallas_call | solution.py:223
  (1 shorter events, 0.0 us)
Async XLA Ops:
  0.0 43.8 %copy-start.3 = (bf16[2,64,64]{2,1,0:T(8,128)(2,1)S(1)}, bf16[2,64,64]{2,1,0:T(8,128)(2,1)}, u32[]{:S(2)}) copy-start(bf16[2,64,64]{2,1,0:T(8,128)(2,1)} %param.9) | copy-start | bytes 49156
  7.4 27.9 %all-to-all-start = ((bf16[32,24,512]{2,1,0:T(8,128)(2,1)}), bf16[32,24,512]{2,1,0:T(8,128)(2,1)S(1)}, u32[]{:S(2)}, u32[]{:S(2)}) async-start(bf16[32,24,512]{2,1,0:T(8,128)(2,1)} %bitcast.24), calls=%async_computation | async-start | bytes 1572864 | tf_op jit(solution)/shard_map/all_to_all | solution.py:237
  35.3 0.9 copy-start.2
  40.2 24.2 %all-to-all-start.1 = ((bf16[32,24,512]{2,1,0:T(8,128)(2,1)}), bf16[32,24,512]{2,1,0:T(8,128)(2,1)S(1)}, u32[]{:S(2)}, u32[]{:S(2)}) async-start(bf16[32,24,512]{2,1,0:T(8,128)(2,1)} %bitcast.21), calls=%async_computation.1 | async-start | bytes 1572864 | tf_op jit(solution)/shard_map/all_to_all | solution.py:237
  64.5 0.9 copy-start.1
  107.4 24.2 %all-to-all-start.3 = ((bf16[32,24,512]{2,1,0:T(8,128)(2,1)}), bf16[32,24,512]{2,1,0:T(8,128)(2,1)S(1)}, u32[]{:S(2)}, u32[]{:S(2)}) async-start(bf16[32,24,512]{2,1,0:T(8,128)(2,1)} %bitcast.22), calls=%async_computation.3 | async-start | bytes 1572864 | tf_op jit(solution)/shard_map/all_to_all | solution.py:237
  131.7 0.9 copy-start

commit v2 on v1

--- a/solution.py
+++ b/solution.py
@@ -11,7 +11,6 @@
 from jax.sharding import PartitionSpec as P
 
 KY = 128
-VMEM = 56 * 2**20
 F32 = jnp.float32
 BF16 = jnp.bfloat16
 
@@ -110,32 +109,75 @@
     return pltpu.VMEM((shape[1] // (2 * channels), shape[0], 2 * channels), F32)
 
 
-def first_kernel(block_rows, channels, devices, rows, fields_ref, table_ref, out_ref, wide_ref):
-    step = pl.program_id(0)
-    modes = dot(table_ref[...], fields_ref[...], ((1,), (1,)))
-    scatter_modes(modes, wide_ref, step * rows, rows, block_rows, channels, devices)
-
-    @pl.when(step == pl.num_programs(0) - 1)
-    def _():
-        pack(wide_ref, out_ref)
+def in_vmem(array):
+    return pltpu.with_memory_space_constraint(array, pltpu.VMEM)
+
+
+def in_hbm(array):
+    return pltpu.with_memory_space_constraint(array, pltpu.HBM)
+
+
+def params(limit):
+    return pltpu.CompilerParams(vmem_limit_bytes=limit * 2**20)
+
+
+OUTSIDE = pl.BlockSpec(memory_space=pltpu.HBM)
+RESIDENT = pl.BlockSpec(memory_space=pltpu.VMEM)
+
+
+def first_kernel(
+    block_rows, channels, devices, rows,
+    fields_ref, table_ref, modes_ref, copy_ref, table_copy, wide_ref, sems,
+):
+    steps, block = block_rows // rows, rows * channels
+    copies = [pltpu.make_async_copy(table_ref, table_copy, sems.at[steps])]
+    for step in range(steps):
+        part = pl.ds(step * block, block)
+        copies.append(
+            pltpu.make_async_copy(fields_ref.at[part], copy_ref.at[part], sems.at[step])
+        )
+    for copy in copies:
+        copy.start()
+    copies[0].wait()
+    for step in range(steps):
+        copies[step + 1].wait()
+        part = slice(step * block, (step + 1) * block)
+        modes = dot(table_copy[...], copy_ref[part, :], ((1,), (1,)))
+        scatter_modes(modes, wide_ref, step * rows, rows, block_rows, channels, devices)
+    pack(wide_ref, modes_ref)
 
 
 def first_transform(fields, table, block_rows, channels, devices, rows):
-    lon_count = fields.shape[1]
-    block = rows * channels
-    wide = (devices * block_rows, table.shape[0] // devices * channels)
+    modes_shape = (devices * block_rows, table.shape[0] // devices * channels)
     return pl.pallas_call(
         functools.partial(first_kernel, block_rows, channels, devices, rows),
-        grid=(block_rows // rows,),
-        in_specs=[
-            pl.BlockSpec((block, lon_count), lambda g: (g, 0)),
-            pl.BlockSpec(table.shape, lambda g: (0, 0)),
+        in_specs=[OUTSIDE, OUTSIDE],
+        out_specs=RESIDENT,
+        out_shape=pltpu.VMEM(modes_shape, BF16),
+        scratch_shapes=[
+            pltpu.VMEM(fields.shape, BF16),
+            pltpu.VMEM(table.shape, BF16),
+            wide_scratch(modes_shape, channels),
+            pltpu.SemaphoreType.DMA((block_rows // rows + 1,)),
         ],
-        out_specs=pl.BlockSpec(wide, lambda g: (0, 0)),
-        out_shape=jax.ShapeDtypeStruct(wide, BF16),
-        scratch_shapes=[wide_scratch(wide, channels)],
-        compiler_params=pltpu.CompilerParams(vmem_limit_bytes=VMEM),
-    )(fields, table)
+        compiler_params=params(24),
+    )(in_hbm(fields), in_hbm(table))
+
+
+def local_kernel(field_ref, weight_ref, out_ref):
+    out_ref[...] = dot(weight_ref[...], field_ref[...], ((1,), (0,))).astype(BF16)
+
+
+def local_mix(field, weight):
+    block = pl.BlockSpec((weight.shape[0], field.shape[1]), lambda g: (g, 0))
+    return pl.pallas_call(
+        local_kernel,
+        grid=(field.shape[0] // weight.shape[0],),
+        in_specs=[block, pl.BlockSpec(weight.shape, lambda g: (0, 0))],
+        out_specs=block,
+        out_shape=pltpu.HBM(field.shape, BF16),
+        compiler_params=params(16),
+    )(in_hbm(field), weight)
 
 
 def middle_kernel(channels, values_ref, weight_ref, forward_ref, backward_ref, out_ref):
@@ -160,9 +202,11 @@
 def middle(values, weight, forward, backward, channels):
     return pl.pallas_call(
         functools.partial(middle_kernel, channels),
-        out_shape=jax.ShapeDtypeStruct(values.shape, BF16),
-        compiler_params=pltpu.CompilerParams(vmem_limit_bytes=VMEM),
-    )(values, weight, forward, backward)
+        in_specs=[RESIDENT] * 4,
+        out_specs=RESIDENT,
+        out_shape=pltpu.VMEM(values.shape, BF16),
+        compiler_params=params(24),
+    )(in_vmem(values), in_vmem(weight), in_vmem(forward), in_vmem(backward))
 
 
 def gelu(x):
@@ -171,64 +215,77 @@
     return half * jnp.tanh(u) + half
 
 
-def back_kernel(
-    block_rows, channels, devices, rows, again,
-    modes_ref, field_ref, local_ref, back_ref, *rest,
-):
+def spectral_block(modes, local_ref, back_ref, out_ref, first):
+    lon_count = back_ref.shape[1]
+    chunk = min(256, lon_count)
+    for start in range(0, lon_count, chunk):
+        place = (slice(first, first + modes.shape[0]), slice(start, start + chunk))
+        total = dot(modes, back_ref[:, place[1]], ((1,), (0,))) + local_ref[place].astype(F32)
+        out_ref[place] = gelu(total).astype(BF16)
+
+
+def row_copies(source_ref, target_ref, sems, steps):
+    block = source_ref.shape[0] // steps
+    parts = [pl.ds(step * block, block) for step in range(steps)]
+    return [
+        pltpu.make_async_copy(source_ref.at[part], target_ref.at[part], sems.at[step])
+        for step, part in enumerate(parts)
+    ]
+
+
+def back_kernel(block_rows, channels, devices, rows, again, modes_ref, local_ref, back_ref, *rest):
     if again:
-        table_ref, field_out_ref, modes_out_ref, wide_ref, wide_out_ref = rest
+        table_ref, field_out_ref, modes_out_ref = rest[:3]
+        wide_out_ref = rest[-1]
+        rest = rest[3:-1]
     else:
-        field_out_ref, wide_ref = rest
-    step = pl.program_id(0)
-
-    @pl.when(step == 0)
-    def _():
-        unpack(modes_ref, wide_ref)
-
-    modes = gather_modes(wide_ref, step * rows, rows, block_rows, channels, devices)
-    modes = modes.T.astype(BF16)
-    lhs = jnp.concatenate([modes, local_ref[...]], axis=1)
-    lon_count = field_ref.shape[1]
-    chunk = min(512, lon_count)
-    total = None
-    for start in range(0, lon_count, chunk):
-        part = slice(start, start + chunk)
-        rhs = jnp.concatenate([back_ref[:, part], field_ref[:, part]], axis=0)
-        new = gelu(dot(lhs, rhs, ((1,), (0,)))).astype(BF16)
-        field_out_ref[:, part] = new
+        field_out_ref = rest[0]
+        rest = rest[1:]
+    local_copy, field_ref, wide_ref, in_sems, out_sems = rest
+    steps, block = block_rows // rows, rows * channels
+    arriving = row_copies(local_ref, local_copy, in_sems, steps)
+    leaving = row_copies(field_ref, field_out_ref, out_sems, steps)
+    for copy in arriving:
+        copy.start()
+    unpack(modes_ref, wide_ref)
+    for step in range(steps):
+        modes = gather_modes(wide_ref, step * rows, rows, block_rows, channels, devices)
+        arriving[step].wait()
+        spectral_block(modes.T.astype(BF16), local_copy, back_ref, field_ref, step * block)
+        leaving[step].start()
         if again:
-            product = dot(table_ref[:, part], new, ((1,), (1,)))
-            total = product if total is None else total + product
+            field = field_ref[step * block : (step + 1) * block, :]
+            product = dot(table_ref[...], field, ((1,), (1,)))
+            scatter_modes(product, wide_out_ref, step * rows, rows, block_rows, channels, devices)
     if again:
-        scatter_modes(total, wide_out_ref, step * rows, rows, block_rows, channels, devices)
-
-        @pl.when(step == pl.num_programs(0) - 1)
-        def _():
-            pack(wide_out_ref, modes_out_ref)
-
-
-def back_transform(modes, field, local, back, table, block_rows, channels, devices, rows):
+        pack(wide_out_ref, modes_out_ref)
+    for copy in leaving:
+        copy.wait()
+
+
+def back_transform(modes, local, back, table, block_rows, channels, devices, rows):
     again = table is not None
-    block = rows * channels
-    lon_count = field.shape[1]
-    whole = lambda array: pl.BlockSpec(array.shape, lambda g: (0, 0))
-    field_spec = pl.BlockSpec((block, lon_count), lambda g: (g, 0))
-    args = [modes, field, local, back] + ([table] if again else [])
-    out_specs, out_shape = [field_spec], [jax.ShapeDtypeStruct(field.shape, BF16)]
-    scratch = [wide_scratch(modes.shape, channels)]
+    steps = block_rows // rows
+    scratch = [
+        pltpu.VMEM(local.shape, BF16),
+        pltpu.VMEM(local.shape, BF16),
+        wide_scratch(modes.shape, channels),
+        pltpu.SemaphoreType.DMA((steps,)),
+        pltpu.SemaphoreType.DMA((steps,)),
+    ]
+    args = [in_vmem(modes), in_hbm(local), in_vmem(back)]
+    out_shape = [pltpu.HBM(local.shape, BF16)]
     if again:
-        out_specs.append(whole(modes))
-        out_shape.append(jax.ShapeDtypeStruct(modes.shape, BF16))
+        args.append(in_vmem(table))
+        out_shape.append(pltpu.VMEM(modes.shape, BF16))
         scratch.append(wide_scratch(modes.shape, channels))
     return pl.pallas_call(
         functools.partial(back_kernel, block_rows, channels, devices, rows, again),
-        grid=(block_rows // rows,),
-        in_specs=[whole(modes), field_spec, whole(local), whole(back)]
-        + ([whole(table)] if again else []),
-        out_specs=out_specs,
+        in_specs=[RESIDENT, OUTSIDE] + [RESIDENT] * (len(args) - 2),
+        out_specs=[OUTSIDE] + [RESIDENT] * (len(out_shape) - 1),
         out_shape=out_shape,
         scratch_shapes=scratch,
-        compiler_params=pltpu.CompilerParams(vmem_limit_bytes=VMEM),
+        compiler_params=params(32),
     )(*args)
 
 
@@ -251,19 +308,22 @@
     mixers = jnp.einsum(
         "rs,lcd->lrdsc", jnp.eye(rows, dtype=BF16), local_weight
     ).reshape(layer_count, rows * channels, rows * channels)
-    sizes = (block_rows, channels, devices, rows)
-    current = fields.reshape(block_rows * channels, lon_count)
-    modes = first_transform(current, forward_lon, *sizes)
+    wide_rows = 2 * rows if block_rows % (2 * rows) == 0 else rows
+    sizes = (block_rows, channels, devices)
+    field = fields.reshape(block_rows * channels, lon_count)
+    modes = first_transform(field, forward_lon, *sizes, rows)
     for layer in range(layer_count):
         arrived = exchange(modes, devices)
         rebuilt = middle(arrived, own[layer], forward_lat, backward_lat, channels)
         returned = exchange(rebuilt, devices)
-        last = layer == layer_count - 1
-        result = back_transform(
-            returned, current, mixers[layer], backward_lon, None if last else forward_lon, *sizes
-        )
-        current, modes = (result[0], None) if last else result
-    return current.reshape(fields.shape)
+        local = local_mix(field, mixers[layer])
+        if layer < layer_count - 1:
+            field, modes = back_transform(
+                returned, local, backward_lon, forward_lon, *sizes, wide_rows
+            )
+        else:
+            field = back_transform(returned, local, backward_lon, None, *sizes, rows)[0]
+    return field.reshape(fields.shape)
 
 
 def solution(mesh):

time: 144 us -> 132 us (0.917)
  waiting for transfers between devices: 58 us -> 41.8 us
  Pallas kernels: 39.8 us -> 46.9 us
  local copies, waits for them, and re-layouts: 6.23 us -> 3.29 us
    all_to_all x3, waiting for transfers between devices: 58 us -> 41.8 us  [exchange(): return lax.all_to_all(parts, 'lat', 0, 0, tiled=True).reshape(array.shape)]
    pallas_call x2 -> x4, Pallas kernels: 8.08 us -> 21.4 us  [the longest x2 16.1 us: local_mix(): pl.pallas_call(local_kernel, grid=(field.shape[0] // weight.shape[0],), i...]
    pallas_call x2, Pallas kernels: 24.4 us -> 18 us  [back_transform(): pl.pallas_call(functools.partial(back_kernel, block_rows, channels, devic...]
    unnamed x9 -> x13, local copies, waits for them, and re-layouts: 2.76 us -> 0.12 us
  transfers between devices with their start and end apart: 3 -> 3, of which waited for: 3 -> 3; matrix products, arithmetic and copies ran while one was open for 3% -> 3% of each run, Pallas kernels for 0% -> 12%
where the time goes in v2:
time: 132 us; the launch traced here: 131 us
  Pallas kernels  46.9 us (36%)
  waiting for transfers between devices  41.8 us (32%)
  blocking collectives  24 us (18%)
  starting transfers between devices  14.9 us (11%)
  local copies, waits for them, and re-layouts  3.29 us (2%)
    all_to_all x3, waiting for transfers between devices, exchange(): return lax.all_to_all(parts, 'lat', 0, 0, tiled=True).reshape(array.shape)  41.8 us
    all_to_all x1, blocking collectives, exchange(): return lax.all_to_all(parts, 'lat', 0, 0, tiled=True).reshape(array.shape)  24 us
    pallas_call x2, Pallas kernels, back_transform(): pl.pallas_call(functools.partial(back_kernel, block_rows, channels, devic...  18 us
    pallas_call x2, Pallas kernels, local_mix(): pl.pallas_call(local_kernel, grid=(field.shape[0] // weight.shape[0],), i...  16.1 us
    all_to_all x3, starting transfers between devices, exchange(): return lax.all_to_all(parts, 'lat', 0, 0, tiled=True).reshape(array.shape)  14.9 us
    pallas_call x1, Pallas kernels, first_transform(): pl.pallas_call(functools.partial(first_kernel, block_rows, channels, devi...  7.41 us
    pallas_call x2, Pallas kernels, middle(): pl.pallas_call(functools.partial(middle_kernel, channels), in_specs=[RESI...  5.32 us
  transfers between devices with their start and end apart: 3, of which 3 were waited for; matrix products, arithmetic and copies ran while one was open for 3% of the time, Pallas kernels for 12%

profile of v2, /device:TPU:0, one launch (start us, length us, event | category | flops | bytes accessed | tf_op | source)
XLA Modules:
  0.0 131.5 jit_solution(9192110002119126251)
XLA Ops:
  0.0 0.0 copy-start.2
  0.0 0.0 copy-start.3
  0.0 0.0 copy-start.5
  0.0 7.4 %shard_map.73 = bf16[768,512]{1,0:T(8,128)(2,1)} custom-call(bf16[1536,2048]{1,0:T(8,128)(2,1)} %bitcast.21, bf16[256,2048]{1,0:T(8,128)(2,1)} %constant.18.clone.table_ref.rest_0_), custom_call_target="tpu_custom_call" | custom-call | tf_op jit(solution)/shard_map/pallas_call | solution.py:152
  7.4 7.3 %all-to-all-start = ((bf16[32,24,512]{2,1,0:T(8,128)(2,1)}), bf16[32,24,512]{2,1,0:T(8,128)(2,1)S(1)}, u32[]{:S(2)}, u32[]{:S(2)}) async-start(bf16[32,24,512]{2,1,0:T(8,128)(2,1)} %bitcast.1), calls=%async_computation | async-start | bytes 1572864 | tf_op jit(solution)/shard_map/all_to_all | solution.py:294
  14.7 0.9 dynamic-slice_bitcast_fusion
  15.6 19.7 %all-to-all-done = bf16[32,24,512]{2,1,0:T(8,128)(2,1)S(1)} async-done(((bf16[32,24,512]{2,1,0:T(8,128)(2,1)}), bf16[32,24,512]{2,1,0:T(8,128)(2,1)S(1)}, u32[]{:S(2)}, u32[]{:S(2)}) %all-to-all-start) | async-done | bytes 786464 | tf_op jit(solution)/shard_map/all_to_all | solution.py:294
  35.4 0.0 copy-done.2
  35.4 0.0 copy-done.3
  35.4 2.7 %shard_map.74 = bf16[768,512]{1,0:T(8,128)(2,1)} custom-call(bf16[768,512]{1,0:T(8,128)(2,1)S(1)} %bitcast.18, bf16[4,64,128]{2,1,0:T(8,128)(2,1)S(1)} %get-tuple-element.10.weight_ref, bf16[256,768]{1,0:T(8,128)(2,1)S(1)} %copy-done.3, bf16[768,256]{1,0:T(8,128)(2,1)S(1)} %copy-done.2), custom_call_target="tpu_custom_call" | custom-call | tf_op jit(solution)/shard_map/pallas_call | solution.py:203
  38.0 3.8 %all-to-all-start.1 = ((bf16[32,24,512]{2,1,0:T(8,128)(2,1)}), bf16[32,24,512]{2,1,0:T(8,128)(2,1)S(1)}, u32[]{:S(2)}, u32[]{:S(2)}) async-start(bf16[32,24,512]{2,1,0:T(8,128)(2,1)} %bitcast.4), calls=%async_computation.1 | async-start | bytes 1572864 | tf_op jit(solution)/shard_map/all_to_all | solution.py:294
  41.8 0.0 copy-done.5
  41.9 0.1 copy.8
  42.0 0.3 multiply_bitcast_fusion
  42.2 0.9 fusion.1
  43.1 0.2 squeeze.13.weight_ref
  43.3 0.0 copy-start
  43.4 0.0 copy-start.1
  43.4 8.1 %shard_map.75.local_ref = bf16[1536,2048]{1,0:T(8,128)(2,1)} custom-call(bf16[1536,2048]{1,0:T(8,128)(2,1)} %bitcast.22, bf16[256,256]{1,0:T(8,128)(2,1)S(1)} %squeeze.13.weight_ref), custom_call_target="tpu_custom_call" | custom-call | tf_op jit(solution)/shard_map/pallas_call | solution.py:173
  51.5 10.8 %all-to-all-done.1 = bf16[32,24,512]{2,1,0:T(8,128)(2,1)S(1)} async-done(((bf16[32,24,512]{2,1,0:T(8,128)(2,1)}), bf16[32,24,512]{2,1,0:T(8,128)(2,1)S(1)}, u32[]{:S(2)}, u32[]{:S(2)}) %all-to-all-start.1) | async-done | bytes 786464 | tf_op jit(solution)/shard_map/all_to_all | solution.py:294
  62.3 0.0 copy-start.4
  62.3 0.0 copy-done
  62.3 0.0 copy-done.1
  62.3 9.8 %shard_map.76 = (bf16[1536,2048]{1,0:T(8,128)(2,1)}, bf16[768,512]{1,0:T(8,128)(2,1)S(1)}) custom-call(bf16[768,512]{1,0:T(8,128)(2,1)S(1)} %bitcast.17, bf16[1536,2048]{1,0:T(8,128)(2,1)} %shard_map.75.local_ref, bf16[256,2048]{1,0:T(8,128)(2,1)S(1)} %copy-done, bf16[256,2048]{1,0:T(8,128)(2,1)S(1)} %copy-done.1), custom_call_target="tpu_custom_call" | custom-call | tf_op jit(solution)/shard_map/pallas_call | solution.py:282
  72.1 24.0 %all_to_all.20 = bf16[32,24,512]{2,1,0:T(8,128)(2,1)S(1)} all-to-all(bf16[32,24,512]{2,1,0:T(8,128)(2,1)S(1)} %bitcast.20), channel_id=1, replica_groups=mesh['grp'=1,'lat'=32] {'lat'}, dimensions={0} | all-to-all | bytes 1572864 | tf_op jit(solution)/shard_map/all_to_all | solution.py:294
  96.1 0.0 copy-done.4
  96.1 2.6 %shard_map.77 = bf16[768,512]{1,0:T(8,128)(2,1)} custom-call(bf16[768,512]{1,0:T(8,128)(2,1)S(1)} %bitcast.19, bf16[4,64,128]{2,1,0:T(8,128)(2,1)S(1)} %get-tuple-element.9.weight_ref, bf16[256,768]{1,0:T(8,128)(2,1)S(1)} %copy-done.4, bf16[768,256]{1,0:T(8,128)(2,1)S(1)} %copy-done.2), custom_call_target="tpu_custom_call" | custom-call | tf_op jit(solution)/shard_map/pallas_call | solution.py:203
  98.8 3.8 %all-to-all-start.3 = ((bf16[32,24,512]{2,1,0:T(8,128)(2,1)}), bf16[32,24,512]{2,1,0:T(8,128)(2,1)S(1)}, u32[]{:S(2)}, u32[]{:S(2)}) async-start(bf16[32,24,512]{2,1,0:T(8,128)(2,1)} %bitcast.10), calls=%async_computation.3 | async-start | bytes 1572864 | tf_op jit(solution)/shard_map/all_to_all | solution.py:294
  102.6 1.2 squeeze.15.weight_ref
  103.8 8.0 %shard_map.78.local_ref = bf16[1536,2048]{1,0:T(8,128)(2,1)} custom-call(bf16[1536,2048]{1,0:T(8,128)(2,1)} %get-tuple-element.8.field_ref, bf16[256,256]{1,0:T(8,128)(2,1)S(1)} %squeeze.15.weight_ref), custom_call_target="tpu_custom_call" | custom-call | tf_op jit(solution)/shard_map/pallas_call | solution.py:173
  111.8 11.2 %all-to-all-done.3 = bf16[32,24,512]{2,1,0:T(8,128)(2,1)S(1)} async-done(((bf16[32,24,512]{2,1,0:T(8,128)(2,1)}), bf16[32,24,512]{2,1,0:T(8,128)(2,1)S(1)}, u32[]{:S(2)}, u32[]{:S(2)}) %all-to-all-start.3) | async-done | bytes 786464 | tf_op jit(solution)/shard_map/all_to_all | solution.py:294
  123.0 8.3 %shard_map.79 = bf16[1536,2048]{1,0:T(8,128)(2,1)} custom-call(bf16[768,512]{1,0:T(8,128)(2,1)S(1)} %bitcast.16, bf16[1536,2048]{1,0:T(8,128)(2,1)} %shard_map.78.local_ref, bf16[256,2048]{1,0:T(8,128)(2,1)S(1)} %copy-done), custom_call_target="tpu_custom_call" | custom-call | tf_op jit(solution)/shard_map/pallas_call | solution.py:282
  (1 shorter events, 0.0 us)
Async XLA Ops:
  0.0 35.4 %copy-start.2 = (bf16[768,256]{1,0:T(8,128)(2,1)S(1)}, bf16[768,256]{1,0:T(8,128)(2,1)}, u32[]{:S(2)}) copy-start(bf16[768,256]{1,0:T(8,128)(2,1)} %constant.20.clone.backward_ref) | copy-start | bytes 1179652
  0.0 35.4 %copy-start.3 = (bf16[256,768]{1,0:T(8,128)(2,1)S(1)}, bf16[256,768]{1,0:T(8,128)(2,1)}, u32[]{:S(2)}) copy-start(bf16[256,768]{1,0:T(8,128)(2,1)} %constant.19.clone.forward_ref) | copy-start | bytes 1179652
  0.0 41.8 %copy-start.5 = (bf16[2,64,64]{2,1,0:T(8,128)(2,1)S(1)}, bf16[2,64,64]{2,1,0:T(8,128)(2,1)}, u32[]{:S(2)}) copy-start(bf16[2,64,64]{2,1,0:T(8,128)(2,1)} %param.9) | copy-start | bytes 49156
  7.4 27.9 %all-to-all-start = ((bf16[32,24,512]{2,1,0:T(8,128)(2,1)}), bf16[32,24,512]{2,1,0:T(8,128)(2,1)S(1)}, u32[]{:S(2)}, u32[]{:S(2)}) async-start(bf16[32,24,512]{2,1,0:T(8,128)(2,1)} %bitcast.1), calls=%async_computation | async-start | bytes 1572864 | tf_op jit(solution)/shard_map/all_to_all | solution.py:294
  38.0 24.2 %all-to-all-start.1 = ((bf16[32,24,512]{2,1,0:T(8,128)(2,1)}), bf16[32,24,512]{2,1,0:T(8,128)(2,1)S(1)}, u32[]{:S(2)}, u32[]{:S(2)}) async-start(bf16[32,24,512]{2,1,0:T(8,128)(2,1)} %bitcast.4), calls=%async_computation.1 | async-start | bytes 1572864 | tf_op jit(solution)/shard_map/all_to_all | solution.py:294
  43.3 19.0 %copy-start = (bf16[256,2048]{1,0:T(8,128)(2,1)S(1)}, bf16[256,2048]{1,0:T(8,128)(2,1)}, u32[]{:S(2)}) copy-start(bf16[256,2048]{1,0:T(8,128)(2,1)} %constant.21.clone.back_ref) | copy-start | bytes 3145732
  43.4 18.9 %copy-start.1 = (bf16[256,2048]{1,0:T(8,128)(2,1)S(1)}, bf16[256,2048]{1,0:T(8,128)(2,1)}, u32[]{:S(2)}) copy-start(bf16[256,2048]{1,0:T(8,128)(2,1)} %constant.18.clone.table_ref.rest_0_) | copy-start | bytes 3145732
  62.3 33.9 %copy-start.4 = (bf16[256,768]{1,0:T(8,128)(2,1)S(1)}, bf16[256,768]{1,0:T(8,128)(2,1)}, u32[]{:S(2)}) copy-start(bf16[256,768]{1,0:T(8,128)(2,1)} %constant.19.clone.forward_ref) | copy-start | bytes 1179652
  98.8 24.2 %all-to-all-start.3 = ((bf16[32,24,512]{2,1,0:T(8,128)(2,1)}), bf16[32,24,512]{2,1,0:T(8,128)(2,1)S(1)}, u32[]{:S(2)}, u32[]{:S(2)}) async-start(bf16[32,24,512]{2,1,0:T(8,128)(2,1)} %bitcast.10), calls=%async_computation.3 | async-start | bytes 1572864 | tf_op jit(solution)/shard_map/all_to_all | solution.py:294

commit v3 on v2

--- a/solution.py
+++ b/solution.py
@@ -29,7 +29,7 @@
     cells = np.arange(lon_count, dtype=np.int64)[None, :]
     angle = 2.0 * np.pi / lon_count * (cells * modes % lon_count)
     both = np.concatenate([np.cos(angle), -np.sin(angle)], axis=0)
-    return (rounded(both / math.sqrt(lon_count)), rounded(both / math.sqrt(mode_count)))
+    return (rounded(both / math.sqrt(lon_count)), rounded(both / math.sqrt(mode_count) * 0.5))
 
 
 def lat_tables(lat_count, kept_count, block_rows):
@@ -130,20 +130,25 @@
     fields_ref, table_ref, modes_ref, copy_ref, table_copy, wide_ref, sems,
 ):
     steps, block = block_rows // rows, rows * channels
-    copies = [pltpu.make_async_copy(table_ref, table_copy, sems.at[steps])]
+    table_read = pltpu.make_async_copy(table_ref, table_copy, sems.at[steps])
+
+    def read(step):
+        part = pl.ds(step * block, block)
+        return pltpu.make_async_copy(fields_ref.at[part], copy_ref.at[part], sems.at[step])
+
+    table_read.start()
     for step in range(steps):
-        part = pl.ds(step * block, block)
-        copies.append(
-            pltpu.make_async_copy(fields_ref.at[part], copy_ref.at[part], sems.at[step])
-        )
-    for copy in copies:
-        copy.start()
-    copies[0].wait()
-    for step in range(steps):
-        copies[step + 1].wait()
-        part = slice(step * block, (step + 1) * block)
-        modes = dot(table_copy[...], copy_ref[part, :], ((1,), (1,)))
+        read(step).start()
+    table_read.wait()
+
+    def body(step, carry):
+        read(step).wait()
+        field = copy_ref[pl.ds(pl.multiple_of(step * block, block), block), :]
+        modes = dot(table_copy[...], field, ((1,), (1,)))
         scatter_modes(modes, wide_ref, step * rows, rows, block_rows, channels, devices)
+        return carry
+
+    lax.fori_loop(0, steps, body, 0)
     pack(wide_ref, modes_ref)
 
 
@@ -209,19 +214,20 @@
     )(in_vmem(values), in_vmem(weight), in_vmem(forward), in_vmem(backward))
 
 
-def gelu(x):
-    u = x * (math.sqrt(2.0 / math.pi) + (0.044715 * math.sqrt(2.0 / math.pi)) * (x * x))
-    half = 0.5 * x
-    return half * jnp.tanh(u) + half
-
-
-def spectral_block(modes, local_ref, back_ref, out_ref, first):
+def gelu_of_double(v):
+    scale = math.sqrt(2.0 / math.pi)
+    return v * jnp.tanh(v * (BF16(2.0 * scale) + BF16(8.0 * 0.044715 * scale) * (v * v))) + v
+
+
+def spectral_block(modes, back_ref, local_ref, out_ref, first):
     lon_count = back_ref.shape[1]
     chunk = min(256, lon_count)
+    rows = slice(first, first + modes.shape[0])
     for start in range(0, lon_count, chunk):
-        place = (slice(first, first + modes.shape[0]), slice(start, start + chunk))
-        total = dot(modes, back_ref[:, place[1]], ((1,), (0,))) + local_ref[place].astype(F32)
-        out_ref[place] = gelu(total).astype(BF16)
+        part = slice(start, start + chunk)
+        total = dot(modes, back_ref[:, part], ((1,), (0,))) + local_ref[rows, part].astype(F32)
+        local_ref[rows, part] = total.astype(BF16)
+    out_ref[rows, :] = gelu_of_double(local_ref[rows, :])
 
 
 def row_copies(source_ref, target_ref, sems, steps):
@@ -241,7 +247,7 @@
     else:
         field_out_ref = rest[0]
         rest = rest[1:]
-    local_copy, field_ref, wide_ref, in_sems, out_sems = rest
+    local_copy, field_ref, wide_ref, lhs_ref, in_sems, out_sems = rest
     steps, block = block_rows // rows, rows * channels
     arriving = row_copies(local_ref, local_copy, in_sems, steps)
     leaving = row_copies(field_ref, field_out_ref, out_sems, steps)
@@ -250,12 +256,14 @@
     unpack(modes_ref, wide_ref)
     for step in range(steps):
         modes = gather_modes(wide_ref, step * rows, rows, block_rows, channels, devices)
+        lhs_ref[step * block : (step + 1) * block, :] = modes.T.astype(BF16)
+    for step in range(steps):
+        part = slice(step * block, (step + 1) * block)
         arriving[step].wait()
-        spectral_block(modes.T.astype(BF16), local_copy, back_ref, field_ref, step * block)
+        spectral_block(lhs_ref[part, :], back_ref, local_copy, field_ref, step * block)
         leaving[step].start()
         if again:
-            field = field_ref[step * block : (step + 1) * block, :]
-            product = dot(table_ref[...], field, ((1,), (1,)))
+            product = dot(table_ref[...], field_ref[part, :], ((1,), (1,)))
             scatter_modes(product, wide_out_ref, step * rows, rows, block_rows, channels, devices)
     if again:
         pack(wide_out_ref, modes_out_ref)
@@ -270,6 +278,7 @@
         pltpu.VMEM(local.shape, BF16),
         pltpu.VMEM(local.shape, BF16),
         wide_scratch(modes.shape, channels),
+        pltpu.VMEM((local.shape[0], back.shape[0]), BF16),
         pltpu.SemaphoreType.DMA((steps,)),
         pltpu.SemaphoreType.DMA((steps,)),
     ]
@@ -306,12 +315,12 @@
         spectral_weight, lax.axis_index("lat") * per_device, per_device, 1
     )
     mixers = jnp.einsum(
-        "rs,lcd->lrdsc", jnp.eye(rows, dtype=BF16), local_weight
+        "rs,lcd->lrdsc", 0.5 * jnp.eye(rows, dtype=BF16), local_weight
     ).reshape(layer_count, rows * channels, rows * channels)
     wide_rows = 2 * rows if block_rows % (2 * rows) == 0 else rows
     sizes = (block_rows, channels, devices)
     field = fields.reshape(block_rows * channels, lon_count)
-    modes = first_transform(field, forward_lon, *sizes, rows)
+    modes = first_transform(field, forward_lon, *sizes, wide_rows)
     for layer in range(layer_count):
         arrived = exchange(modes, devices)
         rebuilt = middle(arrived, own[layer], forward_lat, backward_lat, channels)
@@ -322,7 +331,7 @@
                 returned, local, backward_lon, forward_lon, *sizes, wide_rows
             )
         else:
-            field = back_transform(returned, local, backward_lon, None, *sizes, rows)[0]
+            field = back_transform(returned, local, backward_lon, None, *sizes, wide_rows)[0]
     return field.reshape(fields.shape)
 
 

time: 132 us -> 128 us (0.970)
  Pallas kernels: 46.9 us -> 42.2 us
    pallas_call x2, Pallas kernels: 18 us -> 15.2 us  [back_transform(): pl.pallas_call(functools.partial(back_kernel, block_rows, channels, devic...]
    pallas_call x1, Pallas kernels: 7.41 us -> 5.64 us  [first_transform(): pl.pallas_call(functools.partial(first_kernel, block_rows, channels, devi...]
  transfers between devices with their start and end apart: 3 -> 3, of which waited for: 3 -> 3; matrix products, arithmetic and copies ran while one was open for 3% -> 3% of each run, Pallas kernels for 12% -> 13%
where the time goes in v3:
time: 128 us; the launch traced here: 127 us
  Pallas kernels  42.2 us (33%)
  waiting for transfers between devices  42 us (33%)
  blocking collectives  24.1 us (19%)
  starting transfers between devices  14.7 us (11%)
  local copies, waits for them, and re-layouts  3.29 us (3%)
    all_to_all x3, waiting for transfers between devices, exchange(): return lax.all_to_all(parts, 'lat', 0, 0, tiled=True).reshape(array.shape)  42 us
    all_to_all x1, blocking collectives, exchange(): return lax.all_to_all(parts, 'lat', 0, 0, tiled=True).reshape(array.shape)  24.1 us
    pallas_call x2, Pallas kernels, local_mix(): pl.pallas_call(local_kernel, grid=(field.shape[0] // weight.shape[0],), i...  16.1 us
    pallas_call x2, Pallas kernels, back_transform(): pl.pallas_call(functools.partial(back_kernel, block_rows, channels, devic...  15.2 us
    all_to_all x3, starting transfers between devices, exchange(): return lax.all_to_all(parts, 'lat', 0, 0, tiled=True).reshape(array.shape)  14.7 us
    pallas_call x1, Pallas kernels, first_transform(): pl.pallas_call(functools.partial(first_kernel, block_rows, channels, devi...  5.64 us
    pallas_call x2, Pallas kernels, middle(): pl.pallas_call(functools.partial(middle_kernel, channels), in_specs=[RESI...  5.32 us
  transfers between devices with their start and end apart: 3, of which 3 were waited for; matrix products, arithmetic and copies ran while one was open for 3% of the time, Pallas kernels for 13%

profile of v3, /device:TPU:0, one launch (start us, length us, event | category | flops | bytes accessed | tf_op | source)
XLA Modules:
  0.0 126.8 jit_solution(4566221659283516914)
XLA Ops:
  0.0 0.0 copy-start.2
  0.0 0.0 copy-start.3
  0.0 0.0 copy-start.5
  0.0 5.6 %shard_map.73 = bf16[768,512]{1,0:T(8,128)(2,1)} custom-call(bf16[1536,2048]{1,0:T(8,128)(2,1)} %bitcast.21, bf16[256,2048]{1,0:T(8,128)(2,1)} %constant.22.clone.table_ref.rest_0_), custom_call_target="tpu_custom_call" | custom-call | tf_op jit(solution)/shard_map/pallas_call | solution.py:157
  5.7 7.3 %all-to-all-start = ((bf16[32,24,512]{2,1,0:T(8,128)(2,1)}), bf16[32,24,512]{2,1,0:T(8,128)(2,1)S(1)}, u32[]{:S(2)}, u32[]{:S(2)}) async-start(bf16[32,24,512]{2,1,0:T(8,128)(2,1)} %bitcast.1), calls=%async_computation | async-start | bytes 1572864 | tf_op jit(solution)/shard_map/all_to_all | solution.py:303
  13.0 0.9 dynamic-slice_bitcast_fusion
  13.9 19.7 %all-to-all-done = bf16[32,24,512]{2,1,0:T(8,128)(2,1)S(1)} async-done(((bf16[32,24,512]{2,1,0:T(8,128)(2,1)}), bf16[32,24,512]{2,1,0:T(8,128)(2,1)S(1)}, u32[]{:S(2)}, u32[]{:S(2)}) %all-to-all-start) | async-done | bytes 786464 | tf_op jit(solution)/shard_map/all_to_all | solution.py:303
  33.6 0.0 copy-done.2
  33.6 0.0 copy-done.3
  33.6 2.7 %shard_map.74 = bf16[768,512]{1,0:T(8,128)(2,1)} custom-call(bf16[768,512]{1,0:T(8,128)(2,1)S(1)} %bitcast.18, bf16[4,64,128]{2,1,0:T(8,128)(2,1)S(1)} %get-tuple-element.10.weight_ref, bf16[256,768]{1,0:T(8,128)(2,1)S(1)} %copy-done.3, bf16[768,256]{1,0:T(8,128)(2,1)S(1)} %copy-done.2), custom_call_target="tpu_custom_call" | custom-call | tf_op jit(solution)/shard_map/pallas_call | solution.py:208
  36.3 3.6 %all-to-all-start.1 = ((bf16[32,24,512]{2,1,0:T(8,128)(2,1)}), bf16[32,24,512]{2,1,0:T(8,128)(2,1)S(1)}, u32[]{:S(2)}, u32[]{:S(2)}) async-start(bf16[32,24,512]{2,1,0:T(8,128)(2,1)} %bitcast.4), calls=%async_computation.1 | async-start | bytes 1572864 | tf_op jit(solution)/shard_map/all_to_all | solution.py:303
  39.9 0.0 copy-done.5
  39.9 0.1 copy.8
  40.0 0.3 multiply_bitcast_fusion
  40.3 0.9 fusion.1
  41.2 0.2 squeeze.13.weight_ref
  41.4 0.0 copy-start
  41.4 0.0 copy-start.1
  41.4 8.1 %shard_map.75.local_ref = bf16[1536,2048]{1,0:T(8,128)(2,1)} custom-call(bf16[1536,2048]{1,0:T(8,128)(2,1)} %bitcast.22, bf16[256,256]{1,0:T(8,128)(2,1)S(1)} %squeeze.13.weight_ref), custom_call_target="tpu_custom_call" | custom-call | tf_op jit(solution)/shard_map/pallas_call | solution.py:178
  49.5 11.0 %all-to-all-done.1 = bf16[32,24,512]{2,1,0:T(8,128)(2,1)S(1)} async-done(((bf16[32,24,512]{2,1,0:T(8,128)(2,1)}), bf16[32,24,512]{2,1,0:T(8,128)(2,1)S(1)}, u32[]{:S(2)}, u32[]{:S(2)}) %all-to-all-start.1) | async-done | bytes 786464 | tf_op jit(solution)/shard_map/all_to_all | solution.py:303
  60.5 0.0 copy-start.4
  60.5 0.0 copy-done
  60.5 0.0 copy-done.1
  60.5 8.6 %shard_map.76 = (bf16[1536,2048]{1,0:T(8,128)(2,1)}, bf16[768,512]{1,0:T(8,128)(2,1)S(1)}) custom-call(bf16[768,512]{1,0:T(8,128)(2,1)S(1)} %bitcast.17, bf16[1536,2048]{1,0:T(8,128)(2,1)} %shard_map.75.local_ref, bf16[256,2048]{1,0:T(8,128)(2,1)S(1)} %copy-done, bf16[256,2048]{1,0:T(8,128)(2,1)S(1)} %copy-done.1), custom_call_target="tpu_custom_call" | custom-call | tf_op jit(solution)/shard_map/pallas_call | solution.py:291
  69.1 24.1 %all_to_all.20 = bf16[32,24,512]{2,1,0:T(8,128)(2,1)S(1)} all-to-all(bf16[32,24,512]{2,1,0:T(8,128)(2,1)S(1)} %bitcast.20), channel_id=1, replica_groups=mesh['grp'=1,'lat'=32] {'lat'}, dimensions={0} | all-to-all | bytes 1572864 | tf_op jit(solution)/shard_map/all_to_all | solution.py:303
  93.2 0.0 copy-done.4
  93.2 2.6 %shard_map.77 = bf16[768,512]{1,0:T(8,128)(2,1)} custom-call(bf16[768,512]{1,0:T(8,128)(2,1)S(1)} %bitcast.19, bf16[4,64,128]{2,1,0:T(8,128)(2,1)S(1)} %get-tuple-element.9.weight_ref, bf16[256,768]{1,0:T(8,128)(2,1)S(1)} %copy-done.4, bf16[768,256]{1,0:T(8,128)(2,1)S(1)} %copy-done.2), custom_call_target="tpu_custom_call" | custom-call | tf_op jit(solution)/shard_map/pallas_call | solution.py:208
  95.8 3.8 %all-to-all-start.3 = ((bf16[32,24,512]{2,1,0:T(8,128)(2,1)}), bf16[32,24,512]{2,1,0:T(8,128)(2,1)S(1)}, u32[]{:S(2)}, u32[]{:S(2)}) async-start(bf16[32,24,512]{2,1,0:T(8,128)(2,1)} %bitcast.10), calls=%async_computation.3 | async-start | bytes 1572864 | tf_op jit(solution)/shard_map/all_to_all | solution.py:303
  99.6 1.2 squeeze.15.weight_ref
  100.8 8.0 %shard_map.78.local_ref = bf16[1536,2048]{1,0:T(8,128)(2,1)} custom-call(bf16[1536,2048]{1,0:T(8,128)(2,1)} %get-tuple-element.8.field_ref, bf16[256,256]{1,0:T(8,128)(2,1)S(1)} %squeeze.15.weight_ref), custom_call_target="tpu_custom_call" | custom-call | tf_op jit(solution)/shard_map/pallas_call | solution.py:178
  108.8 11.3 %all-to-all-done.3 = bf16[32,24,512]{2,1,0:T(8,128)(2,1)S(1)} async-done(((bf16[32,24,512]{2,1,0:T(8,128)(2,1)}), bf16[32,24,512]{2,1,0:T(8,128)(2,1)S(1)}, u32[]{:S(2)}, u32[]{:S(2)}) %all-to-all-start.3) | async-done | bytes 786464 | tf_op jit(solution)/shard_map/all_to_all | solution.py:303
  120.1 6.6 %shard_map.79 = bf16[1536,2048]{1,0:T(8,128)(2,1)} custom-call(bf16[768,512]{1,0:T(8,128)(2,1)S(1)} %bitcast.16, bf16[1536,2048]{1,0:T(8,128)(2,1)} %shard_map.78.local_ref, bf16[256,2048]{1,0:T(8,128)(2,1)S(1)} %copy-done), custom_call_target="tpu_custom_call" | custom-call | tf_op jit(solution)/shard_map/pallas_call | solution.py:291
  (1 shorter events, 0.0 us)
Async XLA Ops:
  0.0 33.6 %copy-start.2 = (bf16[768,256]{1,0:T(8,128)(2,1)S(1)}, bf16[768,256]{1,0:T(8,128)(2,1)}, u32[]{:S(2)}) copy-start(bf16[768,256]{1,0:T(8,128)(2,1)} %constant.24.clone.backward_ref) | copy-start | bytes 1179652
  0.0 33.6 %copy-start.3 = (bf16[256,768]{1,0:T(8,128)(2,1)S(1)}, bf16[256,768]{1,0:T(8,128)(2,1)}, u32[]{:S(2)}) copy-start(bf16[256,768]{1,0:T(8,128)(2,1)} %constant.23.clone.forward_ref) | copy-start | bytes 1179652
  0.0 39.9 %copy-start.5 = (bf16[2,64,64]{2,1,0:T(8,128)(2,1)S(1)}, bf16[2,64,64]{2,1,0:T(8,128)(2,1)}, u32[]{:S(2)}) copy-start(bf16[2,64,64]{2,1,0:T(8,128)(2,1)} %param.9) | copy-start | bytes 49156
  5.7 27.9 %all-to-all-start = ((bf16[32,24,512]{2,1,0:T(8,128)(2,1)}), bf16[32,24,512]{2,1,0:T(8,128)(2,1)S(1)}, u32[]{:S(2)}, u32[]{:S(2)}) async-start(bf16[32,24,512]{2,1,0:T(8,128)(2,1)} %bitcast.1), calls=%async_computation | async-start | bytes 1572864 | tf_op jit(solution)/shard_map/all_to_all | solution.py:303
  36.3 24.2 %all-to-all-start.1 = ((bf16[32,24,512]{2,1,0:T(8,128)(2,1)}), bf16[32,24,512]{2,1,0:T(8,128)(2,1)S(1)}, u32[]{:S(2)}, u32[]{:S(2)}) async-start(bf16[32,24,512]{2,1,0:T(8,128)(2,1)} %bitcast.4), calls=%async_computation.1 | async-start | bytes 1572864 | tf_op jit(solution)/shard_map/all_to_all | solution.py:303
  41.4 19.1 %copy-start = (bf16[256,2048]{1,0:T(8,128)(2,1)S(1)}, bf16[256,2048]{1,0:T(8,128)(2,1)}, u32[]{:S(2)}) copy-start(bf16[256,2048]{1,0:T(8,128)(2,1)} %constant.25.clone.back_ref) | copy-start | bytes 3145732
  41.4 19.1 %copy-start.1 = (bf16[256,2048]{1,0:T(8,128)(2,1)S(1)}, bf16[256,2048]{1,0:T(8,128)(2,1)}, u32[]{:S(2)}) copy-start(bf16[256,2048]{1,0:T(8,128)(2,1)} %constant.22.clone.table_ref.rest_0_) | copy-start | bytes 3145732
  60.5 32.6 %copy-start.4 = (bf16[256,768]{1,0:T(8,128)(2,1)S(1)}, bf16[256,768]{1,0:T(8,128)(2,1)}, u32[]{:S(2)}) copy-start(bf16[256,768]{1,0:T(8,128)(2,1)} %constant.23.clone.forward_ref) | copy-start | bytes 1179652
  95.8 24.2 %all-to-all-start.3 = ((bf16[32,24,512]{2,1,0:T(8,128)(2,1)}), bf16[32,24,512]{2,1,0:T(8,128)(2,1)S(1)}, u32[]{:S(2)}, u32[]{:S(2)}) async-start(bf16[32,24,512]{2,1,0:T(8,128)(2,1)} %bitcast.10), calls=%async_computation.3 | async-start | bytes 1572864 | tf_op jit(solution)/shard_map/all_to_all | solution.py:303

commit v4 on v3

--- a/solution.py
+++ b/solution.py
@@ -185,13 +185,20 @@
     )(in_hbm(field), weight)
 
 
-def middle_kernel(channels, values_ref, weight_ref, forward_ref, backward_ref, out_ref):
+def middle_kernel(
+    channels, layer, values_ref, weights_ref, forward_ref, backward_ref, out_ref, weight_ref, sem
+):
     kept = forward_ref.shape[0] // 2
     lanes = 2 * channels
+    per_device = weight_ref.shape[0]
+    own = pl.ds(lax.axis_index("lat") * per_device, per_device)
+    read = pltpu.make_async_copy(weights_ref.at[layer, own], weight_ref, sem)
+    read.start()
     products = dot(forward_ref[...], values_ref[...], ((1,), (0,)))
     low = low_half((kept, lanes), channels)
     low_w = low_half((channels, lanes), channels)
-    for k in range(values_ref.shape[1] // lanes):
+    read.wait()
+    for k in range(per_device):
         part = slice(k * lanes, (k + 1) * lanes)
         turned = pltpu.roll(products[kept:, part], channels, 1)
         modes = (products[:kept, part] + jnp.where(low, turned, -turned)).astype(BF16)
@@ -204,14 +211,19 @@
         out_ref[:, part] = dot(backward_ref[...], both, ((1,), (0,))).astype(BF16)
 
 
-def middle(values, weight, forward, backward, channels):
+def middle(values, weights, layer, forward, backward, channels):
+    per_device = values.shape[1] // (2 * channels)
     return pl.pallas_call(
-        functools.partial(middle_kernel, channels),
-        in_specs=[RESIDENT] * 4,
+        functools.partial(middle_kernel, channels, layer),
+        in_specs=[RESIDENT, OUTSIDE, RESIDENT, RESIDENT],
         out_specs=RESIDENT,
         out_shape=pltpu.VMEM(values.shape, BF16),
+        scratch_shapes=[
+            pltpu.VMEM((per_device,) + weights.shape[2:], BF16),
+            pltpu.SemaphoreType.DMA(()),
+        ],
         compiler_params=params(24),
-    )(in_vmem(values), in_vmem(weight), in_vmem(forward), in_vmem(backward))
+    )(in_vmem(values), in_hbm(weights), in_vmem(forward), in_vmem(backward))
 
 
 def gelu_of_double(v):
@@ -239,18 +251,19 @@
     ]
 
 
-def back_kernel(block_rows, channels, devices, rows, again, modes_ref, local_ref, back_ref, *rest):
-    if again:
-        table_ref, field_out_ref, modes_out_ref = rest[:3]
-        wide_out_ref = rest[-1]
-        rest = rest[3:-1]
+def back_kernel(
+    block_rows, channels, devices, rows, kind, modes_ref, local_ref, back_ref, *rest
+):
+    if kind == "field":
+        out_ref, *rest = rest
     else:
-        field_out_ref = rest[0]
-        rest = rest[1:]
-    local_copy, field_ref, wide_ref, lhs_ref, in_sems, out_sems = rest
+        extra_ref, out_ref, *rest = rest
+    local_copy, field_ref, wide_ref, lhs_ref, in_sems, out_sems, *rest = rest
     steps, block = block_rows // rows, rows * channels
     arriving = row_copies(local_ref, local_copy, in_sems, steps)
-    leaving = row_copies(field_ref, field_out_ref, out_sems, steps)
+    leaving = []
+    if kind != "modes":
+        leaving = row_copies(field_ref, out_ref, out_sems, steps)
     for copy in arriving:
         copy.start()
     unpack(modes_ref, wide_ref)
@@ -261,18 +274,24 @@
         part = slice(step * block, (step + 1) * block)
         arriving[step].wait()
         spectral_block(lhs_ref[part, :], back_ref, local_copy, field_ref, step * block)
-        leaving[step].start()
-        if again:
-            product = dot(table_ref[...], field_ref[part, :], ((1,), (1,)))
-            scatter_modes(product, wide_out_ref, step * rows, rows, block_rows, channels, devices)
-    if again:
-        pack(wide_out_ref, modes_out_ref)
+        if kind == "modes":
+            product = dot(extra_ref[...], field_ref[part, :], ((1,), (1,)))
+            scatter_modes(product, rest[0], step * rows, rows, block_rows, channels, devices)
+        if kind == "mix":
+            unit = extra_ref.shape[0]
+            for start in range(step * block, (step + 1) * block, unit):
+                piece = slice(start, start + unit)
+                mixed = dot(extra_ref[...], field_ref[piece, :], ((1,), (0,)))
+                field_ref[piece, :] = mixed.astype(BF16)
+        if leaving:
+            leaving[step].start()
+    if kind == "modes":
+        pack(rest[0], out_ref)
     for copy in leaving:
         copy.wait()
 
 
-def back_transform(modes, local, back, table, block_rows, channels, devices, rows):
-    again = table is not None
+def back_transform(kind, modes, local, back, extra, block_rows, channels, devices, rows):
     steps = block_rows // rows
     scratch = [
         pltpu.VMEM(local.shape, BF16),
@@ -283,16 +302,17 @@
         pltpu.SemaphoreType.DMA((steps,)),
     ]
     args = [in_vmem(modes), in_hbm(local), in_vmem(back)]
-    out_shape = [pltpu.HBM(local.shape, BF16)]
-    if again:
-        args.append(in_vmem(table))
-        out_shape.append(pltpu.VMEM(modes.shape, BF16))
+    if kind != "field":
+        args.append(in_vmem(extra))
+    if kind == "modes":
         scratch.append(wide_scratch(modes.shape, channels))
     return pl.pallas_call(
-        functools.partial(back_kernel, block_rows, channels, devices, rows, again),
+        functools.partial(back_kernel, block_rows, channels, devices, rows, kind),
         in_specs=[RESIDENT, OUTSIDE] + [RESIDENT] * (len(args) - 2),
-        out_specs=[OUTSIDE] + [RESIDENT] * (len(out_shape) - 1),
-        out_shape=out_shape,
+        out_specs=RESIDENT if kind == "modes" else OUTSIDE,
+        out_shape=pltpu.VMEM(modes.shape, BF16)
+        if kind == "modes"
+        else pltpu.HBM(local.shape, BF16),
         scratch_shapes=scratch,
         compiler_params=params(32),
     )(*args)
@@ -308,30 +328,26 @@
     layer_count, mode_count = spectral_weight.shape[:2]
     devices = lax.axis_size("lat")
     rows = max(2, 256 // channels)
-    per_device = mode_count // devices
     forward_lon, backward_lon = lon_tables(lon_count, mode_count, devices)
     forward_lat, backward_lat = lat_tables(block_rows * devices, KY, block_rows)
-    own = lax.dynamic_slice_in_dim(
-        spectral_weight, lax.axis_index("lat") * per_device, per_device, 1
-    )
     mixers = jnp.einsum(
         "rs,lcd->lrdsc", 0.5 * jnp.eye(rows, dtype=BF16), local_weight
     ).reshape(layer_count, rows * channels, rows * channels)
     wide_rows = 2 * rows if block_rows % (2 * rows) == 0 else rows
-    sizes = (block_rows, channels, devices)
+    sizes = dict(block_rows=block_rows, channels=channels, devices=devices, rows=wide_rows)
     field = fields.reshape(block_rows * channels, lon_count)
-    modes = first_transform(field, forward_lon, *sizes, wide_rows)
+    modes = first_transform(field, forward_lon, **sizes)
+    local = local_mix(field, mixers[0])
     for layer in range(layer_count):
         arrived = exchange(modes, devices)
-        rebuilt = middle(arrived, own[layer], forward_lat, backward_lat, channels)
+        rebuilt = middle(arrived, spectral_weight, layer, forward_lat, backward_lat, channels)
         returned = exchange(rebuilt, devices)
-        local = local_mix(field, mixers[layer])
+        end = functools.partial(back_transform, modes=returned, local=local, back=backward_lon)
         if layer < layer_count - 1:
-            field, modes = back_transform(
-                returned, local, backward_lon, forward_lon, *sizes, wide_rows
-            )
+            modes = end("modes", extra=forward_lon, **sizes)
+            local = end("mix", extra=mixers[layer + 1], **sizes)
         else:
-            field = back_transform(returned, local, backward_lon, None, *sizes, wide_rows)[0]
+            field = end("field", extra=None, **sizes)
     return field.reshape(fields.shape)
 
 

time: 128 us -> 126 us (0.984)
  blocking collectives: 24.1 us -> 51.8 us
  waiting for transfers between devices: 42 us -> 23 us
  starting transfers between devices: 14.7 us -> 7.43 us
  local copies, waits for them, and re-layouts: 3.29 us -> 1.44 us
  Pallas kernels: 42.2 us -> 40.9 us
    all_to_all x1 -> x2, blocking collectives: 24.1 us -> 51.8 us  [exchange(): return lax.all_to_all(parts, 'lat', 0, 0, tiled=True).reshape(array.shape)]
    all_to_all x3 -> x2, waiting for transfers between devices: 42 us -> 23 us  [exchange(): return lax.all_to_all(parts, 'lat', 0, 0, tiled=True).reshape(array.shape)]
    pallas_call x2 -> x1, Pallas kernels: 16.1 us -> 8.1 us  [local_mix(): pl.pallas_call(local_kernel, grid=(field.shape[0] // weight.shape[0],), i...]
    all_to_all x3 -> x2, starting transfers between devices: 14.7 us -> 7.43 us  [exchange(): return lax.all_to_all(parts, 'lat', 0, 0, tiled=True).reshape(array.shape)]
    pallas_call x2 -> x3, Pallas kernels: 15.2 us -> 21.4 us  [back_transform(): pl.pallas_call(functools.partial(back_kernel, block_rows, channels, devic...]
    squeeze x3 -> x2, local copies, waits for them, and re-layouts: 2.28 us -> 0.42 us  [the longest x1 0.21 us: shards(): local = end('mix', extra=mixers[layer + 1], **sizes)]
    pallas_call x2, Pallas kernels: 5.32 us -> 6.65 us  [middle(): pl.pallas_call(functools.partial(middle_kernel, channels, layer), in_spec...]
  transfers between devices with their start and end apart: 3 -> 2, of which waited for: 3 -> 2; matrix products, arithmetic and copies ran while one was open for 3% -> 1% of each run, Pallas kernels for 13% -> 13%
where the time goes in v4:
time: 126 us; the launch traced here: 125 us
  blocking collectives  51.8 us (41%)
  Pallas kernels  40.9 us (32%)
  waiting for transfers between devices  23 us (18%)
  starting transfers between devices  7.43 us (6%)
  local copies, waits for them, and re-layouts  1.44 us (1%)
    all_to_all x2, blocking collectives, exchange(): return lax.all_to_all(parts, 'lat', 0, 0, tiled=True).reshape(array.shape)  51.8 us
    all_to_all x2, waiting for transfers between devices, exchange(): return lax.all_to_all(parts, 'lat', 0, 0, tiled=True).reshape(array.shape)  23 us
    pallas_call x3, Pallas kernels, back_transform(): pl.pallas_call(functools.partial(back_kernel, block_rows, channels, devic...  21.4 us
    pallas_call x1, Pallas kernels, local_mix(): pl.pallas_call(local_kernel, grid=(field.shape[0] // weight.shape[0],), i...  8.1 us
    all_to_all x2, starting transfers between devices, exchange(): return lax.all_to_all(parts, 'lat', 0, 0, tiled=True).reshape(array.shape)  7.43 us
    pallas_call x2, Pallas kernels, middle(): pl.pallas_call(functools.partial(middle_kernel, channels, layer), in_spec...  6.65 us
    pallas_call x1, Pallas kernels, first_transform(): pl.pallas_call(functools.partial(first_kernel, block_rows, channels, devi...  4.76 us
  transfers between devices with their start and end apart: 2, of which 2 were waited for; matrix products, arithmetic and copies ran while one was open for 1% of the time, Pallas kernels for 13%

profile of v4, /device:TPU:0, one launch (start us, length us, event | category | flops | bytes accessed | tf_op | source)
XLA Modules:
  0.0 125.1 jit_solution(17520065995167371118)
XLA Ops:
  0.0 0.0 copy-start.2
  0.0 0.0 copy-start.3
  0.0 4.8 %shard_map.73 = bf16[768,512]{1,0:T(8,128)(2,1)S(1)} custom-call(bf16[1536,2048]{1,0:T(8,128)(2,1)} %bitcast.19, bf16[256,2048]{1,0:T(8,128)(2,1)} %constant.12.clone.table_ref.rest_0_), custom_call_target="tpu_custom_call" | custom-call | tf_op jit(solution)/shard_map/pallas_call | solution.py:157
  4.8 0.0 copy-start.6
  4.8 27.7 %all_to_all.20 = bf16[32,24,512]{2,1,0:T(8,128)(2,1)S(1)} all-to-all(bf16[32,24,512]{2,1,0:T(8,128)(2,1)S(1)} %bitcast.18), channel_id=1, replica_groups=mesh['grp'=1,'lat'=32] {'lat'}, dimensions={0} | all-to-all | bytes 1572864 | tf_op jit(solution)/shard_map/all_to_all | solution.py:323
  32.5 0.0 copy-done.2
  32.5 0.0 copy-done.3
  32.5 3.3 %shard_map.74 = bf16[768,512]{1,0:T(8,128)(2,1)} custom-call(bf16[768,512]{1,0:T(8,128)(2,1)S(1)} %bitcast.16, bf16[2,128,64,128]{3,2,1,0:T(8,128)(2,1)} %weights_ref.3, bf16[256,768]{1,0:T(8,128)(2,1)S(1)} %copy-done.2, bf16[768,256]{1,0:T(8,128)(2,1)S(1)} %copy-done.3), custom_call_target="tpu_custom_call" | custom-call | tf_op jit(solution)/shard_map/pallas_call | solution.py:216
  35.8 3.6 %all-to-all-start.1 = ((bf16[32,24,512]{2,1,0:T(8,128)(2,1)}), bf16[32,24,512]{2,1,0:T(8,128)(2,1)S(1)}, u32[]{:S(2)}, u32[]{:S(2)}) async-start(bf16[32,24,512]{2,1,0:T(8,128)(2,1)} %bitcast.3), calls=%async_computation.1 | async-start | bytes 1572864 | tf_op jit(solution)/shard_map/all_to_all | solution.py:323
  39.5 0.0 copy-done.6
  39.5 0.1 copy.8
  39.6 0.3 multiply_bitcast_fusion
  39.9 0.9 fusion.1
  40.8 0.2 squeeze.6.weight_ref
  41.0 0.0 copy-start
  41.0 0.0 copy-start.1
  41.0 8.1 %shard_map.75.local_ref = bf16[1536,2048]{1,0:T(8,128)(2,1)} custom-call(bf16[1536,2048]{1,0:T(8,128)(2,1)} %bitcast.20, bf16[256,256]{1,0:T(8,128)(2,1)S(1)} %squeeze.6.weight_ref), custom_call_target="tpu_custom_call" | custom-call | tf_op jit(solution)/shard_map/pallas_call | solution.py:178
  49.1 11.0 %all-to-all-done.1 = bf16[32,24,512]{2,1,0:T(8,128)(2,1)S(1)} async-done(((bf16[32,24,512]{2,1,0:T(8,128)(2,1)}), bf16[32,24,512]{2,1,0:T(8,128)(2,1)S(1)}, u32[]{:S(2)}, u32[]{:S(2)}) %all-to-all-start.1) | async-done | bytes 786464 | tf_op jit(solution)/shard_map/all_to_all | solution.py:323
  60.1 0.0 copy-start.4
  60.1 0.0 copy-done
  60.1 0.0 copy-done.1
  60.1 6.6 %shard_map.76 = bf16[768,512]{1,0:T(8,128)(2,1)S(1)} custom-call(bf16[768,512]{1,0:T(8,128)(2,1)S(1)} %bitcast.12, bf16[1536,2048]{1,0:T(8,128)(2,1)} %shard_map.75.local_ref, bf16[256,2048]{1,0:T(8,128)(2,1)S(1)} %copy-done, bf16[256,2048]{1,0:T(8,128)(2,1)S(1)} %copy-done.1), custom_call_target="tpu_custom_call" | custom-call | tf_op jit(solution)/shard_map/pallas_call | solution.py:309
  66.7 0.0 copy-start.5
  66.7 24.0 %all_to_all.21 = bf16[32,24,512]{2,1,0:T(8,128)(2,1)S(1)} all-to-all(bf16[32,24,512]{2,1,0:T(8,128)(2,1)S(1)} %bitcast.17), channel_id=1, replica_groups=mesh['grp'=1,'lat'=32] {'lat'}, dimensions={0} | all-to-all | bytes 1572864 | tf_op jit(solution)/shard_map/all_to_all | solution.py:323
  90.8 0.0 copy-done.4
  90.8 3.3 %shard_map.77 = bf16[768,512]{1,0:T(8,128)(2,1)} custom-call(bf16[768,512]{1,0:T(8,128)(2,1)S(1)} %bitcast.15, bf16[2,128,64,128]{3,2,1,0:T(8,128)(2,1)} %weights_ref.3, bf16[256,768]{1,0:T(8,128)(2,1)S(1)} %copy-done.2, bf16[768,256]{1,0:T(8,128)(2,1)S(1)} %copy-done.4), custom_call_target="tpu_custom_call" | custom-call | tf_op jit(solution)/shard_map/pallas_call | solution.py:216
  94.1 3.8 %all-to-all-start.3 = ((bf16[32,24,512]{2,1,0:T(8,128)(2,1)}), bf16[32,24,512]{2,1,0:T(8,128)(2,1)S(1)}, u32[]{:S(2)}, u32[]{:S(2)}) async-start(bf16[32,24,512]{2,1,0:T(8,128)(2,1)} %bitcast.8), calls=%async_computation.3 | async-start | bytes 1572864 | tf_op jit(solution)/shard_map/all_to_all | solution.py:323
  97.9 0.0 copy-done.5
  97.9 0.2 squeeze.7.rest_0_
  98.2 8.2 %shard_map.78.local_ref = bf16[1536,2048]{1,0:T(8,128)(2,1)} custom-call(bf16[768,512]{1,0:T(8,128)(2,1)S(1)} %bitcast.13, bf16[1536,2048]{1,0:T(8,128)(2,1)} %shard_map.75.local_ref, bf16[256,2048]{1,0:T(8,128)(2,1)S(1)} %copy-done, bf16[256,256]{1,0:T(8,128)(2,1)S(1)} %squeeze.7.rest_0_), custom_call_target="tpu_custom_call" | custom-call | tf_op jit(solution)/shard_map/pallas_call | solution.py:309
  106.4 12.0 %all-to-all-done.3 = bf16[32,24,512]{2,1,0:T(8,128)(2,1)S(1)} async-done(((bf16[32,24,512]{2,1,0:T(8,128)(2,1)}), bf16[32,24,512]{2,1,0:T(8,128)(2,1)S(1)}, u32[]{:S(2)}, u32[]{:S(2)}) %all-to-all-start.3) | async-done | bytes 786464 | tf_op jit(solution)/shard_map/all_to_all | solution.py:323
  118.4 6.6 %shard_map.79 = bf16[1536,2048]{1,0:T(8,128)(2,1)} custom-call(bf16[768,512]{1,0:T(8,128)(2,1)S(1)} %bitcast.14, bf16[1536,2048]{1,0:T(8,128)(2,1)} %shard_map.78.local_ref, bf16[256,2048]{1,0:T(8,128)(2,1)S(1)} %copy-done), custom_call_target="tpu_custom_call" | custom-call | tf_op jit(solution)/shard_map/pallas_call | solution.py:309
  (1 shorter events, 0.0 us)
Async XLA Ops:
  0.0 32.5 %copy-start.2 = (bf16[256,768]{1,0:T(8,128)(2,1)S(1)}, bf16[256,768]{1,0:T(8,128)(2,1)}, u32[]{:S(2)}) copy-start(bf16[256,768]{1,0:T(8,128)(2,1)} %constant.13.clone.forward_ref) | copy-start | bytes 1179652
  0.0 32.5 %copy-start.3 = (bf16[768,256]{1,0:T(8,128)(2,1)S(1)}, bf16[768,256]{1,0:T(8,128)(2,1)}, u32[]{:S(2)}) copy-start(bf16[768,256]{1,0:T(8,128)(2,1)} %constant.14.clone.backward_ref) | copy-start | bytes 1179652
  4.8 34.7 %copy-start.6 = (bf16[2,64,64]{2,1,0:T(8,128)(2,1)S(1)}, bf16[2,64,64]{2,1,0:T(8,128)(2,1)}, u32[]{:S(2)}) copy-start(bf16[2,64,64]{2,1,0:T(8,128)(2,1)} %param.9) | copy-start | bytes 49156
  35.8 24.3 %all-to-all-start.1 = ((bf16[32,24,512]{2,1,0:T(8,128)(2,1)}), bf16[32,24,512]{2,1,0:T(8,128)(2,1)S(1)}, u32[]{:S(2)}, u32[]{:S(2)}) async-start(bf16[32,24,512]{2,1,0:T(8,128)(2,1)} %bitcast.3), calls=%async_computation.1 | async-start | bytes 1572864 | tf_op jit(solution)/shard_map/all_to_all | solution.py:323
  41.0 19.1 %copy-start = (bf16[256,2048]{1,0:T(8,128)(2,1)S(1)}, bf16[256,2048]{1,0:T(8,128)(2,1)}, u32[]{:S(2)}) copy-start(bf16[256,2048]{1,0:T(8,128)(2,1)} %constant.15.clone.back_ref) | copy-start | bytes 3145732
  41.0 19.1 %copy-start.1 = (bf16[256,2048]{1,0:T(8,128)(2,1)S(1)}, bf16[256,2048]{1,0:T(8,128)(2,1)}, u32[]{:S(2)}) copy-start(bf16[256,2048]{1,0:T(8,128)(2,1)} %constant.12.clone.table_ref.rest_0_) | copy-start | bytes 3145732
  60.1 30.7 %copy-start.4 = (bf16[768,256]{1,0:T(8,128)(2,1)S(1)}, bf16[768,256]{1,0:T(8,128)(2,1)}, u32[]{:S(2)}) copy-start(bf16[768,256]{1,0:T(8,128)(2,1)} %constant.14.clone.backward_ref) | copy-start | bytes 1179652
  66.7 31.2 %copy-start.5 = (bf16[1,4,64,4,64]{4,3,2,1,0:T(4,128)(2,1)S(1)}, bf16[1,4,64,4,64]{4,3,2,1,0:T(4,128)(2,1)}, u32[]{:S(2)}) copy-start(bf16[1,4,64,4,64]{4,3,2,1,0:T(4,128)(2,1)} %get-tuple-element.5) | copy-start | bytes 393220
  94.1 24.3 %all-to-all-start.3 = ((bf16[32,24,512]{2,1,0:T(8,128)(2,1)}), bf16[32,24,512]{2,1,0:T(8,128)(2,1)S(1)}, u32[]{:S(2)}, u32[]{:S(2)}) async-start(bf16[32,24,512]{2,1,0:T(8,128)(2,1)} %bitcast.8), calls=%async_computation.3 | async-start | bytes 1572864 | tf_op jit(solution)/shard_map/all_to_all | solution.py:323

commit v5 on v4

--- a/solution.py
+++ b/solution.py
@@ -127,10 +127,13 @@
 
 def first_kernel(
     block_rows, channels, devices, rows,
-    fields_ref, table_ref, modes_ref, copy_ref, table_copy, wide_ref, sems,
+    fields_ref, table_ref, weights_ref, modes_ref, own_ref, copy_ref, table_copy, wide_ref, sems,
 ):
     steps, block = block_rows // rows, rows * channels
     table_read = pltpu.make_async_copy(table_ref, table_copy, sems.at[steps])
+    per_device = own_ref.shape[1]
+    own = pl.ds(lax.axis_index("lat") * per_device, per_device)
+    own_read = pltpu.make_async_copy(weights_ref.at[:, own], own_ref, sems.at[steps + 1])
 
     def read(step):
         part = pl.ds(step * block, block)
@@ -139,6 +142,7 @@
     table_read.start()
     for step in range(steps):
         read(step).start()
+    own_read.start()
     table_read.wait()
 
     def body(step, carry):
@@ -149,24 +153,27 @@
         return carry
 
     lax.fori_loop(0, steps, body, 0)
+    own_read.wait()
     pack(wide_ref, modes_ref)
 
 
-def first_transform(fields, table, block_rows, channels, devices, rows):
+def first_transform(fields, table, weights, block_rows, channels, devices, rows):
+    per_device = weights.shape[1] // devices
+    own_shape = (weights.shape[0], per_device) + weights.shape[2:]
     modes_shape = (devices * block_rows, table.shape[0] // devices * channels)
     return pl.pallas_call(
         functools.partial(first_kernel, block_rows, channels, devices, rows),
-        in_specs=[OUTSIDE, OUTSIDE],
-        out_specs=RESIDENT,
-        out_shape=pltpu.VMEM(modes_shape, BF16),
+        in_specs=[OUTSIDE, OUTSIDE, OUTSIDE],
+        out_specs=[RESIDENT, RESIDENT],
+        out_shape=[pltpu.VMEM(modes_shape, BF16), pltpu.VMEM(own_shape, BF16)],
         scratch_shapes=[
             pltpu.VMEM(fields.shape, BF16),
             pltpu.VMEM(table.shape, BF16),
             wide_scratch(modes_shape, channels),
-            pltpu.SemaphoreType.DMA((block_rows // rows + 1,)),
+            pltpu.SemaphoreType.DMA((block_rows // rows + 2,)),
         ],
         compiler_params=params(24),
-    )(in_hbm(fields), in_hbm(table))
+    )(in_hbm(fields), in_hbm(table), in_hbm(weights))
 
 
 def local_kernel(field_ref, weight_ref, out_ref):
@@ -186,69 +193,51 @@
 
 
 def middle_kernel(
-    channels, layer, values_ref, weights_ref, forward_ref, backward_ref, out_ref, weight_ref, sem
+    channels, layer, values_ref, weights_ref, forward_ref, backward_ref, out_ref, copy_ref, sems
 ):
     kept = forward_ref.shape[0] // 2
     lanes = 2 * channels
-    per_device = weight_ref.shape[0]
-    own = pl.ds(lax.axis_index("lat") * per_device, per_device)
-    read = pltpu.make_async_copy(weights_ref.at[layer, own], weight_ref, sem)
-    read.start()
+    per_device = weights_ref.shape[1]
     products = dot(forward_ref[...], values_ref[...], ((1,), (0,)))
     low = low_half((kept, lanes), channels)
     low_w = low_half((channels, lanes), channels)
-    read.wait()
+    writes = []
     for k in range(per_device):
         part = slice(k * lanes, (k + 1) * lanes)
         turned = pltpu.roll(products[kept:, part], channels, 1)
         modes = (products[:kept, part] + jnp.where(low, turned, -turned)).astype(BF16)
-        weight = weight_ref[k].astype(F32)
+        weight = weights_ref[layer, k].astype(F32)
         swapped = pltpu.roll(weight, channels, 1)
         mixing = jnp.concatenate([weight, jnp.where(low_w, -swapped, swapped)], axis=0)
         mixed = dot(modes, mixing.astype(BF16), ((1,), (0,)))
         swapped = pltpu.roll(mixed, channels, 1)
         both = jnp.concatenate([mixed, jnp.where(low, -swapped, swapped)], axis=0).astype(BF16)
-        out_ref[:, part] = dot(backward_ref[...], both, ((1,), (0,))).astype(BF16)
+        copy_ref[k] = dot(backward_ref[...], both, ((1,), (0,))).astype(BF16)
+        target = out_ref.at[:, pl.ds(k * lanes, lanes)]
+        writes.append(pltpu.make_async_copy(copy_ref.at[k], target, sems.at[k]))
+        writes[-1].start()
+    for write in writes:
+        write.wait()
 
 
 def middle(values, weights, layer, forward, backward, channels):
-    per_device = values.shape[1] // (2 * channels)
+    per_device = weights.shape[1]
     return pl.pallas_call(
         functools.partial(middle_kernel, channels, layer),
-        in_specs=[RESIDENT, OUTSIDE, RESIDENT, RESIDENT],
-        out_specs=RESIDENT,
-        out_shape=pltpu.VMEM(values.shape, BF16),
+        in_specs=[RESIDENT] * 4,
+        out_specs=OUTSIDE,
+        out_shape=pltpu.HBM(values.shape, BF16),
         scratch_shapes=[
-            pltpu.VMEM((per_device,) + weights.shape[2:], BF16),
-            pltpu.SemaphoreType.DMA(()),
+            pltpu.VMEM((per_device, values.shape[0], 2 * channels), BF16),
+            pltpu.SemaphoreType.DMA((per_device,)),
         ],
         compiler_params=params(24),
-    )(in_vmem(values), in_hbm(weights), in_vmem(forward), in_vmem(backward))
+    )(in_vmem(values), in_vmem(weights), in_vmem(forward), in_vmem(backward))
 
 
 def gelu_of_double(v):
     scale = math.sqrt(2.0 / math.pi)
     return v * jnp.tanh(v * (BF16(2.0 * scale) + BF16(8.0 * 0.044715 * scale) * (v * v))) + v
-
-
-def spectral_block(modes, back_ref, local_ref, out_ref, first):
-    lon_count = back_ref.shape[1]
-    chunk = min(256, lon_count)
-    rows = slice(first, first + modes.shape[0])
-    for start in range(0, lon_count, chunk):
-        part = slice(start, start + chunk)
-        total = dot(modes, back_ref[:, part], ((1,), (0,))) + local_ref[rows, part].astype(F32)
-        local_ref[rows, part] = total.astype(BF16)
-    out_ref[rows, :] = gelu_of_double(local_ref[rows, :])
-
-
-def row_copies(source_ref, target_ref, sems, steps):
-    block = source_ref.shape[0] // steps
-    parts = [pl.ds(step * block, block) for step in range(steps)]
-    return [
-        pltpu.make_async_copy(source_ref.at[part], target_ref.at[part], sems.at[step])
-        for step, part in enumerate(parts)
-    ]
 
 
 def back_kernel(
@@ -260,35 +249,61 @@
         extra_ref, out_ref, *rest = rest
     local_copy, field_ref, wide_ref, lhs_ref, in_sems, out_sems, *rest = rest
     steps, block = block_rows // rows, rows * channels
-    arriving = row_copies(local_ref, local_copy, in_sems, steps)
-    leaving = []
-    if kind != "modes":
-        leaving = row_copies(field_ref, out_ref, out_sems, steps)
-    for copy in arriving:
-        copy.start()
+    lon_count = back_ref.shape[1]
+    chunk = min(256, lon_count)
+
+    def arriving(step):
+        part = pl.ds(step * block, block)
+        return pltpu.make_async_copy(local_ref.at[part], local_copy.at[part], in_sems.at[step])
+
+    def leaving(step):
+        part = pl.ds(step * block, block)
+        return pltpu.make_async_copy(field_ref.at[part], out_ref.at[part], out_sems.at[step])
+
+    for step in range(steps):
+        arriving(step).start()
     unpack(modes_ref, wide_ref)
-    for step in range(steps):
-        modes = gather_modes(wide_ref, step * rows, rows, block_rows, channels, devices)
-        lhs_ref[step * block : (step + 1) * block, :] = modes.T.astype(BF16)
-    for step in range(steps):
-        part = slice(step * block, (step + 1) * block)
-        arriving[step].wait()
-        spectral_block(lhs_ref[part, :], back_ref, local_copy, field_ref, step * block)
+    few = math.gcd(rows, max(2, 256 // channels))
+
+    def relayout(step, carry):
+        modes = gather_modes(wide_ref, step * few, few, block_rows, channels, devices)
+        size = few * channels
+        lhs_ref[pl.ds(pl.multiple_of(step * size, size), size), :] = modes.T.astype(BF16)
+        return carry
+
+    lax.fori_loop(0, block_rows // few, relayout, 0)
+
+    def body(step, carry):
+        first = step * block if isinstance(step, int) else pl.multiple_of(step * block, block)
+        part = pl.ds(first, block)
+        arriving(step).wait()
+        for start in range(0, lon_count, chunk):
+            lons = slice(start, start + chunk)
+            total = dot(lhs_ref[part, :], back_ref[:, lons], ((1,), (0,))).astype(BF16)
+            field_ref[part, lons] = gelu_of_double(total + local_copy[part, lons])
         if kind == "modes":
             product = dot(extra_ref[...], field_ref[part, :], ((1,), (1,)))
             scatter_modes(product, rest[0], step * rows, rows, block_rows, channels, devices)
         if kind == "mix":
             unit = extra_ref.shape[0]
-            for start in range(step * block, (step + 1) * block, unit):
-                piece = slice(start, start + unit)
+            for start in range(0, block, unit):
+                piece = pl.ds(first + start, unit)
                 mixed = dot(extra_ref[...], field_ref[piece, :], ((1,), (0,)))
                 field_ref[piece, :] = mixed.astype(BF16)
-        if leaving:
-            leaving[step].start()
+        if kind != "modes":
+            leaving(step).start()
+        return carry
+
+    if kind == "field":
+        lax.fori_loop(0, steps, body, 0)
+    else:
+        for step in range(steps):
+            body(step, 0)
     if kind == "modes":
         pack(rest[0], out_ref)
-    for copy in leaving:
-        copy.wait()
+    else:
+        for step in range(steps):
+            leaving(step).wait()
 
 
 def back_transform(kind, modes, local, back, extra, block_rows, channels, devices, rows):
@@ -336,18 +351,18 @@
     wide_rows = 2 * rows if block_rows % (2 * rows) == 0 else rows
     sizes = dict(block_rows=block_rows, channels=channels, devices=devices, rows=wide_rows)
     field = fields.reshape(block_rows * channels, lon_count)
-    modes = first_transform(field, forward_lon, **sizes)
+    modes, weights = first_transform(field, forward_lon, spectral_weight, **sizes)
     local = local_mix(field, mixers[0])
     for layer in range(layer_count):
         arrived = exchange(modes, devices)
-        rebuilt = middle(arrived, spectral_weight, layer, forward_lat, backward_lat, channels)
+        rebuilt = middle(arrived, weights, layer, forward_lat, backward_lat, channels)
         returned = exchange(rebuilt, devices)
         end = functools.partial(back_transform, modes=returned, local=local, back=backward_lon)
         if layer < layer_count - 1:
             modes = end("modes", extra=forward_lon, **sizes)
             local = end("mix", extra=mixers[layer + 1], **sizes)
         else:
-            field = end("field", extra=None, **sizes)
+            field = end("field", extra=None, **{**sizes, "rows": rows})
     return field.reshape(fields.shape)
 
 

time: 126 us -> 123 us (0.976)
  Pallas kernels: 40.9 us -> 37.9 us
    pallas_call x2, Pallas kernels: 6.65 us -> 4.98 us  [middle(): pl.pallas_call(functools.partial(middle_kernel, channels, layer), in_spec...]
    pallas_call x3, Pallas kernels: 21.4 us -> 20 us  [back_transform(): pl.pallas_call(functools.partial(back_kernel, block_rows, channels, devic...]
  transfers between devices with their start and end apart: 2 -> 2, of which waited for: 2 -> 2; matrix products, arithmetic and copies ran while one was open for 1% -> 2% of each run, Pallas kernels for 13% -> 13%
where the time goes in v5:
time: 123 us
  blocking collectives  51.8 us (42%)
  Pallas kernels  37.9 us (31%)
  waiting for transfers between devices  22.6 us (18%)
  starting transfers between devices  7.43 us (6%)
  local copies, waits for them, and re-layouts  2.4 us (2%)
    all_to_all x2, blocking collectives, exchange(): return lax.all_to_all(parts, 'lat', 0, 0, tiled=True).reshape(array.shape)  51.8 us
    all_to_all x2, waiting for transfers between devices, exchange(): return lax.all_to_all(parts, 'lat', 0, 0, tiled=True).reshape(array.shape)  22.6 us
    pallas_call x3, Pallas kernels, back_transform(): pl.pallas_call(functools.partial(back_kernel, block_rows, channels, devic...  20 us
    pallas_call x1, Pallas kernels, local_mix(): pl.pallas_call(local_kernel, grid=(field.shape[0] // weight.shape[0],), i...  8.1 us
    all_to_all x2, starting transfers between devices, exchange(): return lax.all_to_all(parts, 'lat', 0, 0, tiled=True).reshape(array.shape)  7.43 us
    pallas_call x2, Pallas kernels, middle(): pl.pallas_call(functools.partial(middle_kernel, channels, layer), in_spec...  4.98 us
    pallas_call x1, Pallas kernels, first_transform(): pl.pallas_call(functools.partial(first_kernel, block_rows, channels, devi...  4.77 us
  transfers between devices with their start and end apart: 2, of which 2 were waited for; matrix products, arithmetic and copies ran while one was open for 2% of the time, Pallas kernels for 13%

profile of v5, /device:TPU:0, one launch (start us, length us, event | category | flops | bytes accessed | tf_op | source)
XLA Modules:
  0.0 122.6 jit_solution(15173237838092144920)
XLA Ops:
  0.0 0.0 copy-start.2
  0.0 0.0 copy-start.3
  0.0 0.0 copy-start.5
  0.0 4.8 %shard_map.73 = (bf16[768,512]{1,0:T(8,128)(2,1)S(1)}, bf16[2,4,64,128]{3,2,1,0:T(8,128)(2,1)S(1)}) custom-call(bf16[1536,2048]{1,0:T(8,128)(2,1)} %bitcast.19, bf16[256,2048]{1,0:T(8,128)(2,1)} %constant.12.clone.table_ref.rest_0_, bf16[2,128,64,128]{3,2,1,0:T(8,128)(2,1)} %weights_ref.1), custom_call_target="tpu_custom_call" | custom-call | tf_op jit(solution)/shard_map/pallas_call | solution.py:164
  4.8 27.7 %all_to_all.20 = bf16[32,24,512]{2,1,0:T(8,128)(2,1)S(1)} all-to-all(bf16[32,24,512]{2,1,0:T(8,128)(2,1)S(1)} %bitcast.18), channel_id=1, replica_groups=mesh['grp'=1,'lat'=32] {'lat'}, dimensions={0} | all-to-all | bytes 1572864 | tf_op jit(solution)/shard_map/all_to_all | solution.py:338
  32.5 0.0 copy-done.2
  32.5 0.0 copy-done.3
  32.5 2.5 %shard_map.74 = bf16[768,512]{1,0:T(8,128)(2,1)} custom-call(bf16[768,512]{1,0:T(8,128)(2,1)S(1)} %bitcast.16, bf16[2,4,64,128]{3,2,1,0:T(8,128)(2,1)S(1)} %get-tuple-element.8.weights_ref, bf16[256,768]{1,0:T(8,128)(2,1)S(1)} %copy-done.2, bf16[768,256]{1,0:T(8,128)(2,1)S(1)} %copy-done.3), custom_call_target="tpu_custom_call" | custom-call | tf_op jit(solution)/shard_map/pallas_call | solution.py:225
  35.0 3.6 %all-to-all-start.1 = ((bf16[32,24,512]{2,1,0:T(8,128)(2,1)}), bf16[32,24,512]{2,1,0:T(8,128)(2,1)S(1)}, u32[]{:S(2)}, u32[]{:S(2)}) async-start(bf16[32,24,512]{2,1,0:T(8,128)(2,1)} %bitcast.21), calls=%async_computation.1 | async-start | bytes 1572864 | tf_op jit(solution)/shard_map/all_to_all | solution.py:338
  38.7 0.0 copy-done.5
  38.7 0.1 copy.8
  38.8 0.3 multiply_bitcast_fusion
  39.0 0.9 fusion.1
  39.9 0.2 squeeze.6.weight_ref
  40.1 0.0 copy-start
  40.2 0.0 copy-start.1
  40.2 8.1 %shard_map.75.local_ref = bf16[1536,2048]{1,0:T(8,128)(2,1)} custom-call(bf16[1536,2048]{1,0:T(8,128)(2,1)} %bitcast.20, bf16[256,256]{1,0:T(8,128)(2,1)S(1)} %squeeze.6.weight_ref), custom_call_target="tpu_custom_call" | custom-call | tf_op jit(solution)/shard_map/pallas_call | solution.py:185
  48.3 11.0 %all-to-all-done.1 = bf16[32,24,512]{2,1,0:T(8,128)(2,1)S(1)} async-done(((bf16[32,24,512]{2,1,0:T(8,128)(2,1)}), bf16[32,24,512]{2,1,0:T(8,128)(2,1)S(1)}, u32[]{:S(2)}, u32[]{:S(2)}) %all-to-all-start.1) | async-done | bytes 786464 | tf_op jit(solution)/shard_map/all_to_all | solution.py:338
  59.3 0.0 copy-start.4
  59.3 0.0 copy-done
  59.3 0.0 copy-done.1
  59.3 6.3 %shard_map.76 = bf16[768,512]{1,0:T(8,128)(2,1)S(1)} custom-call(bf16[768,512]{1,0:T(8,128)(2,1)S(1)} %bitcast.12, bf16[1536,2048]{1,0:T(8,128)(2,1)} %shard_map.75.local_ref, bf16[256,2048]{1,0:T(8,128)(2,1)S(1)} %copy-done, bf16[256,2048]{1,0:T(8,128)(2,1)S(1)} %copy-done.1), custom_call_target="tpu_custom_call" | custom-call | tf_op jit(solution)/shard_map/pallas_call | solution.py:324
  65.6 24.0 %all_to_all.21 = bf16[32,24,512]{2,1,0:T(8,128)(2,1)S(1)} all-to-all(bf16[32,24,512]{2,1,0:T(8,128)(2,1)S(1)} %bitcast.17), channel_id=1, replica_groups=mesh['grp'=1,'lat'=32] {'lat'}, dimensions={0} | all-to-all | bytes 1572864 | tf_op jit(solution)/shard_map/all_to_all | solution.py:338
  89.6 0.0 copy-done.4
  89.7 2.5 %shard_map.77 = bf16[768,512]{1,0:T(8,128)(2,1)} custom-call(bf16[768,512]{1,0:T(8,128)(2,1)S(1)} %bitcast.15, bf16[2,4,64,128]{3,2,1,0:T(8,128)(2,1)S(1)} %get-tuple-element.8.weights_ref, bf16[256,768]{1,0:T(8,128)(2,1)S(1)} %copy-done.2, bf16[768,256]{1,0:T(8,128)(2,1)S(1)} %copy-done.4), custom_call_target="tpu_custom_call" | custom-call | tf_op jit(solution)/shard_map/pallas_call | solution.py:225
  92.2 3.8 %all-to-all-start.3 = ((bf16[32,24,512]{2,1,0:T(8,128)(2,1)}), bf16[32,24,512]{2,1,0:T(8,128)(2,1)S(1)}, u32[]{:S(2)}, u32[]{:S(2)}) async-start(bf16[32,24,512]{2,1,0:T(8,128)(2,1)} %bitcast.22), calls=%async_computation.3 | async-start | bytes 1572864 | tf_op jit(solution)/shard_map/all_to_all | solution.py:338
  96.0 1.2 squeeze.7.rest_0_
  97.2 7.7 %shard_map.78.local_ref = bf16[1536,2048]{1,0:T(8,128)(2,1)} custom-call(bf16[768,512]{1,0:T(8,128)(2,1)S(1)} %bitcast.13, bf16[1536,2048]{1,0:T(8,128)(2,1)} %shard_map.75.local_ref, bf16[256,2048]{1,0:T(8,128)(2,1)S(1)} %copy-done, bf16[256,256]{1,0:T(8,128)(2,1)S(1)} %squeeze.7.rest_0_), custom_call_target="tpu_custom_call" | custom-call | tf_op jit(solution)/shard_map/pallas_call | solution.py:324
  104.8 11.6 %all-to-all-done.3 = bf16[32,24,512]{2,1,0:T(8,128)(2,1)S(1)} async-done(((bf16[32,24,512]{2,1,0:T(8,128)(2,1)}), bf16[32,24,512]{2,1,0:T(8,128)(2,1)S(1)}, u32[]{:S(2)}, u32[]{:S(2)}) %all-to-all-start.3) | async-done | bytes 786464 | tf_op jit(solution)/shard_map/all_to_all | solution.py:338
  116.4 6.0 %shard_map.79 = bf16[1536,2048]{1,0:T(8,128)(2,1)} custom-call(bf16[768,512]{1,0:T(8,128)(2,1)S(1)} %bitcast.14, bf16[1536,2048]{1,0:T(8,128)(2,1)} %shard_map.78.local_ref, bf16[256,2048]{1,0:T(8,128)(2,1)S(1)} %copy-done), custom_call_target="tpu_custom_call" | custom-call | tf_op jit(solution)/shard_map/pallas_call | solution.py:324
  (1 shorter events, 0.0 us)
Async XLA Ops:
  0.0 32.5 %copy-start.2 = (bf16[256,768]{1,0:T(8,128)(2,1)S(1)}, bf16[256,768]{1,0:T(8,128)(2,1)}, u32[]{:S(2)}) copy-start(bf16[256,768]{1,0:T(8,128)(2,1)} %constant.13.clone.forward_ref) | copy-start | bytes 1179652
  0.0 32.5 %copy-start.3 = (bf16[768,256]{1,0:T(8,128)(2,1)S(1)}, bf16[768,256]{1,0:T(8,128)(2,1)}, u32[]{:S(2)}) copy-start(bf16[768,256]{1,0:T(8,128)(2,1)} %constant.14.clone.backward_ref) | copy-start | bytes 1179652
  0.0 38.6 %copy-start.5 = (bf16[2,64,64]{2,1,0:T(8,128)(2,1)S(1)}, bf16[2,64,64]{2,1,0:T(8,128)(2,1)}, u32[]{:S(2)}) copy-start(bf16[2,64,64]{2,1,0:T(8,128)(2,1)} %param.9) | copy-start | bytes 49156
  35.0 24.3 %all-to-all-start.1 = ((bf16[32,24,512]{2,1,0:T(8,128)(2,1)}), bf16[32,24,512]{2,1,0:T(8,128)(2,1)S(1)}, u32[]{:S(2)}, u32[]{:S(2)}) async-start(bf16[32,24,512]{2,1,0:T(8,128)(2,1)} %bitcast.21), calls=%async_computation.1 | async-start | bytes 1572864 | tf_op jit(solution)/shard_map/all_to_all | solution.py:338
  40.1 19.1 %copy-start = (bf16[256,2048]{1,0:T(8,128)(2,1)S(1)}, bf16[256,2048]{1,0:T(8,128)(2,1)}, u32[]{:S(2)}) copy-start(bf16[256,2048]{1,0:T(8,128)(2,1)} %constant.15.clone.back_ref) | copy-start | bytes 3145732
  40.2 19.1 %copy-start.1 = (bf16[256,2048]{1,0:T(8,128)(2,1)S(1)}, bf16[256,2048]{1,0:T(8,128)(2,1)}, u32[]{:S(2)}) copy-start(bf16[256,2048]{1,0:T(8,128)(2,1)} %constant.12.clone.table_ref.rest_0_) | copy-start | bytes 3145732
  59.3 30.4 %copy-start.4 = (bf16[768,256]{1,0:T(8,128)(2,1)S(1)}, bf16[768,256]{1,0:T(8,128)(2,1)}, u32[]{:S(2)}) copy-start(bf16[768,256]{1,0:T(8,128)(2,1)} %constant.14.clone.backward_ref) | copy-start | bytes 1179652
  92.2 24.3 %all-to-all-start.3 = ((bf16[32,24,512]{2,1,0:T(8,128)(2,1)}), bf16[32,24,512]{2,1,0:T(8,128)(2,1)S(1)}, u32[]{:S(2)}, u32[]{:S(2)}) async-start(bf16[32,24,512]{2,1,0:T(8,128)(2,1)} %bitcast.22), calls=%async_computation.3 | async-start | bytes 1572864 | tf_op jit(solution)/shard_map/all_to_all | solution.py:338

commit v6 on v5

--- a/solution.py
+++ b/solution.py
@@ -132,7 +132,7 @@
     steps, block = block_rows // rows, rows * channels
     table_read = pltpu.make_async_copy(table_ref, table_copy, sems.at[steps])
     per_device = own_ref.shape[1]
-    own = pl.ds(lax.axis_index("lat") * per_device, per_device)
+    own = pl.ds(lax.rem(lax.axis_index("lat"), devices) * per_device, per_device)
     own_read = pltpu.make_async_copy(weights_ref.at[:, own], own_ref, sems.at[steps + 1])
 
     def read(step):
@@ -192,47 +192,78 @@
     )(in_hbm(field), weight)
 
 
+def partial_kernel(channels, first, values_ref, forward_ref, out_ref):
+    kept = forward_ref.shape[1] // 2
+    lanes = 2 * channels
+    half = lax.axis_index("lat") * forward_ref.shape[0] // lax.axis_size("lat")
+    columns = slice(first * lanes, first * lanes + out_ref.shape[1])
+    products = dot(forward_ref[half], values_ref[:, columns], ((1,), (0,)))
+    low = low_half((kept, lanes), channels)
+    for start in range(0, out_ref.shape[1], lanes):
+        part = slice(start, start + lanes)
+        turned = pltpu.roll(products[kept:, part], channels, 1)
+        sums = products[:kept, part] + jnp.where(low, turned, -turned)
+        out_ref[:, part] = sums.astype(BF16)
+
+
+def partial_sums(values, forward, first, count, channels):
+    shape = (forward.shape[1] // 2, count * 2 * channels)
+    return pl.pallas_call(
+        functools.partial(partial_kernel, channels, first),
+        in_specs=[RESIDENT] * 2,
+        out_specs=RESIDENT,
+        out_shape=jax.ShapeDtypeStruct(shape, BF16),
+        compiler_params=params(24),
+    )(in_vmem(values), in_vmem(forward))
+
+
 def middle_kernel(
-    channels, layer, values_ref, weights_ref, forward_ref, backward_ref, out_ref, copy_ref, sems
+    channels, layer, first, own_ref, other_ref, weights_ref, backward_ref, *rest
 ):
-    kept = forward_ref.shape[0] // 2
+    out_ref, copy_ref, sems = rest[-3:]
+    kept = own_ref.shape[0]
     lanes = 2 * channels
-    per_device = weights_ref.shape[1]
-    products = dot(forward_ref[...], values_ref[...], ((1,), (0,)))
+    half = lax.axis_index("lat") * backward_ref.shape[0] // lax.axis_size("lat")
     low = low_half((kept, lanes), channels)
     low_w = low_half((channels, lanes), channels)
     writes = []
-    for k in range(per_device):
+    for k in range(own_ref.shape[1] // lanes):
         part = slice(k * lanes, (k + 1) * lanes)
-        turned = pltpu.roll(products[kept:, part], channels, 1)
-        modes = (products[:kept, part] + jnp.where(low, turned, -turned)).astype(BF16)
-        weight = weights_ref[layer, k].astype(F32)
+        modes = (own_ref[:, part].astype(F32) + other_ref[:, part].astype(F32)).astype(BF16)
+        weight = weights_ref[layer, first + k].astype(F32)
         swapped = pltpu.roll(weight, channels, 1)
         mixing = jnp.concatenate([weight, jnp.where(low_w, -swapped, swapped)], axis=0)
         mixed = dot(modes, mixing.astype(BF16), ((1,), (0,)))
         swapped = pltpu.roll(mixed, channels, 1)
         both = jnp.concatenate([mixed, jnp.where(low, -swapped, swapped)], axis=0).astype(BF16)
-        copy_ref[k] = dot(backward_ref[...], both, ((1,), (0,))).astype(BF16)
-        target = out_ref.at[:, pl.ds(k * lanes, lanes)]
+        copy_ref[k] = dot(backward_ref[half], both, ((1,), (0,))).astype(BF16)
+        target = out_ref.at[:, pl.ds((first + k) * lanes, lanes)]
         writes.append(pltpu.make_async_copy(copy_ref.at[k], target, sems.at[k]))
         writes[-1].start()
     for write in writes:
         write.wait()
 
 
-def middle(values, weights, layer, forward, backward, channels):
-    per_device = weights.shape[1]
+def middle(own, other, weights, layer, first, backward, so_far, channels):
+    count = own.shape[1] // (2 * channels)
+    rows = backward.shape[1]
+    args = [in_vmem(own), in_vmem(other), in_vmem(weights), in_vmem(backward)]
+    specs = [RESIDENT] * 4
+    if so_far is not None:
+        args.append(in_hbm(so_far))
+        specs.append(OUTSIDE)
     return pl.pallas_call(
-        functools.partial(middle_kernel, channels, layer),
-        in_specs=[RESIDENT] * 4,
+        functools.partial(middle_kernel, channels, layer, first),
+        in_specs=specs,
         out_specs=OUTSIDE,
-        out_shape=pltpu.HBM(values.shape, BF16),
+        out_shape=pltpu.HBM((rows, weights.shape[1] * 2 * channels), BF16),
         scratch_shapes=[
-            pltpu.VMEM((per_device, values.shape[0], 2 * channels), BF16),
-            pltpu.SemaphoreType.DMA((per_device,)),
+            pltpu.VMEM((count, rows, 2 * channels), BF16),
+            pltpu.SemaphoreType.DMA((count,)),
         ],
+        input_output_aliases={} if so_far is None else {4: 0},
         compiler_params=params(24),
-    )(in_vmem(values), in_vmem(weights), in_vmem(forward), in_vmem(backward))
+    )(*args)
 
 
 def gelu_of_double(v):
@@ -333,9 +364,11 @@
     )(*args)
 
 
-def exchange(array, devices):
-    parts = array.reshape(devices, array.shape[0] // devices, array.shape[1])
-    return lax.all_to_all(parts, "lat", 0, 0, tiled=True).reshape(array.shape)
+def exchange(array, peers, devices):
+    parts = array.reshape(peers, array.shape[0] // peers, array.shape[1])
+    groups = [list(range(start, start + peers)) for start in range(0, devices, peers)]
+    moved = lax.all_to_all(parts, "lat", 0, 0, tiled=True, axis_index_groups=groups)
+    return moved.reshape(array.shape)
 
 
 def shards(fields, spectral_weight, local_weight):
@@ -343,20 +376,32 @@
     layer_count, mode_count = spectral_weight.shape[:2]
     devices = lax.axis_size("lat")
     rows = max(2, 256 // channels)
-    forward_lon, backward_lon = lon_tables(lon_count, mode_count, devices)
+    peers = devices // 2
+    per_device = mode_count // peers
+    counts = [per_device - per_device // 2, per_device // 2]
+    swap = [(source, (source + peers) % devices) for source in range(devices)]
+    forward_lon, backward_lon = lon_tables(lon_count, mode_count, peers)
     forward_lat, backward_lat = lat_tables(block_rows * devices, KY, block_rows)
+    forward_lat = np.stack(np.split(forward_lat, 2, axis=1))
+    backward_lat = np.stack(np.split(backward_lat, 2, axis=0))
     mixers = jnp.einsum(
         "rs,lcd->lrdsc", 0.5 * jnp.eye(rows, dtype=BF16), local_weight
     ).reshape(layer_count, rows * channels, rows * channels)
     wide_rows = 2 * rows if block_rows % (2 * rows) == 0 else rows
-    sizes = dict(block_rows=block_rows, channels=channels, devices=devices, rows=wide_rows)
+    sizes = dict(block_rows=block_rows, channels=channels, devices=peers, rows=wide_rows)
     field = fields.reshape(block_rows * channels, lon_count)
     modes, weights = first_transform(field, forward_lon, spectral_weight, **sizes)
     local = local_mix(field, mixers[0])
     for layer in range(layer_count):
-        arrived = exchange(modes, devices)
-        rebuilt = middle(arrived, weights, layer, forward_lat, backward_lat, channels)
-        returned = exchange(rebuilt, devices)
+        arrived = exchange(modes, peers, devices)
+        sums = []
+        for first, count in zip((0, counts[0]), counts, strict=True):
+            own = partial_sums(arrived, forward_lat, first, count, channels)
+            sums.append((first, own, lax.ppermute(own, "lat", swap)))
+        rebuilt = None
+        for first, own, other in sums:
+            rebuilt = middle(own, other, weights, layer, first, backward_lat, rebuilt, channels)
+        returned = exchange(rebuilt, peers, devices)
         end = functools.partial(back_transform, modes=returned, local=local, back=backward_lon)
         if layer < layer_count - 1:
             modes = end("modes", extra=forward_lon, **sizes)

time: 123 us -> 121 us (0.984)
  blocking collectives: 51.8 us -> 35.4 us
  starting transfers between devices: 7.43 us -> 13.6 us
  waiting for transfers between devices: 22.6 us -> 27.9 us
  Pallas kernels: 37.9 us -> 40.7 us
    ppermute x0 -> x4, waiting for transfers between devices: none -> 18.2 us  [shards(): sums.append((first, own, lax.ppermute(own, 'lat', swap)))]
    all_to_all x2, blocking collectives: 51.8 us -> 35.4 us  [exchange(): lax.all_to_all(parts, 'lat', 0, 0, tiled=True, axis_index_groups=groups)]
    all_to_all x2, waiting for transfers between devices: 22.6 us -> 9.7 us  [exchange(): lax.all_to_all(parts, 'lat', 0, 0, tiled=True, axis_index_groups=groups)]
    ppermute x0 -> x4, starting transfers between devices: none -> 6.12 us  [shards(): sums.append((first, own, lax.ppermute(own, 'lat', swap)))]
    pallas_call x2 -> x8, Pallas kernels: 4.98 us -> 7.79 us  [the longest x4 6.18 us: middle(): pl.pallas_call(functools.partial(middle_kernel, channels, layer, first),...]
  transfers between devices with their start and end apart: 2 -> 6, of which waited for: 2 -> 6; matrix products, arithmetic and copies ran while one was open for 2% -> 1% of each run, Pallas kernels for 13% -> 16%
where the time goes in v6:
time: 121 us; the launch traced here: 120 us
  Pallas kernels  40.7 us (34%)
  blocking collectives  35.4 us (29%)
  waiting for transfers between devices  27.9 us (23%)
  starting transfers between devices  13.6 us (11%)
  local copies, waits for them, and re-layouts  1.95 us (2%)
    all_to_all x2, blocking collectives, exchange(): lax.all_to_all(parts, 'lat', 0, 0, tiled=True, axis_index_groups=groups)  35.4 us
    pallas_call x3, Pallas kernels, back_transform(): pl.pallas_call(functools.partial(back_kernel, block_rows, channels, devic...  20 us
    ppermute x4, waiting for transfers between devices, shards(): sums.append((first, own, lax.ppermute(own, 'lat', swap)))  18.2 us
    all_to_all x2, waiting for transfers between devices, exchange(): lax.all_to_all(parts, 'lat', 0, 0, tiled=True, axis_index_groups=groups)  9.7 us
    pallas_call x1, Pallas kernels, local_mix(): pl.pallas_call(local_kernel, grid=(field.shape[0] // weight.shape[0],), i...  8.04 us
    all_to_all x2, starting transfers between devices, exchange(): lax.all_to_all(parts, 'lat', 0, 0, tiled=True, axis_index_groups=groups)  7.43 us
    pallas_call x4, Pallas kernels, middle(): pl.pallas_call(functools.partial(middle_kernel, channels, layer, first),...  6.18 us
    ppermute x4, starting transfers between devices, shards(): sums.append((first, own, lax.ppermute(own, 'lat', swap)))  6.12 us
  transfers between devices with their start and end apart: 6, of which 6 were waited for; matrix products, arithmetic and copies ran while one was open for 1% of the time, Pallas kernels for 16%

profile of v6, /device:TPU:0, one launch (start us, length us, event | category | flops | bytes accessed | tf_op | source)
XLA Modules:
  0.0 120.1 jit_solution(7952871518916299326)
XLA Ops:
  0.0 0.0 copy-start.2
  0.0 0.0 copy-start.1
  0.0 4.9 %shard_map.73 = (bf16[384,1024]{1,0:T(8,128)(2,1)S(1)}, bf16[2,8,64,128]{3,2,1,0:T(8,128)(2,1)S(1)}) custom-call(bf16[1536,2048]{1,0:T(8,128)(2,1)} %bitcast.21, bf16[256,2048]{1,0:T(8,128)(2,1)} %constant.12.clone.table_ref.rest_0_, bf16[2,128,64,128]{3,2,1,0:T(8,128)(2,1)} %weights_ref.1), custom_call_target="tpu_custom_call" | custom-call | tf_op jit(solution)/shard_map/pallas_call | solution.py:164
  4.9 0.0 copy-start.4
  4.9 19.4 %all_to_all.20 = bf16[16,24,1024]{2,1,0:T(8,128)(2,1)S(1)} all-to-all(bf16[16,24,1024]{2,1,0:T(8,128)(2,1)S(1)} %bitcast.20), channel_id=1, replica_groups={{0,1,2,3,4,5,6,7,8,9,10,11,12,13,14,15},{16,17,18,19,20,21,22,23,24,25,..., dimensions={0} | all-to-all | bytes 1572864 | tf_op jit(solution)/shard_map/all_to_all | solution.py:370
  24.3 0.0 copy-done.2
  24.3 0.4 shard_map.75.own_ref
  24.7 2.7 %collective-permute-start.1 = (bf16[128,512]{1,0:T(8,128)(2,1)S(1)}, bf16[128,512]{1,0:T(8,128)(2,1)S(1)}, u32[]{:S(2)}, u32[]{:S(2)}) collective-permute-start(bf16[128,512]{1,0:T(8,128)(2,1)S(1)} %shard_map.75.own_ref), channel_id=1, source_target_pairs={{0,16},{1,17},{2,18},{3,19},{4,20},{5,21},{6,22},{7,23},{8,24},{9,... | collective-permute-start | bytes 393224 | tf_op jit(solution)/shard_map/ppermute | solution.py:400
  27.4 0.4 shard_map.74.own_ref
  27.8 0.4 collective-permute-start
  28.2 8.4 %collective-permute-done.1.other_ref = bf16[128,512]{1,0:T(8,128)(2,1)S(1)} collective-permute-done((bf16[128,512]{1,0:T(8,128)(2,1)S(1)}, bf16[128,512]{1,0:T(8,128)(2,1)S(1)}, u32[]{:S(2)}, u32[]{:S(2)}) %collective-permute-start.1) | collective-permute-done | bytes 131104 | tf_op jit(solution)/shard_map/ppermute | solution.py:400
  36.7 0.0 copy-done.1
  36.7 1.6 %shard_map.76.rest_0_ = bf16[384,1024]{1,0:T(8,128)(2,1)} custom-call(bf16[128,512]{1,0:T(8,128)(2,1)S(1)} %shard_map.75.own_ref, bf16[128,512]{1,0:T(8,128)(2,1)S(1)} %collective-permute-done.1.other_ref, bf16[2,8,64,128]{3,2,1,0:T(8,128)(2,1)S(1)} %get-tuple-element.8.weights_ref, bf16[2,384,256]{2,1,0:T(8,128)(2,1)S(1)} %copy-done.1), custom_call_target="tpu_custom_call" | custom-call | tf_op jit(solution)/shard_map/pallas_call | solution.py:255
  38.2 0.6 collective-permute-done.other_ref
  38.9 1.5 %shard_map.77 = bf16[384,1024]{1,0:T(8,128)(2,1)} custom-call(bf16[128,512]{1,0:T(8,128)(2,1)S(1)} %shard_map.74.own_ref, bf16[128,512]{1,0:T(8,128)(2,1)S(1)} %collective-permute-done.other_ref, bf16[2,8,64,128]{3,2,1,0:T(8,128)(2,1)S(1)} %get-tuple-element.8.weights_ref, bf16[2,384,256]{2,1,0:T(8,128)(2,1)S(1)} %copy-done.1, ...), custom_call_target="tpu_custom_call", output_to_operand_aliasing={{}: (4, {})} | custom-call | tf_op jit(solution)/shard_map/pallas_call | solution.py:255
  40.4 3.6 %all-to-all-start.1 = ((bf16[16,24,1024]{2,1,0:T(8,128)(2,1)}), bf16[16,24,1024]{2,1,0:T(8,128)(2,1)S(1)}, u32[]{:S(2)}, u32[]{:S(2)}) async-start(bf16[16,24,1024]{2,1,0:T(8,128)(2,1)} %bitcast.24), calls=%async_computation.1 | async-start | bytes 1572864 | tf_op jit(solution)/shard_map/all_to_all | solution.py:370
  44.0 0.0 copy-done.4
  44.1 0.1 copy.10
  44.2 0.3 multiply_bitcast_fusion
  44.4 0.2 fusion.1
  44.6 0.2 squeeze.6.weight_ref
  44.9 0.0 copy-start
  44.9 8.0 %shard_map.78.local_ref = bf16[1536,2048]{1,0:T(8,128)(2,1)} custom-call(bf16[1536,2048]{1,0:T(8,128)(2,1)} %bitcast.22, bf16[256,256]{1,0:T(8,128)(2,1)S(1)} %squeeze.6.weight_ref), custom_call_target="tpu_custom_call" | custom-call | tf_op jit(solution)/shard_map/pallas_call | solution.py:185
  52.9 4.5 %all-to-all-done.1 = bf16[16,24,1024]{2,1,0:T(8,128)(2,1)S(1)} async-done(((bf16[16,24,1024]{2,1,0:T(8,128)(2,1)}), bf16[16,24,1024]{2,1,0:T(8,128)(2,1)S(1)}, u32[]{:S(2)}, u32[]{:S(2)}) %all-to-all-start.1) | async-done | bytes 786464 | tf_op jit(solution)/shard_map/all_to_all | solution.py:370
  57.4 0.0 copy-done
  57.4 0.0 copy-start.3
  57.4 1.2 %copy-done.3 = bf16[256,2048]{1,0:T(8,128)(2,1)S(1)} copy-done((bf16[256,2048]{1,0:T(8,128)(2,1)S(1)}, bf16[256,2048]{1,0:T(8,128)(2,1)}, u32[]{:S(2)}) %copy-start.3) | copy-done | bytes 1048600
  58.6 6.3 %shard_map.79 = bf16[384,1024]{1,0:T(8,128)(2,1)S(1)} custom-call(bf16[384,1024]{1,0:T(8,128)(2,1)S(1)} %bitcast.12, bf16[1536,2048]{1,0:T(8,128)(2,1)} %shard_map.78.local_ref, bf16[256,2048]{1,0:T(8,128)(2,1)S(1)} %copy-done, bf16[256,2048]{1,0:T(8,128)(2,1)S(1)} %copy-done.3), custom_call_target="tpu_custom_call" | custom-call | tf_op jit(solution)/shard_map/pallas_call | solution.py:355
  64.9 16.0 %all_to_all.21 = bf16[16,24,1024]{2,1,0:T(8,128)(2,1)S(1)} all-to-all(bf16[16,24,1024]{2,1,0:T(8,128)(2,1)S(1)} %bitcast.19), channel_id=1, replica_groups={{0,1,2,3,4,5,6,7,8,9,10,11,12,13,14,15},{16,17,18,19,20,21,22,23,24,25,..., dimensions={0} | all-to-all | bytes 1572864 | tf_op jit(solution)/shard_map/all_to_all | solution.py:370
  80.9 0.4 shard_map.81.own_ref
  81.3 1.7 %collective-permute-start.3 = (bf16[128,512]{1,0:T(8,128)(2,1)S(1)}, bf16[128,512]{1,0:T(8,128)(2,1)S(1)}, u32[]{:S(2)}, u32[]{:S(2)}) collective-permute-start(bf16[128,512]{1,0:T(8,128)(2,1)S(1)} %shard_map.81.own_ref), channel_id=1, source_target_pairs={{0,16},{1,17},{2,18},{3,19},{4,20},{5,21},{6,22},{7,23},{8,24},{9,... | collective-permute-start | bytes 393224 | tf_op jit(solution)/shard_map/ppermute | solution.py:400
  83.1 0.4 shard_map.80.own_ref
  83.5 1.3 %collective-permute-start.2 = (bf16[128,512]{1,0:T(8,128)(2,1)S(1)}, bf16[128,512]{1,0:T(8,128)(2,1)S(1)}, u32[]{:S(2)}, u32[]{:S(2)}) collective-permute-start(bf16[128,512]{1,0:T(8,128)(2,1)S(1)} %shard_map.80.own_ref), channel_id=1, source_target_pairs={{0,16},{1,17},{2,18},{3,19},{4,20},{5,21},{6,22},{7,23},{8,24},{9,... | collective-permute-start | bytes 393224 | tf_op jit(solution)/shard_map/ppermute | solution.py:400
  84.8 8.4 %collective-permute-done.3.other_ref = bf16[128,512]{1,0:T(8,128)(2,1)S(1)} collective-permute-done((bf16[128,512]{1,0:T(8,128)(2,1)S(1)}, bf16[128,512]{1,0:T(8,128)(2,1)S(1)}, u32[]{:S(2)}, u32[]{:S(2)}) %collective-permute-start.3) | collective-permute-done | bytes 131104 | tf_op jit(solution)/shard_map/ppermute | solution.py:400
  93.2 1.5 %shard_map.82.rest_0_ = bf16[384,1024]{1,0:T(8,128)(2,1)} custom-call(bf16[128,512]{1,0:T(8,128)(2,1)S(1)} %shard_map.81.own_ref, bf16[128,512]{1,0:T(8,128)(2,1)S(1)} %collective-permute-done.3.other_ref, bf16[2,8,64,128]{3,2,1,0:T(8,128)(2,1)S(1)} %get-tuple-element.8.weights_ref, bf16[2,384,256]{2,1,0:T(8,128)(2,1)S(1)} %copy-done.1), custom_call_target="tpu_custom_call" | custom-call | tf_op jit(solution)/shard_map/pallas_call | solution.py:255
  94.8 0.7 collective-permute-done.2.other_ref
  95.4 1.5 %shard_map.83 = bf16[384,1024]{1,0:T(8,128)(2,1)} custom-call(bf16[128,512]{1,0:T(8,128)(2,1)S(1)} %shard_map.80.own_ref, bf16[128,512]{1,0:T(8,128)(2,1)S(1)} %collective-permute-done.2.other_ref, bf16[2,8,64,128]{3,2,1,0:T(8,128)(2,1)S(1)} %get-tuple-element.8.weights_ref, bf16[2,384,256]{2,1,0:T(8,128)(2,1)S(1)} %copy-done.1, ...), custom_call_target="tpu_custom_call", output_to_operand_aliasing={{}: (4, {})} | custom-call | tf_op jit(solution)/shard_map/pallas_call | solution.py:255
  97.0 3.8 %all-to-all-start.3 = ((bf16[16,24,1024]{2,1,0:T(8,128)(2,1)}), bf16[16,24,1024]{2,1,0:T(8,128)(2,1)S(1)}, u32[]{:S(2)}, u32[]{:S(2)}) async-start(bf16[16,24,1024]{2,1,0:T(8,128)(2,1)} %bitcast.23), calls=%async_computation.3 | async-start | bytes 1572864 | tf_op jit(solution)/shard_map/all_to_all | solution.py:370
  100.8 0.2 squeeze.7.rest_0_
  101.0 7.7 %shard_map.84.local_ref = bf16[1536,2048]{1,0:T(8,128)(2,1)} custom-call(bf16[384,1024]{1,0:T(8,128)(2,1)S(1)} %bitcast.13, bf16[1536,2048]{1,0:T(8,128)(2,1)} %shard_map.78.local_ref, bf16[256,2048]{1,0:T(8,128)(2,1)S(1)} %copy-done, bf16[256,256]{1,0:T(8,128)(2,1)S(1)} %squeeze.7.rest_0_), custom_call_target="tpu_custom_call" | custom-call | tf_op jit(solution)/shard_map/pallas_call | solution.py:355
  108.7 5.2 %all-to-all-done.3 = bf16[16,24,1024]{2,1,0:T(8,128)(2,1)S(1)} async-done(((bf16[16,24,1024]{2,1,0:T(8,128)(2,1)}), bf16[16,24,1024]{2,1,0:T(8,128)(2,1)S(1)}, u32[]{:S(2)}, u32[]{:S(2)}) %all-to-all-start.3) | async-done | bytes 786464 | tf_op jit(solution)/shard_map/all_to_all | solution.py:370
  113.9 6.0 %shard_map.85 = bf16[1536,2048]{1,0:T(8,128)(2,1)} custom-call(bf16[384,1024]{1,0:T(8,128)(2,1)S(1)} %bitcast.18, bf16[1536,2048]{1,0:T(8,128)(2,1)} %shard_map.84.local_ref, bf16[256,2048]{1,0:T(8,128)(2,1)S(1)} %copy-done), custom_call_target="tpu_custom_call" | custom-call | tf_op jit(solution)/shard_map/pallas_call | solution.py:355
  (1 shorter events, 0.0 us)
Async XLA Ops:
  0.0 24.3 %copy-start.2 = (bf16[2,256,384]{2,1,0:T(8,128)(2,1)S(1)}, bf16[2,256,384]{2,1,0:T(8,128)(2,1)}, u32[]{:S(2)}) copy-start(bf16[2,256,384]{2,1,0:T(8,128)(2,1)} %constant.13.clone.forward_ref) | copy-start | bytes 1179652
  0.0 36.7 %copy-start.1 = (bf16[2,384,256]{2,1,0:T(8,128)(2,1)S(1)}, bf16[2,384,256]{2,1,0:T(8,128)(2,1)}, u32[]{:S(2)}) copy-start(bf16[2,384,256]{2,1,0:T(8,128)(2,1)} %constant.14.clone.backward_ref) | copy-start | bytes 1179652
  4.9 39.2 %copy-start.4 = (bf16[2,64,64]{2,1,0:T(8,128)(2,1)S(1)}, bf16[2,64,64]{2,1,0:T(8,128)(2,1)}, u32[]{:S(2)}) copy-start(bf16[2,64,64]{2,1,0:T(8,128)(2,1)} %param.9) | copy-start | bytes 49156
  24.7 11.9 %collective-permute-start.1 = (bf16[128,512]{1,0:T(8,128)(2,1)S(1)}, bf16[128,512]{1,0:T(8,128)(2,1)S(1)}, u32[]{:S(2)}, u32[]{:S(2)}) collective-permute-start(bf16[128,512]{1,0:T(8,128)(2,1)S(1)} %shard_map.75.own_ref), channel_id=1, source_target_pairs={{0,16},{1,17},{2,18},{3,19},{4,20},{5,21},{6,22},{7,23},{8,24},{9,... | collective-permute-start | bytes 393224 | tf_op jit(solution)/shard_map/ppermute | solution.py:400
  27.8 11.1 %collective-permute-start = (bf16[128,512]{1,0:T(8,128)(2,1)S(1)}, bf16[128,512]{1,0:T(8,128)(2,1)S(1)}, u32[]{:S(2)}, u32[]{:S(2)}) collective-permute-start(bf16[128,512]{1,0:T(8,128)(2,1)S(1)} %shard_map.74.own_ref), channel_id=1, source_target_pairs={{0,16},{1,17},{2,18},{3,19},{4,20},{5,21},{6,22},{7,23},{8,24},{9,... | collective-permute-start | bytes 393224 | tf_op jit(solution)/shard_map/ppermute | solution.py:400
  40.4 17.0 %all-to-all-start.1 = ((bf16[16,24,1024]{2,1,0:T(8,128)(2,1)}), bf16[16,24,1024]{2,1,0:T(8,128)(2,1)S(1)}, u32[]{:S(2)}, u32[]{:S(2)}) async-start(bf16[16,24,1024]{2,1,0:T(8,128)(2,1)} %bitcast.24), calls=%async_computation.1 | async-start | bytes 1572864 | tf_op jit(solution)/shard_map/all_to_all | solution.py:370
  44.9 12.5 %copy-start = (bf16[256,2048]{1,0:T(8,128)(2,1)S(1)}, bf16[256,2048]{1,0:T(8,128)(2,1)}, u32[]{:S(2)}) copy-start(bf16[256,2048]{1,0:T(8,128)(2,1)} %constant.15.clone.back_ref) | copy-start | bytes 3145732
  57.4 1.2 %copy-start.3 = (bf16[256,2048]{1,0:T(8,128)(2,1)S(1)}, bf16[256,2048]{1,0:T(8,128)(2,1)}, u32[]{:S(2)}) copy-start(bf16[256,2048]{1,0:T(8,128)(2,1)} %constant.12.clone.table_ref.rest_0_) | copy-start | bytes 3145732
  81.3 11.9 %collective-permute-start.3 = (bf16[128,512]{1,0:T(8,128)(2,1)S(1)}, bf16[128,512]{1,0:T(8,128)(2,1)S(1)}, u32[]{:S(2)}, u32[]{:S(2)}) collective-permute-start(bf16[128,512]{1,0:T(8,128)(2,1)S(1)} %shard_map.81.own_ref), channel_id=1, source_target_pairs={{0,16},{1,17},{2,18},{3,19},{4,20},{5,21},{6,22},{7,23},{8,24},{9,... | collective-permute-start | bytes 393224 | tf_op jit(solution)/shard_map/ppermute | solution.py:400
  83.5 12.0 %collective-permute-start.2 = (bf16[128,512]{1,0:T(8,128)(2,1)S(1)}, bf16[128,512]{1,0:T(8,128)(2,1)S(1)}, u32[]{:S(2)}, u32[]{:S(2)}) collective-permute-start(bf16[128,512]{1,0:T(8,128)(2,1)S(1)} %shard_map.80.own_ref), channel_id=1, source_target_pairs={{0,16},{1,17},{2,18},{3,19},{4,20},{5,21},{6,22},{7,23},{8,24},{9,... | collective-permute-start | bytes 393224 | tf_op jit(solution)/shard_map/ppermute | solution.py:400
  97.0 17.0 %all-to-all-start.3 = ((bf16[16,24,1024]{2,1,0:T(8,128)(2,1)}), bf16[16,24,1024]{2,1,0:T(8,128)(2,1)S(1)}, u32[]{:S(2)}, u32[]{:S(2)}) async-start(bf16[16,24,1024]{2,1,0:T(8,128)(2,1)} %bitcast.23), calls=%async_computation.3 | async-start | bytes 1572864 | tf_op jit(solution)/shard_map/all_to_all | solution.py:370

commit v7 on v6

--- a/solution.py
+++ b/solution.py
@@ -293,6 +293,10 @@
 
     for step in range(steps):
         arriving(step).start()
+    if kind == "modes":
+        wide_out_ref, table_ref, table_sem = rest
+        table_read = pltpu.make_async_copy(extra_ref, table_ref, table_sem)
+        table_read.start()
     unpack(modes_ref, wide_ref)
     few = math.gcd(rows, max(2, 256 // channels))
 
@@ -313,8 +317,10 @@
             total = dot(lhs_ref[part, :], back_ref[:, lons], ((1,), (0,))).astype(BF16)
             field_ref[part, lons] = gelu_of_double(total + local_copy[part, lons])
         if kind == "modes":
-            product = dot(extra_ref[...], field_ref[part, :], ((1,), (1,)))
-            scatter_modes(product, rest[0], step * rows, rows, block_rows, channels, devices)
+            if step == 0:
+                table_read.wait()
+            product = dot(table_ref[...], field_ref[part, :], ((1,), (1,)))
+            scatter_modes(product, wide_out_ref, step * rows, rows, block_rows, channels, devices)
         if kind == "mix":
             unit = extra_ref.shape[0]
             for start in range(0, block, unit):
@@ -331,7 +337,7 @@
         for step in range(steps):
             body(step, 0)
     if kind == "modes":
-        pack(rest[0], out_ref)
+        pack(wide_out_ref, out_ref)
     else:
         for step in range(steps):
             leaving(step).wait()
@@ -348,13 +354,19 @@
         pltpu.SemaphoreType.DMA((steps,)),
     ]
     args = [in_vmem(modes), in_hbm(local), in_vmem(back)]
-    if kind != "field":
+    specs = [RESIDENT, OUTSIDE, RESIDENT]
+    if kind == "mix":
         args.append(in_vmem(extra))
+        specs.append(RESIDENT)
     if kind == "modes":
+        args.append(in_hbm(extra))
+        specs.append(OUTSIDE)
         scratch.append(wide_scratch(modes.shape, channels))
+        scratch.append(pltpu.VMEM(extra.shape, BF16))
+        scratch.append(pltpu.SemaphoreType.DMA(()))
     return pl.pallas_call(
         functools.partial(back_kernel, block_rows, channels, devices, rows, kind),
-        in_specs=[RESIDENT, OUTSIDE] + [RESIDENT] * (len(args) - 2),
+        in_specs=specs,
         out_specs=RESIDENT if kind == "modes" else OUTSIDE,
         out_shape=pltpu.VMEM(modes.shape, BF16)
         if kind == "modes"

time: 121 us -> 120 us (level)
  local copies, waits for them, and re-layouts: 1.95 us -> 0.73 us
    unnamed x11 -> x9, local copies, waits for them, and re-layouts: 1.34 us -> 0.12 us
where the time goes in v7:
time: 120 us
  Pallas kernels  41.6 us (35%)
  blocking collectives  35.4 us (30%)
  waiting for transfers between devices  27.9 us (23%)
  starting transfers between devices  13.6 us (11%)
    all_to_all x2, blocking collectives, exchange(): lax.all_to_all(parts, 'lat', 0, 0, tiled=True, axis_index_groups=groups)  35.4 us
    pallas_call x3, Pallas kernels, back_transform(): pl.pallas_call(functools.partial(back_kernel, block_rows, channels, devic...  20.9 us
    ppermute x4, waiting for transfers between devices, shards(): sums.append((first, own, lax.ppermute(own, 'lat', swap)))  18.2 us
    all_to_all x2, waiting for transfers between devices, exchange(): lax.all_to_all(parts, 'lat', 0, 0, tiled=True, axis_index_groups=groups)  9.69 us
    pallas_call x1, Pallas kernels, local_mix(): pl.pallas_call(local_kernel, grid=(field.shape[0] // weight.shape[0],), i...  8.04 us
    all_to_all x2, starting transfers between devices, exchange(): lax.all_to_all(parts, 'lat', 0, 0, tiled=True, axis_index_groups=groups)  7.43 us
    pallas_call x4, Pallas kernels, middle(): pl.pallas_call(functools.partial(middle_kernel, channels, layer, first),...  6.2 us
    ppermute x4, starting transfers between devices, shards(): sums.append((first, own, lax.ppermute(own, 'lat', swap)))  6.12 us
  transfers between devices with their start and end apart: 6, of which 6 were waited for; matrix products, arithmetic and copies ran while one was open for 1% of the time, Pallas kernels for 16%

profile of v7, /device:TPU:0, one launch (start us, length us, event | category | flops | bytes accessed | tf_op | source)
XLA Modules:
  0.0 119.8 jit_solution(7345703103780339579)
XLA Ops:
  0.0 0.0 copy-start.2
  0.0 0.0 copy-start.1
  0.0 4.9 %shard_map.73 = (bf16[384,1024]{1,0:T(8,128)(2,1)S(1)}, bf16[2,8,64,128]{3,2,1,0:T(8,128)(2,1)S(1)}) custom-call(bf16[1536,2048]{1,0:T(8,128)(2,1)} %bitcast.21, bf16[256,2048]{1,0:T(8,128)(2,1)} %constant.12.clone.table_ref.rest_0_, bf16[2,128,64,128]{3,2,1,0:T(8,128)(2,1)} %weights_ref.1), custom_call_target="tpu_custom_call" | custom-call | tf_op jit(solution)/shard_map/pallas_call | solution.py:164
  4.9 0.0 copy-start.3
  4.9 19.4 %all_to_all.20 = bf16[16,24,1024]{2,1,0:T(8,128)(2,1)S(1)} all-to-all(bf16[16,24,1024]{2,1,0:T(8,128)(2,1)S(1)} %bitcast.20), channel_id=1, replica_groups={{0,1,2,3,4,5,6,7,8,9,10,11,12,13,14,15},{16,17,18,19,20,21,22,23,24,25,..., dimensions={0} | all-to-all | bytes 1572864 | tf_op jit(solution)/shard_map/all_to_all | solution.py:382
  24.3 0.0 copy-done.2
  24.3 0.4 shard_map.75.own_ref
  24.7 2.7 %collective-permute-start.1 = (bf16[128,512]{1,0:T(8,128)(2,1)S(1)}, bf16[128,512]{1,0:T(8,128)(2,1)S(1)}, u32[]{:S(2)}, u32[]{:S(2)}) collective-permute-start(bf16[128,512]{1,0:T(8,128)(2,1)S(1)} %shard_map.75.own_ref), channel_id=1, source_target_pairs={{0,16},{1,17},{2,18},{3,19},{4,20},{5,21},{6,22},{7,23},{8,24},{9,... | collective-permute-start | bytes 393224 | tf_op jit(solution)/shard_map/ppermute | solution.py:412
  27.4 0.4 shard_map.74.own_ref
  27.8 0.4 collective-permute-start
  28.2 8.4 %collective-permute-done.1.other_ref = bf16[128,512]{1,0:T(8,128)(2,1)S(1)} collective-permute-done((bf16[128,512]{1,0:T(8,128)(2,1)S(1)}, bf16[128,512]{1,0:T(8,128)(2,1)S(1)}, u32[]{:S(2)}, u32[]{:S(2)}) %collective-permute-start.1) | collective-permute-done | bytes 131104 | tf_op jit(solution)/shard_map/ppermute | solution.py:412
  36.7 0.0 copy-done.1
  36.7 1.6 %shard_map.76.rest_0_ = bf16[384,1024]{1,0:T(8,128)(2,1)} custom-call(bf16[128,512]{1,0:T(8,128)(2,1)S(1)} %shard_map.75.own_ref, bf16[128,512]{1,0:T(8,128)(2,1)S(1)} %collective-permute-done.1.other_ref, bf16[2,8,64,128]{3,2,1,0:T(8,128)(2,1)S(1)} %get-tuple-element.8.weights_ref, bf16[2,384,256]{2,1,0:T(8,128)(2,1)S(1)} %copy-done.1), custom_call_target="tpu_custom_call" | custom-call | tf_op jit(solution)/shard_map/pallas_call | solution.py:255
  38.2 0.6 collective-permute-done.other_ref
  38.9 1.5 %shard_map.77 = bf16[384,1024]{1,0:T(8,128)(2,1)} custom-call(bf16[128,512]{1,0:T(8,128)(2,1)S(1)} %shard_map.74.own_ref, bf16[128,512]{1,0:T(8,128)(2,1)S(1)} %collective-permute-done.other_ref, bf16[2,8,64,128]{3,2,1,0:T(8,128)(2,1)S(1)} %get-tuple-element.8.weights_ref, bf16[2,384,256]{2,1,0:T(8,128)(2,1)S(1)} %copy-done.1, ...), custom_call_target="tpu_custom_call", output_to_operand_aliasing={{}: (4, {})} | custom-call | tf_op jit(solution)/shard_map/pallas_call | solution.py:255
  40.4 3.6 %all-to-all-start.1 = ((bf16[16,24,1024]{2,1,0:T(8,128)(2,1)}), bf16[16,24,1024]{2,1,0:T(8,128)(2,1)S(1)}, u32[]{:S(2)}, u32[]{:S(2)}) async-start(bf16[16,24,1024]{2,1,0:T(8,128)(2,1)} %bitcast.24), calls=%async_computation.1 | async-start | bytes 1572864 | tf_op jit(solution)/shard_map/all_to_all | solution.py:382
  44.1 0.0 copy-done.3
  44.1 0.1 copy.10
  44.2 0.3 multiply_bitcast_fusion
  44.4 0.2 fusion.1
  44.6 0.2 squeeze.6.weight_ref
  44.9 0.0 copy-start
  44.9 8.0 %shard_map.78.local_ref = bf16[1536,2048]{1,0:T(8,128)(2,1)} custom-call(bf16[1536,2048]{1,0:T(8,128)(2,1)} %bitcast.22, bf16[256,256]{1,0:T(8,128)(2,1)S(1)} %squeeze.6.weight_ref), custom_call_target="tpu_custom_call" | custom-call | tf_op jit(solution)/shard_map/pallas_call | solution.py:185
  52.9 4.5 %all-to-all-done.1 = bf16[16,24,1024]{2,1,0:T(8,128)(2,1)S(1)} async-done(((bf16[16,24,1024]{2,1,0:T(8,128)(2,1)}), bf16[16,24,1024]{2,1,0:T(8,128)(2,1)S(1)}, u32[]{:S(2)}, u32[]{:S(2)}) %all-to-all-start.1) | async-done | bytes 786464 | tf_op jit(solution)/shard_map/all_to_all | solution.py:382
  57.4 0.0 copy-done
  57.4 7.2 %shard_map.79 = bf16[384,1024]{1,0:T(8,128)(2,1)S(1)} custom-call(bf16[384,1024]{1,0:T(8,128)(2,1)S(1)} %bitcast.12, bf16[1536,2048]{1,0:T(8,128)(2,1)} %shard_map.78.local_ref, bf16[256,2048]{1,0:T(8,128)(2,1)S(1)} %copy-done, bf16[256,2048]{1,0:T(8,128)(2,1)} %constant.12.clone.table_ref.rest_0_), custom_call_target="tpu_custom_call" | custom-call | tf_op jit(solution)/shard_map/pallas_call | solution.py:367
  64.6 16.0 %all_to_all.21 = bf16[16,24,1024]{2,1,0:T(8,128)(2,1)S(1)} all-to-all(bf16[16,24,1024]{2,1,0:T(8,128)(2,1)S(1)} %bitcast.19), channel_id=1, replica_groups={{0,1,2,3,4,5,6,7,8,9,10,11,12,13,14,15},{16,17,18,19,20,21,22,23,24,25,..., dimensions={0} | all-to-all | bytes 1572864 | tf_op jit(solution)/shard_map/all_to_all | solution.py:382
  80.6 0.4 shard_map.81.own_ref
  81.0 1.8 %collective-permute-start.3 = (bf16[128,512]{1,0:T(8,128)(2,1)S(1)}, bf16[128,512]{1,0:T(8,128)(2,1)S(1)}, u32[]{:S(2)}, u32[]{:S(2)}) collective-permute-start(bf16[128,512]{1,0:T(8,128)(2,1)S(1)} %shard_map.81.own_ref), channel_id=1, source_target_pairs={{0,16},{1,17},{2,18},{3,19},{4,20},{5,21},{6,22},{7,23},{8,24},{9,... | collective-permute-start | bytes 393224 | tf_op jit(solution)/shard_map/ppermute | solution.py:412
  82.8 0.4 shard_map.80.own_ref
  83.2 1.3 %collective-permute-start.2 = (bf16[128,512]{1,0:T(8,128)(2,1)S(1)}, bf16[128,512]{1,0:T(8,128)(2,1)S(1)}, u32[]{:S(2)}, u32[]{:S(2)}) collective-permute-start(bf16[128,512]{1,0:T(8,128)(2,1)S(1)} %shard_map.80.own_ref), channel_id=1, source_target_pairs={{0,16},{1,17},{2,18},{3,19},{4,20},{5,21},{6,22},{7,23},{8,24},{9,... | collective-permute-start | bytes 393224 | tf_op jit(solution)/shard_map/ppermute | solution.py:412
  84.4 8.4 %collective-permute-done.3.other_ref = bf16[128,512]{1,0:T(8,128)(2,1)S(1)} collective-permute-done((bf16[128,512]{1,0:T(8,128)(2,1)S(1)}, bf16[128,512]{1,0:T(8,128)(2,1)S(1)}, u32[]{:S(2)}, u32[]{:S(2)}) %collective-permute-start.3) | collective-permute-done | bytes 131104 | tf_op jit(solution)/shard_map/ppermute | solution.py:412
  92.9 1.5 %shard_map.82.rest_0_ = bf16[384,1024]{1,0:T(8,128)(2,1)} custom-call(bf16[128,512]{1,0:T(8,128)(2,1)S(1)} %shard_map.81.own_ref, bf16[128,512]{1,0:T(8,128)(2,1)S(1)} %collective-permute-done.3.other_ref, bf16[2,8,64,128]{3,2,1,0:T(8,128)(2,1)S(1)} %get-tuple-element.8.weights_ref, bf16[2,384,256]{2,1,0:T(8,128)(2,1)S(1)} %copy-done.1), custom_call_target="tpu_custom_call" | custom-call | tf_op jit(solution)/shard_map/pallas_call | solution.py:255
  94.4 0.7 collective-permute-done.2.other_ref
  95.1 1.5 %shard_map.83 = bf16[384,1024]{1,0:T(8,128)(2,1)} custom-call(bf16[128,512]{1,0:T(8,128)(2,1)S(1)} %shard_map.80.own_ref, bf16[128,512]{1,0:T(8,128)(2,1)S(1)} %collective-permute-done.2.other_ref, bf16[2,8,64,128]{3,2,1,0:T(8,128)(2,1)S(1)} %get-tuple-element.8.weights_ref, bf16[2,384,256]{2,1,0:T(8,128)(2,1)S(1)} %copy-done.1, ...), custom_call_target="tpu_custom_call", output_to_operand_aliasing={{}: (4, {})} | custom-call | tf_op jit(solution)/shard_map/pallas_call | solution.py:255
  96.7 3.8 %all-to-all-start.3 = ((bf16[16,24,1024]{2,1,0:T(8,128)(2,1)}), bf16[16,24,1024]{2,1,0:T(8,128)(2,1)S(1)}, u32[]{:S(2)}, u32[]{:S(2)}) async-start(bf16[16,24,1024]{2,1,0:T(8,128)(2,1)} %bitcast.23), calls=%async_computation.3 | async-start | bytes 1572864 | tf_op jit(solution)/shard_map/all_to_all | solution.py:382
  100.5 0.2 squeeze.7.rest_0_
  100.7 7.7 %shard_map.84.local_ref = bf16[1536,2048]{1,0:T(8,128)(2,1)} custom-call(bf16[384,1024]{1,0:T(8,128)(2,1)S(1)} %bitcast.13, bf16[1536,2048]{1,0:T(8,128)(2,1)} %shard_map.78.local_ref, bf16[256,2048]{1,0:T(8,128)(2,1)S(1)} %copy-done, bf16[256,256]{1,0:T(8,128)(2,1)S(1)} %squeeze.7.rest_0_), custom_call_target="tpu_custom_call" | custom-call | tf_op jit(solution)/shard_map/pallas_call | solution.py:367
  108.4 5.2 %all-to-all-done.3 = bf16[16,24,1024]{2,1,0:T(8,128)(2,1)S(1)} async-done(((bf16[16,24,1024]{2,1,0:T(8,128)(2,1)}), bf16[16,24,1024]{2,1,0:T(8,128)(2,1)S(1)}, u32[]{:S(2)}, u32[]{:S(2)}) %all-to-all-start.3) | async-done | bytes 786464 | tf_op jit(solution)/shard_map/all_to_all | solution.py:382
  113.6 6.0 %shard_map.85 = bf16[1536,2048]{1,0:T(8,128)(2,1)} custom-call(bf16[384,1024]{1,0:T(8,128)(2,1)S(1)} %bitcast.18, bf16[1536,2048]{1,0:T(8,128)(2,1)} %shard_map.84.local_ref, bf16[256,2048]{1,0:T(8,128)(2,1)S(1)} %copy-done), custom_call_target="tpu_custom_call" | custom-call | tf_op jit(solution)/shard_map/pallas_call | solution.py:367
  (1 shorter events, 0.0 us)
Async XLA Ops:
  0.0 24.3 %copy-start.2 = (bf16[2,256,384]{2,1,0:T(8,128)(2,1)S(1)}, bf16[2,256,384]{2,1,0:T(8,128)(2,1)}, u32[]{:S(2)}) copy-start(bf16[2,256,384]{2,1,0:T(8,128)(2,1)} %constant.13.clone.forward_ref) | copy-start | bytes 1179652
  0.0 36.7 %copy-start.1 = (bf16[2,384,256]{2,1,0:T(8,128)(2,1)S(1)}, bf16[2,384,256]{2,1,0:T(8,128)(2,1)}, u32[]{:S(2)}) copy-start(bf16[2,384,256]{2,1,0:T(8,128)(2,1)} %constant.14.clone.backward_ref) | copy-start | bytes 1179652
  4.9 39.2 %copy-start.3 = (bf16[2,64,64]{2,1,0:T(8,128)(2,1)S(1)}, bf16[2,64,64]{2,1,0:T(8,128)(2,1)}, u32[]{:S(2)}) copy-start(bf16[2,64,64]{2,1,0:T(8,128)(2,1)} %param.9) | copy-start | bytes 49156
  24.7 11.9 %collective-permute-start.1 = (bf16[128,512]{1,0:T(8,128)(2,1)S(1)}, bf16[128,512]{1,0:T(8,128)(2,1)S(1)}, u32[]{:S(2)}, u32[]{:S(2)}) collective-permute-start(bf16[128,512]{1,0:T(8,128)(2,1)S(1)} %shard_map.75.own_ref), channel_id=1, source_target_pairs={{0,16},{1,17},{2,18},{3,19},{4,20},{5,21},{6,22},{7,23},{8,24},{9,... | collective-permute-start | bytes 393224 | tf_op jit(solution)/shard_map/ppermute | solution.py:412
  27.8 11.1 %collective-permute-start = (bf16[128,512]{1,0:T(8,128)(2,1)S(1)}, bf16[128,512]{1,0:T(8,128)(2,1)S(1)}, u32[]{:S(2)}, u32[]{:S(2)}) collective-permute-start(bf16[128,512]{1,0:T(8,128)(2,1)S(1)} %shard_map.74.own_ref), channel_id=1, source_target_pairs={{0,16},{1,17},{2,18},{3,19},{4,20},{5,21},{6,22},{7,23},{8,24},{9,... | collective-permute-start | bytes 393224 | tf_op jit(solution)/shard_map/ppermute | solution.py:412
  40.4 17.0 %all-to-all-start.1 = ((bf16[16,24,1024]{2,1,0:T(8,128)(2,1)}), bf16[16,24,1024]{2,1,0:T(8,128)(2,1)S(1)}, u32[]{:S(2)}, u32[]{:S(2)}) async-start(bf16[16,24,1024]{2,1,0:T(8,128)(2,1)} %bitcast.24), calls=%async_computation.1 | async-start | bytes 1572864 | tf_op jit(solution)/shard_map/all_to_all | solution.py:382
  44.9 12.5 %copy-start = (bf16[256,2048]{1,0:T(8,128)(2,1)S(1)}, bf16[256,2048]{1,0:T(8,128)(2,1)}, u32[]{:S(2)}) copy-start(bf16[256,2048]{1,0:T(8,128)(2,1)} %constant.15.clone.back_ref) | copy-start | bytes 3145732
  81.0 11.9 %collective-permute-start.3 = (bf16[128,512]{1,0:T(8,128)(2,1)S(1)}, bf16[128,512]{1,0:T(8,128)(2,1)S(1)}, u32[]{:S(2)}, u32[]{:S(2)}) collective-permute-start(bf16[128,512]{1,0:T(8,128)(2,1)S(1)} %shard_map.81.own_ref), channel_id=1, source_target_pairs={{0,16},{1,17},{2,18},{3,19},{4,20},{5,21},{6,22},{7,23},{8,24},{9,... | collective-permute-start | bytes 393224 | tf_op jit(solution)/shard_map/ppermute | solution.py:412
  83.2 12.0 %collective-permute-start.2 = (bf16[128,512]{1,0:T(8,128)(2,1)S(1)}, bf16[128,512]{1,0:T(8,128)(2,1)S(1)}, u32[]{:S(2)}, u32[]{:S(2)}) collective-permute-start(bf16[128,512]{1,0:T(8,128)(2,1)S(1)} %shard_map.80.own_ref), channel_id=1, source_target_pairs={{0,16},{1,17},{2,18},{3,19},{4,20},{5,21},{6,22},{7,23},{8,24},{9,... | collective-permute-start | bytes 393224 | tf_op jit(solution)/shard_map/ppermute | solution.py:412
  96.7 17.0 %all-to-all-start.3 = ((bf16[16,24,1024]{2,1,0:T(8,128)(2,1)}), bf16[16,24,1024]{2,1,0:T(8,128)(2,1)S(1)}, u32[]{:S(2)}, u32[]{:S(2)}) async-start(bf16[16,24,1024]{2,1,0:T(8,128)(2,1)} %bitcast.23), calls=%async_computation.3 | async-start | bytes 1572864 | tf_op jit(solution)/shard_map/all_to_all | solution.py:382

commit v8 on v6

--- a/solution.py
+++ b/solution.py
@@ -127,13 +127,19 @@
 
 def first_kernel(
     block_rows, channels, devices, rows,
-    fields_ref, table_ref, weights_ref, modes_ref, own_ref, copy_ref, table_copy, wide_ref, sems,
+    fields_ref, table_ref, weights_ref, forward_ref, backward_ref,
+    modes_ref, own_ref, own_forward, own_backward, copy_ref, table_copy, wide_ref, sems,
 ):
     steps, block = block_rows // rows, rows * channels
     table_read = pltpu.make_async_copy(table_ref, table_copy, sems.at[steps])
     per_device = own_ref.shape[1]
     own = pl.ds(lax.rem(lax.axis_index("lat"), devices) * per_device, per_device)
-    own_read = pltpu.make_async_copy(weights_ref.at[:, own], own_ref, sems.at[steps + 1])
+    half = lax.axis_index("lat") * forward_ref.shape[0] // lax.axis_size("lat")
+    own_reads = [
+        pltpu.make_async_copy(weights_ref.at[:, own], own_ref, sems.at[steps + 1]),
+        pltpu.make_async_copy(forward_ref.at[half], own_forward, sems.at[steps + 2]),
+        pltpu.make_async_copy(backward_ref.at[half], own_backward, sems.at[steps + 3]),
+    ]
 
     def read(step):
         part = pl.ds(step * block, block)
@@ -142,7 +148,8 @@
     table_read.start()
     for step in range(steps):
         read(step).start()
-    own_read.start()
+    for own_read in own_reads:
+        own_read.start()
     table_read.wait()
 
     def body(step, carry):
@@ -153,27 +160,29 @@
         return carry
 
     lax.fori_loop(0, steps, body, 0)
-    own_read.wait()
+    for own_read in own_reads:
+        own_read.wait()
     pack(wide_ref, modes_ref)
 
 
-def first_transform(fields, table, weights, block_rows, channels, devices, rows):
+def first_transform(fields, table, weights, lat_pair, block_rows, channels, devices, rows):
     per_device = weights.shape[1] // devices
     own_shape = (weights.shape[0], per_device) + weights.shape[2:]
     modes_shape = (devices * block_rows, table.shape[0] // devices * channels)
     return pl.pallas_call(
         functools.partial(first_kernel, block_rows, channels, devices, rows),
-        in_specs=[OUTSIDE, OUTSIDE, OUTSIDE],
-        out_specs=[RESIDENT, RESIDENT],
-        out_shape=[pltpu.VMEM(modes_shape, BF16), pltpu.VMEM(own_shape, BF16)],
+        in_specs=[OUTSIDE] * 5,
+        out_specs=[RESIDENT] * 4,
+        out_shape=[pltpu.VMEM(modes_shape, BF16), pltpu.VMEM(own_shape, BF16)]
+        + [pltpu.VMEM(pair.shape[1:], BF16) for pair in lat_pair],
         scratch_shapes=[
             pltpu.VMEM(fields.shape, BF16),
             pltpu.VMEM(table.shape, BF16),
             wide_scratch(modes_shape, channels),
-            pltpu.SemaphoreType.DMA((block_rows // rows + 2,)),
+            pltpu.SemaphoreType.DMA((block_rows // rows + 4,)),
         ],
         compiler_params=params(24),
-    )(in_hbm(fields), in_hbm(table), in_hbm(weights))
+    )(*[in_hbm(array) for array in (fields, table, weights, *lat_pair)])
 
 
 def local_kernel(field_ref, weight_ref, out_ref):
@@ -193,11 +202,10 @@
 
 
 def partial_kernel(channels, first, values_ref, forward_ref, out_ref):
-    kept = forward_ref.shape[1] // 2
+    kept = forward_ref.shape[0] // 2
     lanes = 2 * channels
-    half = lax.axis_index("lat") * forward_ref.shape[0] // lax.axis_size("lat")
     columns = slice(first * lanes, first * lanes + out_ref.shape[1])
-    products = dot(forward_ref[half], values_ref[:, columns], ((1,), (0,)))
+    products = dot(forward_ref[...], values_ref[:, columns], ((1,), (0,)))
     low = low_half((kept, lanes), channels)
     for start in range(0, out_ref.shape[1], lanes):
         part = slice(start, start + lanes)
@@ -207,7 +215,7 @@
 
 
 def partial_sums(values, forward, first, count, channels):
-    shape = (forward.shape[1] // 2, count * 2 * channels)
+    shape = (forward.shape[0] // 2, count * 2 * channels)
     return pl.pallas_call(
         functools.partial(partial_kernel, channels, first),
         in_specs=[RESIDENT] * 2,
@@ -223,7 +231,6 @@
     out_ref, copy_ref, sems = rest[-3:]
     kept = own_ref.shape[0]
     lanes = 2 * channels
-    half = lax.axis_index("lat") * backward_ref.shape[0] // lax.axis_size("lat")
     low = low_half((kept, lanes), channels)
     low_w = low_half((channels, lanes), channels)
     writes = []
@@ -236,7 +243,7 @@
         mixed = dot(modes, mixing.astype(BF16), ((1,), (0,)))
         swapped = pltpu.roll(mixed, channels, 1)
         both = jnp.concatenate([mixed, jnp.where(low, -swapped, swapped)], axis=0).astype(BF16)
-        copy_ref[k] = dot(backward_ref[half], both, ((1,), (0,))).astype(BF16)
+        copy_ref[k] = dot(backward_ref[...], both, ((1,), (0,))).astype(BF16)
         target = out_ref.at[:, pl.ds((first + k) * lanes, lanes)]
         writes.append(pltpu.make_async_copy(copy_ref.at[k], target, sems.at[k]))
         writes[-1].start()
@@ -246,7 +253,7 @@
 
 def middle(own, other, weights, layer, first, backward, so_far, channels):
     count = own.shape[1] // (2 * channels)
-    rows = backward.shape[1]
+    rows = backward.shape[0]
     args = [in_vmem(own), in_vmem(other), in_vmem(weights), in_vmem(backward)]
     specs = [RESIDENT] * 4
     if so_far is not None:
@@ -390,7 +397,9 @@
     wide_rows = 2 * rows if block_rows % (2 * rows) == 0 else rows
     sizes = dict(block_rows=block_rows, channels=channels, devices=peers, rows=wide_rows)
     field = fields.reshape(block_rows * channels, lon_count)
-    modes, weights = first_transform(field, forward_lon, spectral_weight, **sizes)
+    modes, weights, forward_lat, backward_lat = first_transform(
+        field, forward_lon, spectral_weight, (forward_lat, backward_lat), **sizes
+    )
     local = local_mix(field, mixers[0])
     for layer in range(layer_count):
         arrived = exchange(modes, peers, devices)

time: 121 us -> 120 us (level)
  waiting for transfers between devices: 27.9 us -> 25.6 us
    all_to_all x2, waiting for transfers between devices: 9.7 us -> 7.36 us  [exchange(): lax.all_to_all(parts, 'lat', 0, 0, tiled=True, axis_index_groups=groups)]
  transfers between devices with their start and end apart: 6 -> 6, of which waited for: 6 -> 6; matrix products, arithmetic and copies ran while one was open for 1% -> 2% of each run, Pallas kernels for 16% -> 17%
where the time goes in v8:
time: 120 us; the launch traced here: 119 us
  Pallas kernels  40.7 us (34%)
  blocking collectives  35.7 us (30%)
  waiting for transfers between devices  25.6 us (21%)
  starting transfers between devices  13.5 us (11%)
  local copies, waits for them, and re-layouts  3 us (2%)
    all_to_all x2, blocking collectives, exchange(): lax.all_to_all(parts, 'lat', 0, 0, tiled=True, axis_index_groups=groups)  35.7 us
    pallas_call x3, Pallas kernels, back_transform(): pl.pallas_call(functools.partial(back_kernel, block_rows, channels, devic...  20 us
    ppermute x4, waiting for transfers between devices, shards(): sums.append((first, own, lax.ppermute(own, 'lat', swap)))  18.2 us
    pallas_call x1, Pallas kernels, local_mix(): pl.pallas_call(local_kernel, grid=(field.shape[0] // weight.shape[0],), i...  8.1 us
    all_to_all x2, starting transfers between devices, exchange(): lax.all_to_all(parts, 'lat', 0, 0, tiled=True, axis_index_groups=groups)  7.43 us
    all_to_all x2, waiting for transfers between devices, exchange(): lax.all_to_all(parts, 'lat', 0, 0, tiled=True, axis_index_groups=groups)  7.36 us
    pallas_call x4, Pallas kernels, middle(): pl.pallas_call(functools.partial(middle_kernel, channels, layer, first),...  6.18 us
    ppermute x4, starting transfers between devices, shards(): sums.append((first, own, lax.ppermute(own, 'lat', swap)))  6.11 us
  transfers between devices with their start and end apart: 6, of which 6 were waited for; matrix products, arithmetic and copies ran while one was open for 2% of the time, Pallas kernels for 17%

profile of v8, /device:TPU:0, one launch (start us, length us, event | category | flops | bytes accessed | tf_op | source)
XLA Modules:
  0.0 119.1 jit_solution(5588359290787315496)
XLA Ops:
  0.0 4.8 %shard_map.73 = (bf16[384,1024]{1,0:T(8,128)(2,1)S(1)}, bf16[2,8,64,128]{3,2,1,0:T(8,128)(2,1)S(1)}, bf16[256,384]{1,0:T(8,128)(2,1)S(1)}, bf16[384,256]{1,0:T(8,128)(2,1)S(1)}) custom-call(bf16[1536,2048]{1,0:T(8,128)(2,1)} %bitcast.21, bf16[256,2048]{1,0:T(8,128)(2,1)} %constant.12.clone.table_ref.rest_0_, bf16[2,128,64,128]{3,2,1,0:T(8,128)(2,1)} %weights_ref.1, ...), custom_call_target="tpu_custom_call" | custom-call | tf_op jit(solution)/shard_map/pallas_call | solution.py:172
  4.8 0.0 copy-start.4
  4.8 19.4 %all_to_all.20 = bf16[16,24,1024]{2,1,0:T(8,128)(2,1)S(1)} all-to-all(bf16[16,24,1024]{2,1,0:T(8,128)(2,1)S(1)} %bitcast.20), channel_id=1, replica_groups={{0,1,2,3,4,5,6,7,8,9,10,11,12,13,14,15},{16,17,18,19,20,21,22,23,24,25,..., dimensions={0} | all-to-all | bytes 1572864 | tf_op jit(solution)/shard_map/all_to_all | solution.py:377
  24.3 0.4 shard_map.75.own_ref
  24.7 2.7 %collective-permute-start.1 = (bf16[128,512]{1,0:T(8,128)(2,1)S(1)}, bf16[128,512]{1,0:T(8,128)(2,1)S(1)}, u32[]{:S(2)}, u32[]{:S(2)}) collective-permute-start(bf16[128,512]{1,0:T(8,128)(2,1)S(1)} %shard_map.75.own_ref), channel_id=1, source_target_pairs={{0,16},{1,17},{2,18},{3,19},{4,20},{5,21},{6,22},{7,23},{8,24},{9,... | collective-permute-start | bytes 393224 | tf_op jit(solution)/shard_map/ppermute | solution.py:409
  27.3 0.4 shard_map.74.own_ref
  27.8 0.4 collective-permute-start
  28.2 8.5 %collective-permute-done.1.other_ref = bf16[128,512]{1,0:T(8,128)(2,1)S(1)} collective-permute-done((bf16[128,512]{1,0:T(8,128)(2,1)S(1)}, bf16[128,512]{1,0:T(8,128)(2,1)S(1)}, u32[]{:S(2)}, u32[]{:S(2)}) %collective-permute-start.1) | collective-permute-done | bytes 131104 | tf_op jit(solution)/shard_map/ppermute | solution.py:409
  36.6 1.6 %shard_map.76.rest_0_ = bf16[384,1024]{1,0:T(8,128)(2,1)} custom-call(bf16[128,512]{1,0:T(8,128)(2,1)S(1)} %shard_map.75.own_ref, bf16[128,512]{1,0:T(8,128)(2,1)S(1)} %collective-permute-done.1.other_ref, bf16[2,8,64,128]{3,2,1,0:T(8,128)(2,1)S(1)} %get-tuple-element.11.weights_ref, bf16[384,256]{1,0:T(8,128)(2,1)S(1)} %get-tuple-element.12.backward_ref), custom_call_target="tpu_custom_call" | custom-call | tf_op jit(solution)/shard_map/pallas_call | solution.py:262
  38.2 0.7 collective-permute-done.other_ref
  38.8 1.5 %shard_map.77 = bf16[384,1024]{1,0:T(8,128)(2,1)} custom-call(bf16[128,512]{1,0:T(8,128)(2,1)S(1)} %shard_map.74.own_ref, bf16[128,512]{1,0:T(8,128)(2,1)S(1)} %collective-permute-done.other_ref, bf16[2,8,64,128]{3,2,1,0:T(8,128)(2,1)S(1)} %get-tuple-element.11.weights_ref, ...), custom_call_target="tpu_custom_call", output_to_operand_aliasing={{}: (4, {})} | custom-call | tf_op jit(solution)/shard_map/pallas_call | solution.py:262
  40.4 3.6 %all-to-all-start.1 = ((bf16[16,24,1024]{2,1,0:T(8,128)(2,1)}), bf16[16,24,1024]{2,1,0:T(8,128)(2,1)S(1)}, u32[]{:S(2)}, u32[]{:S(2)}) async-start(bf16[16,24,1024]{2,1,0:T(8,128)(2,1)} %bitcast.24), calls=%async_computation.1 | async-start | bytes 1572864 | tf_op jit(solution)/shard_map/all_to_all | solution.py:377
  44.0 0.0 copy-done.4
  44.0 0.1 copy.10
  44.1 0.3 multiply_bitcast_fusion
  44.4 0.9 fusion.1
  45.3 0.9 squeeze.6.weight_ref
  46.2 0.0 copy-start.2
  46.2 0.9 copy-done.2
  47.1 0.0 copy-start
  47.1 0.0 copy-start.1
  47.1 8.1 %shard_map.78.local_ref = bf16[1536,2048]{1,0:T(8,128)(2,1)} custom-call(bf16[1536,2048]{1,0:T(8,128)(2,1)} %bitcast.22, bf16[256,256]{1,0:T(8,128)(2,1)S(1)} %copy-done.2), custom_call_target="tpu_custom_call" | custom-call | tf_op jit(solution)/shard_map/pallas_call | solution.py:194
  55.2 2.1 %all-to-all-done.1 = bf16[16,24,1024]{2,1,0:T(8,128)(2,1)S(1)} async-done(((bf16[16,24,1024]{2,1,0:T(8,128)(2,1)}), bf16[16,24,1024]{2,1,0:T(8,128)(2,1)S(1)}, u32[]{:S(2)}, u32[]{:S(2)}) %all-to-all-start.1) | async-done | bytes 786464 | tf_op jit(solution)/shard_map/all_to_all | solution.py:377
  57.3 0.0 copy-done
  57.3 0.0 copy-done.1
  57.3 6.3 %shard_map.79 = bf16[384,1024]{1,0:T(8,128)(2,1)S(1)} custom-call(bf16[384,1024]{1,0:T(8,128)(2,1)S(1)} %bitcast.12, bf16[1536,2048]{1,0:T(8,128)(2,1)} %shard_map.78.local_ref, bf16[256,2048]{1,0:T(8,128)(2,1)S(1)} %copy-done, bf16[256,2048]{1,0:T(8,128)(2,1)S(1)} %copy-done.1), custom_call_target="tpu_custom_call" | custom-call | tf_op jit(solution)/shard_map/pallas_call | solution.py:362
  63.7 0.0 copy-start.3
  63.7 16.2 %all_to_all.21 = bf16[16,24,1024]{2,1,0:T(8,128)(2,1)S(1)} all-to-all(bf16[16,24,1024]{2,1,0:T(8,128)(2,1)S(1)} %bitcast.19), channel_id=1, replica_groups={{0,1,2,3,4,5,6,7,8,9,10,11,12,13,14,15},{16,17,18,19,20,21,22,23,24,25,..., dimensions={0} | all-to-all | bytes 1572864 | tf_op jit(solution)/shard_map/all_to_all | solution.py:377
  79.9 0.4 shard_map.81.own_ref
  80.3 1.7 %collective-permute-start.3 = (bf16[128,512]{1,0:T(8,128)(2,1)S(1)}, bf16[128,512]{1,0:T(8,128)(2,1)S(1)}, u32[]{:S(2)}, u32[]{:S(2)}) collective-permute-start(bf16[128,512]{1,0:T(8,128)(2,1)S(1)} %shard_map.81.own_ref), channel_id=1, source_target_pairs={{0,16},{1,17},{2,18},{3,19},{4,20},{5,21},{6,22},{7,23},{8,24},{9,... | collective-permute-start | bytes 393224 | tf_op jit(solution)/shard_map/ppermute | solution.py:409
  82.1 0.4 shard_map.80.own_ref
  82.5 1.3 %collective-permute-start.2 = (bf16[128,512]{1,0:T(8,128)(2,1)S(1)}, bf16[128,512]{1,0:T(8,128)(2,1)S(1)}, u32[]{:S(2)}, u32[]{:S(2)}) collective-permute-start(bf16[128,512]{1,0:T(8,128)(2,1)S(1)} %shard_map.80.own_ref), channel_id=1, source_target_pairs={{0,16},{1,17},{2,18},{3,19},{4,20},{5,21},{6,22},{7,23},{8,24},{9,... | collective-permute-start | bytes 393224 | tf_op jit(solution)/shard_map/ppermute | solution.py:409
  83.8 8.4 %collective-permute-done.3.other_ref = bf16[128,512]{1,0:T(8,128)(2,1)S(1)} collective-permute-done((bf16[128,512]{1,0:T(8,128)(2,1)S(1)}, bf16[128,512]{1,0:T(8,128)(2,1)S(1)}, u32[]{:S(2)}, u32[]{:S(2)}) %collective-permute-start.3) | collective-permute-done | bytes 131104 | tf_op jit(solution)/shard_map/ppermute | solution.py:409
  92.2 1.5 %shard_map.82.rest_0_ = bf16[384,1024]{1,0:T(8,128)(2,1)} custom-call(bf16[128,512]{1,0:T(8,128)(2,1)S(1)} %shard_map.81.own_ref, bf16[128,512]{1,0:T(8,128)(2,1)S(1)} %collective-permute-done.3.other_ref, bf16[2,8,64,128]{3,2,1,0:T(8,128)(2,1)S(1)} %get-tuple-element.11.weights_ref, bf16[384,256]{1,0:T(8,128)(2,1)S(1)} %get-tuple-element.12.backward_ref), custom_call_target="tpu_custom_call" | custom-call | tf_op jit(solution)/shard_map/pallas_call | solution.py:262
  93.8 0.7 collective-permute-done.2.other_ref
  94.5 1.5 %shard_map.83 = bf16[384,1024]{1,0:T(8,128)(2,1)} custom-call(bf16[128,512]{1,0:T(8,128)(2,1)S(1)} %shard_map.80.own_ref, bf16[128,512]{1,0:T(8,128)(2,1)S(1)} %collective-permute-done.2.other_ref, bf16[2,8,64,128]{3,2,1,0:T(8,128)(2,1)S(1)} %get-tuple-element.11.weights_ref, ...), custom_call_target="tpu_custom_call", output_to_operand_aliasing={{}: (4, {})} | custom-call | tf_op jit(solution)/shard_map/pallas_call | solution.py:262
  96.0 3.8 %all-to-all-start.3 = ((bf16[16,24,1024]{2,1,0:T(8,128)(2,1)}), bf16[16,24,1024]{2,1,0:T(8,128)(2,1)S(1)}, u32[]{:S(2)}, u32[]{:S(2)}) async-start(bf16[16,24,1024]{2,1,0:T(8,128)(2,1)} %bitcast.23), calls=%async_computation.3 | async-start | bytes 1572864 | tf_op jit(solution)/shard_map/all_to_all | solution.py:377
  99.8 0.0 copy-done.3
  99.8 0.2 squeeze.7.rest_0_
  100.1 7.7 %shard_map.84.local_ref = bf16[1536,2048]{1,0:T(8,128)(2,1)} custom-call(bf16[384,1024]{1,0:T(8,128)(2,1)S(1)} %bitcast.13, bf16[1536,2048]{1,0:T(8,128)(2,1)} %shard_map.78.local_ref, bf16[256,2048]{1,0:T(8,128)(2,1)S(1)} %copy-done, bf16[256,256]{1,0:T(8,128)(2,1)S(1)} %squeeze.7.rest_0_), custom_call_target="tpu_custom_call" | custom-call | tf_op jit(solution)/shard_map/pallas_call | solution.py:362
  107.7 5.2 %all-to-all-done.3 = bf16[16,24,1024]{2,1,0:T(8,128)(2,1)S(1)} async-done(((bf16[16,24,1024]{2,1,0:T(8,128)(2,1)}), bf16[16,24,1024]{2,1,0:T(8,128)(2,1)S(1)}, u32[]{:S(2)}, u32[]{:S(2)}) %all-to-all-start.3) | async-done | bytes 786464 | tf_op jit(solution)/shard_map/all_to_all | solution.py:377
  113.0 6.0 %shard_map.85 = bf16[1536,2048]{1,0:T(8,128)(2,1)} custom-call(bf16[384,1024]{1,0:T(8,128)(2,1)S(1)} %bitcast.18, bf16[1536,2048]{1,0:T(8,128)(2,1)} %shard_map.84.local_ref, bf16[256,2048]{1,0:T(8,128)(2,1)S(1)} %copy-done), custom_call_target="tpu_custom_call" | custom-call | tf_op jit(solution)/shard_map/pallas_call | solution.py:362
  (1 shorter events, 0.0 us)
Async XLA Ops:
  4.8 39.2 %copy-start.4 = (bf16[2,64,64]{2,1,0:T(8,128)(2,1)S(1)}, bf16[2,64,64]{2,1,0:T(8,128)(2,1)}, u32[]{:S(2)}) copy-start(bf16[2,64,64]{2,1,0:T(8,128)(2,1)} %param.9) | copy-start | bytes 49156
  24.7 11.9 %collective-permute-start.1 = (bf16[128,512]{1,0:T(8,128)(2,1)S(1)}, bf16[128,512]{1,0:T(8,128)(2,1)S(1)}, u32[]{:S(2)}, u32[]{:S(2)}) collective-permute-start(bf16[128,512]{1,0:T(8,128)(2,1)S(1)} %shard_map.75.own_ref), channel_id=1, source_target_pairs={{0,16},{1,17},{2,18},{3,19},{4,20},{5,21},{6,22},{7,23},{8,24},{9,... | collective-permute-start | bytes 393224 | tf_op jit(solution)/shard_map/ppermute | solution.py:409
  27.8 11.1 %collective-permute-start = (bf16[128,512]{1,0:T(8,128)(2,1)S(1)}, bf16[128,512]{1,0:T(8,128)(2,1)S(1)}, u32[]{:S(2)}, u32[]{:S(2)}) collective-permute-start(bf16[128,512]{1,0:T(8,128)(2,1)S(1)} %shard_map.74.own_ref), channel_id=1, source_target_pairs={{0,16},{1,17},{2,18},{3,19},{4,20},{5,21},{6,22},{7,23},{8,24},{9,... | collective-permute-start | bytes 393224 | tf_op jit(solution)/shard_map/ppermute | solution.py:409
  40.4 17.0 %all-to-all-start.1 = ((bf16[16,24,1024]{2,1,0:T(8,128)(2,1)}), bf16[16,24,1024]{2,1,0:T(8,128)(2,1)S(1)}, u32[]{:S(2)}, u32[]{:S(2)}) async-start(bf16[16,24,1024]{2,1,0:T(8,128)(2,1)} %bitcast.24), calls=%async_computation.1 | async-start | bytes 1572864 | tf_op jit(solution)/shard_map/all_to_all | solution.py:377
  46.2 0.9 copy-start.2
  47.1 10.2 %copy-start = (bf16[256,2048]{1,0:T(8,128)(2,1)S(1)}, bf16[256,2048]{1,0:T(8,128)(2,1)}, u32[]{:S(2)}) copy-start(bf16[256,2048]{1,0:T(8,128)(2,1)} %constant.15.clone.back_ref) | copy-start | bytes 3145732
  47.1 10.2 %copy-start.1 = (bf16[256,2048]{1,0:T(8,128)(2,1)S(1)}, bf16[256,2048]{1,0:T(8,128)(2,1)}, u32[]{:S(2)}) copy-start(bf16[256,2048]{1,0:T(8,128)(2,1)} %constant.12.clone.table_ref.rest_0_) | copy-start | bytes 3145732
  63.7 36.1 %copy-start.3 = (bf16[1,4,64,4,64]{4,3,2,1,0:T(4,128)(2,1)S(1)}, bf16[1,4,64,4,64]{4,3,2,1,0:T(4,128)(2,1)}, u32[]{:S(2)}) copy-start(bf16[1,4,64,4,64]{4,3,2,1,0:T(4,128)(2,1)} %get-tuple-element.13) | copy-start | bytes 393220
  80.3 11.9 %collective-permute-start.3 = (bf16[128,512]{1,0:T(8,128)(2,1)S(1)}, bf16[128,512]{1,0:T(8,128)(2,1)S(1)}, u32[]{:S(2)}, u32[]{:S(2)}) collective-permute-start(bf16[128,512]{1,0:T(8,128)(2,1)S(1)} %shard_map.81.own_ref), channel_id=1, source_target_pairs={{0,16},{1,17},{2,18},{3,19},{4,20},{5,21},{6,22},{7,23},{8,24},{9,... | collective-permute-start | bytes 393224 | tf_op jit(solution)/shard_map/ppermute | solution.py:409
  82.5 12.0 %collective-permute-start.2 = (bf16[128,512]{1,0:T(8,128)(2,1)S(1)}, bf16[128,512]{1,0:T(8,128)(2,1)S(1)}, u32[]{:S(2)}, u32[]{:S(2)}) collective-permute-start(bf16[128,512]{1,0:T(8,128)(2,1)S(1)} %shard_map.80.own_ref), channel_id=1, source_target_pairs={{0,16},{1,17},{2,18},{3,19},{4,20},{5,21},{6,22},{7,23},{8,24},{9,... | collective-permute-start | bytes 393224 | tf_op jit(solution)/shard_map/ppermute | solution.py:409
  96.0 17.0 %all-to-all-start.3 = ((bf16[16,24,1024]{2,1,0:T(8,128)(2,1)}), bf16[16,24,1024]{2,1,0:T(8,128)(2,1)S(1)}, u32[]{:S(2)}, u32[]{:S(2)}) async-start(bf16[16,24,1024]{2,1,0:T(8,128)(2,1)} %bitcast.23), calls=%async_computation.3 | async-start | bytes 1572864 | tf_op jit(solution)/shard_map/all_to_all | solution.py:377

commit v9 on v8

--- a/solution.py
+++ b/solution.py
@@ -233,8 +233,9 @@
     lanes = 2 * channels
     low = low_half((kept, lanes), channels)
     low_w = low_half((channels, lanes), channels)
-    writes = []
-    for k in range(own_ref.shape[1] // lanes):
+    writes, rhs = [], []
+    count = own_ref.shape[1] // lanes
+    for k in range(count):
         part = slice(k * lanes, (k + 1) * lanes)
         modes = (own_ref[:, part].astype(F32) + other_ref[:, part].astype(F32)).astype(BF16)
         weight = weights_ref[layer, first + k].astype(F32)
@@ -243,10 +244,15 @@
         mixed = dot(modes, mixing.astype(BF16), ((1,), (0,)))
         swapped = pltpu.roll(mixed, channels, 1)
         both = jnp.concatenate([mixed, jnp.where(low, -swapped, swapped)], axis=0).astype(BF16)
-        copy_ref[k] = dot(backward_ref[...], both, ((1,), (0,))).astype(BF16)
-        target = out_ref.at[:, pl.ds((first + k) * lanes, lanes)]
-        writes.append(pltpu.make_async_copy(copy_ref.at[k], target, sems.at[k]))
-        writes[-1].start()
+        rhs.append(both)
+    for start in range(0, count, 2):
+        pair = rhs[start : start + 2]
+        back = dot(backward_ref[...], jnp.concatenate(pair, axis=1), ((1,), (0,))).astype(BF16)
+        for k in range(start, start + len(pair)):
+            copy_ref[k] = back[:, (k - start) * lanes : (k - start + 1) * lanes]
+            target = out_ref.at[:, pl.ds((first + k) * lanes, lanes)]
+            writes.append(pltpu.make_async_copy(copy_ref.at[k], target, sems.at[k]))
+            writes[-1].start()
     for write in writes:
         write.wait()
 

time: 120 us -> 119 us (level)
  transfers between devices with their start and end apart: 6 -> 6, of which waited for: 6 -> 6; matrix products, arithmetic and copies ran while one was open for 2% -> 2% of each run, Pallas kernels for 17% -> 16%
where the time goes in v9:
time: 119 us
  Pallas kernels  40 us (34%)
  blocking collectives  35.7 us (30%)
  waiting for transfers between devices  26 us (22%)
  starting transfers between devices  13.5 us (11%)
  local copies, waits for them, and re-layouts  3 us (3%)
    all_to_all x2, blocking collectives, exchange(): lax.all_to_all(parts, 'lat', 0, 0, tiled=True, axis_index_groups=groups)  35.7 us
    pallas_call x3, Pallas kernels, back_transform(): pl.pallas_call(functools.partial(back_kernel, block_rows, channels, devic...  20 us
    ppermute x4, waiting for transfers between devices, shards(): sums.append((first, own, lax.ppermute(own, 'lat', swap)))  18.6 us
    pallas_call x1, Pallas kernels, local_mix(): pl.pallas_call(local_kernel, grid=(field.shape[0] // weight.shape[0],), i...  8.1 us
    all_to_all x2, starting transfers between devices, exchange(): lax.all_to_all(parts, 'lat', 0, 0, tiled=True, axis_index_groups=groups)  7.43 us
    all_to_all x2, waiting for transfers between devices, exchange(): lax.all_to_all(parts, 'lat', 0, 0, tiled=True, axis_index_groups=groups)  7.36 us
    ppermute x4, starting transfers between devices, shards(): sums.append((first, own, lax.ppermute(own, 'lat', swap)))  6.12 us
    pallas_call x4, Pallas kernels, middle(): pl.pallas_call(functools.partial(middle_kernel, channels, layer, first),...  5.42 us
  transfers between devices with their start and end apart: 6, of which 6 were waited for; matrix products, arithmetic and copies ran while one was open for 2% of the time, Pallas kernels for 16%

profile of v9, /device:TPU:0, one launch (start us, length us, event | category | flops | bytes accessed | tf_op | source)
XLA Modules:
  0.0 118.8 jit_solution(110880795292070068)
XLA Ops:
  0.0 4.8 %shard_map.73 = (bf16[384,1024]{1,0:T(8,128)(2,1)S(1)}, bf16[2,8,64,128]{3,2,1,0:T(8,128)(2,1)S(1)}, bf16[256,384]{1,0:T(8,128)(2,1)S(1)}, bf16[384,256]{1,0:T(8,128)(2,1)S(1)}) custom-call(bf16[1536,2048]{1,0:T(8,128)(2,1)} %bitcast.21, bf16[256,2048]{1,0:T(8,128)(2,1)} %constant.12.clone.table_ref.rest_0_, bf16[2,128,64,128]{3,2,1,0:T(8,128)(2,1)} %weights_ref.1, ...), custom_call_target="tpu_custom_call" | custom-call | tf_op jit(solution)/shard_map/pallas_call | solution.py:172
  4.8 0.0 copy-start.4
  4.8 19.4 %all_to_all.20 = bf16[16,24,1024]{2,1,0:T(8,128)(2,1)S(1)} all-to-all(bf16[16,24,1024]{2,1,0:T(8,128)(2,1)S(1)} %bitcast.20), channel_id=1, replica_groups={{0,1,2,3,4,5,6,7,8,9,10,11,12,13,14,15},{16,17,18,19,20,21,22,23,24,25,..., dimensions={0} | all-to-all | bytes 1572864 | tf_op jit(solution)/shard_map/all_to_all | solution.py:383
  24.3 0.4 shard_map.75.own_ref
  24.7 2.7 %collective-permute-start.1 = (bf16[128,512]{1,0:T(8,128)(2,1)S(1)}, bf16[128,512]{1,0:T(8,128)(2,1)S(1)}, u32[]{:S(2)}, u32[]{:S(2)}) collective-permute-start(bf16[128,512]{1,0:T(8,128)(2,1)S(1)} %shard_map.75.own_ref), channel_id=1, source_target_pairs={{0,16},{1,17},{2,18},{3,19},{4,20},{5,21},{6,22},{7,23},{8,24},{9,... | collective-permute-start | bytes 393224 | tf_op jit(solution)/shard_map/ppermute | solution.py:415
  27.3 0.4 shard_map.74.own_ref
  27.8 0.4 collective-permute-start
  28.2 8.5 %collective-permute-done.1.other_ref = bf16[128,512]{1,0:T(8,128)(2,1)S(1)} collective-permute-done((bf16[128,512]{1,0:T(8,128)(2,1)S(1)}, bf16[128,512]{1,0:T(8,128)(2,1)S(1)}, u32[]{:S(2)}, u32[]{:S(2)}) %collective-permute-start.1) | collective-permute-done | bytes 131104 | tf_op jit(solution)/shard_map/ppermute | solution.py:415
  36.6 1.3 %shard_map.76.rest_0_ = bf16[384,1024]{1,0:T(8,128)(2,1)} custom-call(bf16[128,512]{1,0:T(8,128)(2,1)S(1)} %shard_map.75.own_ref, bf16[128,512]{1,0:T(8,128)(2,1)S(1)} %collective-permute-done.1.other_ref, bf16[2,8,64,128]{3,2,1,0:T(8,128)(2,1)S(1)} %get-tuple-element.11.weights_ref, bf16[384,256]{1,0:T(8,128)(2,1)S(1)} %get-tuple-element.12.backward_ref), custom_call_target="tpu_custom_call" | custom-call | tf_op jit(solution)/shard_map/pallas_call | solution.py:268
  38.0 0.9 collective-permute-done.other_ref
  38.8 1.4 %shard_map.77 = bf16[384,1024]{1,0:T(8,128)(2,1)} custom-call(bf16[128,512]{1,0:T(8,128)(2,1)S(1)} %shard_map.74.own_ref, bf16[128,512]{1,0:T(8,128)(2,1)S(1)} %collective-permute-done.other_ref, bf16[2,8,64,128]{3,2,1,0:T(8,128)(2,1)S(1)} %get-tuple-element.11.weights_ref, ...), custom_call_target="tpu_custom_call", output_to_operand_aliasing={{}: (4, {})} | custom-call | tf_op jit(solution)/shard_map/pallas_call | solution.py:268
  40.2 3.6 %all-to-all-start.1 = ((bf16[16,24,1024]{2,1,0:T(8,128)(2,1)}), bf16[16,24,1024]{2,1,0:T(8,128)(2,1)S(1)}, u32[]{:S(2)}, u32[]{:S(2)}) async-start(bf16[16,24,1024]{2,1,0:T(8,128)(2,1)} %bitcast.24), calls=%async_computation.1 | async-start | bytes 1572864 | tf_op jit(solution)/shard_map/all_to_all | solution.py:383
  43.8 0.0 copy-done.4
  43.8 0.1 copy.10
  44.0 0.3 multiply_bitcast_fusion
  44.2 0.9 fusion.1
  45.1 0.9 squeeze.6.weight_ref
  46.0 0.0 copy-start.2
  46.0 0.9 copy-done.2
  46.9 0.0 copy-start
  46.9 0.0 copy-start.1
  46.9 8.1 %shard_map.78.local_ref = bf16[1536,2048]{1,0:T(8,128)(2,1)} custom-call(bf16[1536,2048]{1,0:T(8,128)(2,1)} %bitcast.22, bf16[256,256]{1,0:T(8,128)(2,1)S(1)} %copy-done.2), custom_call_target="tpu_custom_call" | custom-call | tf_op jit(solution)/shard_map/pallas_call | solution.py:194
  55.0 2.1 %all-to-all-done.1 = bf16[16,24,1024]{2,1,0:T(8,128)(2,1)S(1)} async-done(((bf16[16,24,1024]{2,1,0:T(8,128)(2,1)}), bf16[16,24,1024]{2,1,0:T(8,128)(2,1)S(1)}, u32[]{:S(2)}, u32[]{:S(2)}) %all-to-all-start.1) | async-done | bytes 786464 | tf_op jit(solution)/shard_map/all_to_all | solution.py:383
  57.2 0.0 copy-done
  57.2 0.0 copy-done.1
  57.2 6.3 %shard_map.79 = bf16[384,1024]{1,0:T(8,128)(2,1)S(1)} custom-call(bf16[384,1024]{1,0:T(8,128)(2,1)S(1)} %bitcast.12, bf16[1536,2048]{1,0:T(8,128)(2,1)} %shard_map.78.local_ref, bf16[256,2048]{1,0:T(8,128)(2,1)S(1)} %copy-done, bf16[256,2048]{1,0:T(8,128)(2,1)S(1)} %copy-done.1), custom_call_target="tpu_custom_call" | custom-call | tf_op jit(solution)/shard_map/pallas_call | solution.py:368
  63.5 0.0 copy-start.3
  63.5 16.2 %all_to_all.21 = bf16[16,24,1024]{2,1,0:T(8,128)(2,1)S(1)} all-to-all(bf16[16,24,1024]{2,1,0:T(8,128)(2,1)S(1)} %bitcast.19), channel_id=1, replica_groups={{0,1,2,3,4,5,6,7,8,9,10,11,12,13,14,15},{16,17,18,19,20,21,22,23,24,25,..., dimensions={0} | all-to-all | bytes 1572864 | tf_op jit(solution)/shard_map/all_to_all | solution.py:383
  79.7 0.4 shard_map.81.own_ref
  80.2 1.7 %collective-permute-start.3 = (bf16[128,512]{1,0:T(8,128)(2,1)S(1)}, bf16[128,512]{1,0:T(8,128)(2,1)S(1)}, u32[]{:S(2)}, u32[]{:S(2)}) collective-permute-start(bf16[128,512]{1,0:T(8,128)(2,1)S(1)} %shard_map.81.own_ref), channel_id=1, source_target_pairs={{0,16},{1,17},{2,18},{3,19},{4,20},{5,21},{6,22},{7,23},{8,24},{9,... | collective-permute-start | bytes 393224 | tf_op jit(solution)/shard_map/ppermute | solution.py:415
  81.9 0.4 shard_map.80.own_ref
  82.3 1.3 %collective-permute-start.2 = (bf16[128,512]{1,0:T(8,128)(2,1)S(1)}, bf16[128,512]{1,0:T(8,128)(2,1)S(1)}, u32[]{:S(2)}, u32[]{:S(2)}) collective-permute-start(bf16[128,512]{1,0:T(8,128)(2,1)S(1)} %shard_map.80.own_ref), channel_id=1, source_target_pairs={{0,16},{1,17},{2,18},{3,19},{4,20},{5,21},{6,22},{7,23},{8,24},{9,... | collective-permute-start | bytes 393224 | tf_op jit(solution)/shard_map/ppermute | solution.py:415
  83.6 8.4 %collective-permute-done.3.other_ref = bf16[128,512]{1,0:T(8,128)(2,1)S(1)} collective-permute-done((bf16[128,512]{1,0:T(8,128)(2,1)S(1)}, bf16[128,512]{1,0:T(8,128)(2,1)S(1)}, u32[]{:S(2)}, u32[]{:S(2)}) %collective-permute-start.3) | collective-permute-done | bytes 131104 | tf_op jit(solution)/shard_map/ppermute | solution.py:415
  92.1 1.4 %shard_map.82.rest_0_ = bf16[384,1024]{1,0:T(8,128)(2,1)} custom-call(bf16[128,512]{1,0:T(8,128)(2,1)S(1)} %shard_map.81.own_ref, bf16[128,512]{1,0:T(8,128)(2,1)S(1)} %collective-permute-done.3.other_ref, bf16[2,8,64,128]{3,2,1,0:T(8,128)(2,1)S(1)} %get-tuple-element.11.weights_ref, bf16[384,256]{1,0:T(8,128)(2,1)S(1)} %get-tuple-element.12.backward_ref), custom_call_target="tpu_custom_call" | custom-call | tf_op jit(solution)/shard_map/pallas_call | solution.py:268
  93.4 0.9 collective-permute-done.2.other_ref
  94.3 1.4 %shard_map.83 = bf16[384,1024]{1,0:T(8,128)(2,1)} custom-call(bf16[128,512]{1,0:T(8,128)(2,1)S(1)} %shard_map.80.own_ref, bf16[128,512]{1,0:T(8,128)(2,1)S(1)} %collective-permute-done.2.other_ref, bf16[2,8,64,128]{3,2,1,0:T(8,128)(2,1)S(1)} %get-tuple-element.11.weights_ref, ...), custom_call_target="tpu_custom_call", output_to_operand_aliasing={{}: (4, {})} | custom-call | tf_op jit(solution)/shard_map/pallas_call | solution.py:268
  95.7 3.8 %all-to-all-start.3 = ((bf16[16,24,1024]{2,1,0:T(8,128)(2,1)}), bf16[16,24,1024]{2,1,0:T(8,128)(2,1)S(1)}, u32[]{:S(2)}, u32[]{:S(2)}) async-start(bf16[16,24,1024]{2,1,0:T(8,128)(2,1)} %bitcast.23), calls=%async_computation.3 | async-start | bytes 1572864 | tf_op jit(solution)/shard_map/all_to_all | solution.py:383
  99.5 0.0 copy-done.3
  99.5 0.2 squeeze.7.rest_0_
  99.7 7.7 %shard_map.84.local_ref = bf16[1536,2048]{1,0:T(8,128)(2,1)} custom-call(bf16[384,1024]{1,0:T(8,128)(2,1)S(1)} %bitcast.13, bf16[1536,2048]{1,0:T(8,128)(2,1)} %shard_map.78.local_ref, bf16[256,2048]{1,0:T(8,128)(2,1)S(1)} %copy-done, bf16[256,256]{1,0:T(8,128)(2,1)S(1)} %squeeze.7.rest_0_), custom_call_target="tpu_custom_call" | custom-call | tf_op jit(solution)/shard_map/pallas_call | solution.py:368
  107.4 5.2 %all-to-all-done.3 = bf16[16,24,1024]{2,1,0:T(8,128)(2,1)S(1)} async-done(((bf16[16,24,1024]{2,1,0:T(8,128)(2,1)}), bf16[16,24,1024]{2,1,0:T(8,128)(2,1)S(1)}, u32[]{:S(2)}, u32[]{:S(2)}) %all-to-all-start.3) | async-done | bytes 786464 | tf_op jit(solution)/shard_map/all_to_all | solution.py:383
  112.6 6.0 %shard_map.85 = bf16[1536,2048]{1,0:T(8,128)(2,1)} custom-call(bf16[384,1024]{1,0:T(8,128)(2,1)S(1)} %bitcast.18, bf16[1536,2048]{1,0:T(8,128)(2,1)} %shard_map.84.local_ref, bf16[256,2048]{1,0:T(8,128)(2,1)S(1)} %copy-done), custom_call_target="tpu_custom_call" | custom-call | tf_op jit(solution)/shard_map/pallas_call | solution.py:368
  (1 shorter events, 0.0 us)
Async XLA Ops:
  4.8 39.0 %copy-start.4 = (bf16[2,64,64]{2,1,0:T(8,128)(2,1)S(1)}, bf16[2,64,64]{2,1,0:T(8,128)(2,1)}, u32[]{:S(2)}) copy-start(bf16[2,64,64]{2,1,0:T(8,128)(2,1)} %param.9) | copy-start | bytes 49156
  24.7 11.9 %collective-permute-start.1 = (bf16[128,512]{1,0:T(8,128)(2,1)S(1)}, bf16[128,512]{1,0:T(8,128)(2,1)S(1)}, u32[]{:S(2)}, u32[]{:S(2)}) collective-permute-start(bf16[128,512]{1,0:T(8,128)(2,1)S(1)} %shard_map.75.own_ref), channel_id=1, source_target_pairs={{0,16},{1,17},{2,18},{3,19},{4,20},{5,21},{6,22},{7,23},{8,24},{9,... | collective-permute-start | bytes 393224 | tf_op jit(solution)/shard_map/ppermute | solution.py:415
  27.8 11.1 %collective-permute-start = (bf16[128,512]{1,0:T(8,128)(2,1)S(1)}, bf16[128,512]{1,0:T(8,128)(2,1)S(1)}, u32[]{:S(2)}, u32[]{:S(2)}) collective-permute-start(bf16[128,512]{1,0:T(8,128)(2,1)S(1)} %shard_map.74.own_ref), channel_id=1, source_target_pairs={{0,16},{1,17},{2,18},{3,19},{4,20},{5,21},{6,22},{7,23},{8,24},{9,... | collective-permute-start | bytes 393224 | tf_op jit(solution)/shard_map/ppermute | solution.py:415
  40.2 17.0 %all-to-all-start.1 = ((bf16[16,24,1024]{2,1,0:T(8,128)(2,1)}), bf16[16,24,1024]{2,1,0:T(8,128)(2,1)S(1)}, u32[]{:S(2)}, u32[]{:S(2)}) async-start(bf16[16,24,1024]{2,1,0:T(8,128)(2,1)} %bitcast.24), calls=%async_computation.1 | async-start | bytes 1572864 | tf_op jit(solution)/shard_map/all_to_all | solution.py:383
  46.0 0.9 copy-start.2
  46.9 10.2 %copy-start = (bf16[256,2048]{1,0:T(8,128)(2,1)S(1)}, bf16[256,2048]{1,0:T(8,128)(2,1)}, u32[]{:S(2)}) copy-start(bf16[256,2048]{1,0:T(8,128)(2,1)} %constant.15.clone.back_ref) | copy-start | bytes 3145732
  46.9 10.2 %copy-start.1 = (bf16[256,2048]{1,0:T(8,128)(2,1)S(1)}, bf16[256,2048]{1,0:T(8,128)(2,1)}, u32[]{:S(2)}) copy-start(bf16[256,2048]{1,0:T(8,128)(2,1)} %constant.12.clone.table_ref.rest_0_) | copy-start | bytes 3145732
  63.5 36.0 %copy-start.3 = (bf16[1,4,64,4,64]{4,3,2,1,0:T(4,128)(2,1)S(1)}, bf16[1,4,64,4,64]{4,3,2,1,0:T(4,128)(2,1)}, u32[]{:S(2)}) copy-start(bf16[1,4,64,4,64]{4,3,2,1,0:T(4,128)(2,1)} %get-tuple-element.13) | copy-start | bytes 393220
  80.2 11.9 %collective-permute-start.3 = (bf16[128,512]{1,0:T(8,128)(2,1)S(1)}, bf16[128,512]{1,0:T(8,128)(2,1)S(1)}, u32[]{:S(2)}, u32[]{:S(2)}) collective-permute-start(bf16[128,512]{1,0:T(8,128)(2,1)S(1)} %shard_map.81.own_ref), channel_id=1, source_target_pairs={{0,16},{1,17},{2,18},{3,19},{4,20},{5,21},{6,22},{7,23},{8,24},{9,... | collective-permute-start | bytes 393224 | tf_op jit(solution)/shard_map/ppermute | solution.py:415
  82.3 12.0 %collective-permute-start.2 = (bf16[128,512]{1,0:T(8,128)(2,1)S(1)}, bf16[128,512]{1,0:T(8,128)(2,1)S(1)}, u32[]{:S(2)}, u32[]{:S(2)}) collective-permute-start(bf16[128,512]{1,0:T(8,128)(2,1)S(1)} %shard_map.80.own_ref), channel_id=1, source_target_pairs={{0,16},{1,17},{2,18},{3,19},{4,20},{5,21},{6,22},{7,23},{8,24},{9,... | collective-permute-start | bytes 393224 | tf_op jit(solution)/shard_map/ppermute | solution.py:415
  95.7 17.0 %all-to-all-start.3 = ((bf16[16,24,1024]{2,1,0:T(8,128)(2,1)}), bf16[16,24,1024]{2,1,0:T(8,128)(2,1)S(1)}, u32[]{:S(2)}, u32[]{:S(2)}) async-start(bf16[16,24,1024]{2,1,0:T(8,128)(2,1)} %bitcast.23), calls=%async_computation.3 | async-start | bytes 1572864 | tf_op jit(solution)/shard_map/all_to_all | solution.py:383
